TPU v7x, 32 devices: a whole 2x2x4 slice. The times are simulated.
32 devices in a mesh: rep: 8 (over y, x, core), shard: 4 (over z).
Axes of the slice: x: 2, y: 2, z: 4, core: 2. Of those that a mesh axis runs over, the one named last changes fastest.
Arguments:
- tokens: bfloat16 [2, 4096, 2048], P(None, ('rep', 'shard')), may hold values from -6 to 6
- attn_gain: float32 [2048], P('shard'), may hold values from 0.25 to 1.75
- q_weight: float32 [3072, 2048], P(None, 'shard'), may hold values from -0.125 to 0.125
- kva_weight: float32 [576, 2048], P(None, 'shard'), may hold values from -0.125 to 0.125
- kv_gain: float32 [512], P('shard'), may hold values from 0.25 to 1.75
- kvb_weight: float32 [512, 4096], P('shard'), may hold values from -0.25 to 0.25
- out_weight: float32 [2048, 2048], P('shard'), may hold values from -2 to 2
- ffn_gain: float32 [2048], P('shard'), may hold values from 0.25 to 1.75
- router_weight: float32 [64, 2048], P(None, 'shard'), may hold values from -0.066 to 0.066
- shared_gate: float32 [1408, 2048], P('shard'), may hold values from -0.125 to 0.125
- shared_up: float32 [1408, 2048], P('shard'), may hold values from -0.125 to 0.125
- shared_down: float32 [1408, 2048], P('shard'), may hold values from -0.15625 to 0.15625
- expert_gate: float32 [2, 1408, 2048], P(None, 'shard'), may hold values from -0.125 to 0.125
- expert_up: float32 [2, 1408, 2048], P(None, 'shard'), may hold values from -0.125 to 0.125
- expert_down: float32 [2, 1408, 2048], P(None, 'shard'), may hold values from -12 to 12
- expert_ids: int32 [2, 4096, 6], P(None, ('rep', 'shard')), may hold values from 0 to 63, as said below
- cotangent: bfloat16 [2, 4096, 2048], P(None, ('rep', 'shard')), may hold values from -6 to 6
Outputs:
- layer_output: bfloat16 [2, 4096, 2048], P(None, ('rep', 'shard'))
- input_grad: bfloat16 [2, 4096, 2048], P(None, ('rep', 'shard'))
- attn_gain_grad: float32 [2048], P('shard')
- q_weight_grad: float32 [3072, 2048], P(None, 'shard')
- kva_weight_grad: float32 [576, 2048], P(None, 'shard')
- kv_gain_grad: float32 [512], P('shard')
- kvb_weight_grad: float32 [512, 4096], P('shard')
- out_weight_grad: float32 [2048, 2048], P('shard')
- ffn_gain_grad: float32 [2048], P('shard')
- router_weight_grad: float32 [64, 2048], P(None, 'shard')
- shared_gate_grad: float32 [1408, 2048], P('shard')
- shared_up_grad: float32 [1408, 2048], P('shard')
- shared_down_grad: float32 [1408, 2048], P('shard')
- expert_gate_grad: float32 [2, 1408, 2048], P(None, 'shard')
- expert_up_grad: float32 [2, 1408, 2048], P(None, 'shard')
- expert_down_grad: float32 [2, 1408, 2048], P(None, 'shard')
Inputs may be any that keep to these rules, and one draw needn't show every extreme that they name: `expert_ids`: each row names 6 different experts. In each micro-batch the 128 rows of one device name each expert below 2 at least 8 and at most 16 times, and for each expert below 2 the rows of some device and micro-batch name it exactly 16 times.
All inputs are finite; a program needn't handle non-finite values.
Results may differ from a plain program's by a relative error of at most 0.04.
Values may be sent and summed in bfloat16 or wider, within the bound.
A program may use at most 384 MiB of HBM per device.

v0:
```python
import jax
import jax.numpy as jnp
from jax import lax
from jax.sharding import PartitionSpec as P

HEADS = 16
NOPE = 128
ROPE = 64
VDIM = 128
RANK = 512
EXPERTS = 64
EXP_WIN = 2
MASK_BLOCK = 256
CAP = 16


epsilon = 1e-06
rope_base = 10000.0
masked_score = -1e30
highest = lax.Precision.HIGHEST


def rms_scale(tensor):
    return lax.rsqrt(jnp.mean(tensor * tensor, axis=-1, keepdims=True) + epsilon)


def rotary_tables(positions, rope_width):
    half_width = rope_width // 2
    frequency = jnp.exp(
        -jnp.log(rope_base) * (2.0 * jnp.arange(half_width, dtype=jnp.float32) / rope_width)
    )
    angles = positions.astype(jnp.float32)[:, None] * frequency[None, :]
    return (jnp.cos(angles), jnp.sin(angles))


def rotate(tensor, cosine, sine_tab):
    half_width = tensor.shape[-1] // 2
    first_half = tensor[..., :half_width]
    second_half = tensor[..., half_width:]
    return jnp.concatenate(
        [
            first_half * cosine - second_half * sine_tab,
            second_half * cosine + first_half * sine_tab,
        ],
        axis=-1,
    )


def rotate_back(gradient, cosine, sine_tab):
    half_width = gradient.shape[-1] // 2
    first_half = gradient[..., :half_width]
    second_half = gradient[..., half_width:]
    return jnp.concatenate(
        [
            first_half * cosine + second_half * sine_tab,
            second_half * cosine - first_half * sine_tab,
        ],
        axis=-1,
    )


def norm_back(tensor, inv_rms, gain_vec, gradient):
    scaled_grad = gradient * gain_vec
    inner_mean = jnp.mean(scaled_grad * tensor, axis=-1, keepdims=True)
    input_part = inv_rms * scaled_grad - tensor * (inv_rms * inv_rms * inv_rms) * inner_mean
    gain_part = jnp.sum((gradient * tensor * inv_rms).reshape(-1, tensor.shape[-1]), axis=0)
    return (input_part, gain_part)


def swiglu_back(gate_pre, up_pre, hidden_grad):
    sigmoid_gate = jax.nn.sigmoid(gate_pre)
    silu_gate = gate_pre * sigmoid_gate
    slope = sigmoid_gate * (1.0 + gate_pre * (1.0 - sigmoid_gate))
    return (
        (hidden_grad * up_pre * slope).astype(jnp.bfloat16),
        (hidden_grad * silu_gate).astype(jnp.bfloat16),
    )


def slot_table(expert_rows):
    window_ids = jnp.arange(EXP_WIN, dtype=jnp.int32)
    member = jnp.any(expert_rows[..., None, :] == window_ids[:, None], axis=-1).astype(jnp.int32)
    member = jnp.swapaxes(member, -1, -2)
    placed = jnp.cumsum(member, axis=-1) - 1
    slot_ids = jnp.arange(CAP, dtype=jnp.int32)
    hits = (member[None] == 1) & (placed[None] == slot_ids[:, None, None, None])
    return hits.astype(jnp.float32)


def owner_order(tensor, along, outer_count, inner_count):
    old_shape = tensor.shape
    piece_rows = old_shape[along] // (outer_count * inner_count)
    regrouped = tensor.reshape(
        old_shape[:along] + (inner_count, outer_count, piece_rows) + old_shape[along + 1 :]
    )
    return jnp.swapaxes(regrouped, along, along + 1).reshape(old_shape)


def block_scores(q_block, q_pos, keys_nope, keys_rope, key_pos, score_scale):
    nope_width = keys_nope.shape[-1]
    scores = jnp.einsum(
        "qhd,khd->hqk", q_block[..., :nope_width], keys_nope, preferred_element_type=jnp.float32
    )
    scores = scores + jnp.einsum(
        "qhd,kd->hqk", q_block[..., nope_width:], keys_rope, preferred_element_type=jnp.float32
    )
    visible = q_pos[:, None] // MASK_BLOCK >= key_pos[None, :] // MASK_BLOCK
    return jnp.where(visible[None], scores * score_scale, masked_score)


def shards(
    tokens,
    attn_gain,
    q_weight,
    kva_weight,
    kv_gain,
    kvb_weight,
    out_weight,
    ffn_gain,
    router_weight,
    shared_gate,
    shared_up,
    shared_down,
    expert_gate,
    expert_up,
    expert_down,
    expert_ids,
    cotangent,
):
    shard_count = lax.axis_size("shard")
    shard_index = lax.axis_index("shard")
    micro_count, rows_dev, model_width = tokens.shape
    seq_len = rows_dev * shard_count
    head_width = NOPE + ROPE
    score_scale = (NOPE + ROPE) ** (-0.5)
    rep_count = lax.axis_size("rep")

    def arrange(tensor, along):
        return owner_order(tensor, along, rep_count, shard_count)

    attn_gain_b, query_mat, kv_down_mat, kv_gain_b, kv_up_mat, output_mat = (
        lax.all_gather(attn_gain.astype(jnp.bfloat16), "shard", axis=0, tiled=True),
        lax.all_gather(q_weight.astype(jnp.bfloat16), "shard", axis=1, tiled=True),
        lax.all_gather(kva_weight.astype(jnp.bfloat16), "shard", axis=1, tiled=True),
        lax.all_gather(kv_gain.astype(jnp.bfloat16), "shard", axis=0, tiled=True),
        lax.all_gather(kvb_weight.astype(jnp.bfloat16), "shard", axis=0, tiled=True),
        lax.all_gather(out_weight.astype(jnp.bfloat16), "shard", axis=0, tiled=True),
    )
    x_in = tokens.astype(jnp.float32)
    inv_one = rms_scale(x_in)
    h_attn = (x_in * inv_one * attn_gain_b.astype(jnp.float32)).astype(jnp.bfloat16)
    positions = shard_index * rows_dev + jnp.arange(rows_dev, dtype=jnp.int32)
    cosine, sine_tab = rotary_tables(positions, ROPE)
    q_raw = jnp.einsum("mtd,od->mto", h_attn, query_mat, preferred_element_type=jnp.float32)
    q_raw = q_raw.reshape(micro_count, rows_dev, HEADS, head_width)
    queries = jnp.concatenate(
        [q_raw[..., :NOPE], rotate(q_raw[..., NOPE:], cosine[:, None], sine_tab[:, None])], axis=-1
    ).astype(jnp.bfloat16)
    kv_down = jnp.einsum("mtd,od->mto", h_attn, kv_down_mat, preferred_element_type=jnp.float32)
    latent = kv_down[..., :RANK]
    inv_kv = rms_scale(latent)
    latent_norm = (latent * inv_kv * kv_gain_b.astype(jnp.float32)).astype(jnp.bfloat16)
    key_rope = rotate(kv_down[..., RANK:], cosine, sine_tab).astype(jnp.bfloat16)
    kv_up = jnp.einsum(
        "mtr,rk->mtk", latent_norm, kv_up_mat, preferred_element_type=jnp.float32
    ).astype(jnp.bfloat16)
    kv_all, rope_all = (
        lax.all_gather(kv_up, "shard", axis=1, tiled=True),
        lax.all_gather(key_rope, "shard", axis=1, tiled=True),
    )
    q_rows = rows_dev
    while q_rows % 2 == 0 and q_rows * seq_len > 1 << 18:
        q_rows = q_rows // 2
    block_count = rows_dev // q_rows
    key_pos = jnp.arange(seq_len, dtype=jnp.int32)
    pos_blocks = positions.reshape(block_count, q_rows)
    attended_list = []
    lse_list = []
    for micro_idx in range(micro_count):
        heads_kv = kv_all[micro_idx].reshape(seq_len, HEADS, NOPE + VDIM)
        keys_nope = heads_kv[..., :NOPE]
        values_all = heads_kv[..., NOPE:]
        rope_keys = rope_all[micro_idx]

        def forward_block(block_item):
            q_block, q_pos = block_item
            scores = block_scores(q_block, q_pos, keys_nope, rope_keys, key_pos, score_scale)
            row_top = jnp.max(scores, axis=-1, keepdims=True)
            expo_scores = jnp.exp(scores - row_top)
            row_total = jnp.sum(expo_scores, axis=-1, keepdims=True)
            attn_probs = (expo_scores / row_total).astype(jnp.bfloat16)
            mixed = jnp.einsum(
                "hqk,khd->qhd", attn_probs, values_all, preferred_element_type=jnp.float32
            )
            return (mixed, (row_top + jnp.log(row_total))[..., 0])

        mixed_all, lse_all = lax.map(
            forward_block,
            (queries[micro_idx].reshape(block_count, q_rows, HEADS, head_width), pos_blocks),
        )
        attended_list.append(mixed_all.reshape(rows_dev, HEADS * VDIM))
        lse_list.append(lse_all)
    attended = jnp.stack(attended_list).astype(jnp.bfloat16)
    x_mid = x_in + jnp.einsum(
        "mto,od->mtd", attended, output_mat, preferred_element_type=jnp.float32
    )
    ffn_gain_b, router_mat, shared_gate_mat, shared_up_mat, shared_down_mat = (
        lax.all_gather(ffn_gain.astype(jnp.bfloat16), "shard", axis=0, tiled=True),
        lax.all_gather(router_weight.astype(jnp.bfloat16), "shard", axis=1, tiled=True),
        lax.all_gather(shared_gate.astype(jnp.bfloat16), "shard", axis=0, tiled=True),
        lax.all_gather(shared_up.astype(jnp.bfloat16), "shard", axis=0, tiled=True),
        lax.all_gather(shared_down.astype(jnp.bfloat16), "shard", axis=0, tiled=True),
    )
    inv_two = rms_scale(x_mid)
    h_ffn = (x_mid * inv_two * ffn_gain_b.astype(jnp.float32)).astype(jnp.bfloat16)
    logits = jnp.einsum("mtd,ed->mte", h_ffn, router_mat, preferred_element_type=jnp.float32)
    router_probs = jax.nn.softmax(logits, axis=-1)
    gate_pre = jnp.einsum("mtd,fd->mtf", h_ffn, shared_gate_mat, preferred_element_type=jnp.float32)
    up_pre = jnp.einsum("mtd,fd->mtf", h_ffn, shared_up_mat, preferred_element_type=jnp.float32)
    shared_hidden = (jax.nn.silu(gate_pre) * up_pre).astype(jnp.bfloat16)
    shared_out = jnp.einsum(
        "mtf,fd->mtd", shared_hidden, shared_down_mat, preferred_element_type=jnp.float32
    )
    select = slot_table(expert_ids)
    select_b = select.astype(jnp.bfloat16)
    slot_rows = jnp.einsum(
        "cmet,mtd->cmed", select_b, h_ffn, preferred_element_type=jnp.float32
    ).astype(jnp.bfloat16)
    slot_gates = jnp.einsum("cmet,mte->cme", select, router_probs[..., :EXP_WIN], precision=highest)
    gate_mats = expert_gate.astype(jnp.bfloat16)
    up_mats = expert_up.astype(jnp.bfloat16)
    down_mats = expert_down.astype(jnp.bfloat16)
    rows_all = lax.all_gather(slot_rows, "shard", axis=0, tiled=True)
    expert_pre = jnp.einsum(
        "cmed,efd->cmef", rows_all, gate_mats, preferred_element_type=jnp.float32
    )
    expert_upv = jnp.einsum("cmed,efd->cmef", rows_all, up_mats, preferred_element_type=jnp.float32)
    expert_hidden = (jax.nn.silu(expert_pre) * expert_upv).astype(jnp.bfloat16)
    expert_out = lax.psum_scatter(
        jnp.einsum("cmef,efd->cmed", expert_hidden, down_mats, preferred_element_type=jnp.float32),
        "shard",
        scatter_dimension=0,
        tiled=True,
    )
    routed = jnp.einsum("cmet,cme,cmed->mtd", select, slot_gates, expert_out, precision=highest)
    layer_output = (x_mid + shared_out + routed).astype(jnp.bfloat16)
    grad_out = cotangent.astype(jnp.float32)
    shared_down_grad = jnp.einsum(
        "mtf,mtd->fd", arrange(shared_hidden, 2), cotangent, preferred_element_type=jnp.float32
    )
    shared_hidden_grad = jnp.einsum(
        "mtd,fd->mtf", cotangent, shared_down_mat, preferred_element_type=jnp.float32
    )
    gate_grad_b, up_grad_b = swiglu_back(gate_pre, up_pre, shared_hidden_grad)
    shared_gate_grad = jnp.einsum(
        "mtf,mtd->fd", arrange(gate_grad_b, 2), h_ffn, preferred_element_type=jnp.float32
    )
    shared_up_grad = jnp.einsum(
        "mtf,mtd->fd", arrange(up_grad_b, 2), h_ffn, preferred_element_type=jnp.float32
    )
    ffn_grad = jnp.einsum(
        "mtf,fd->mtd", gate_grad_b, shared_gate_mat, preferred_element_type=jnp.float32
    )
    ffn_grad = ffn_grad + jnp.einsum(
        "mtf,fd->mtd", up_grad_b, shared_up_mat, preferred_element_type=jnp.float32
    )
    picked_grad = jnp.einsum(
        "cmet,mtd->cmed", select_b, cotangent, preferred_element_type=jnp.float32
    )
    slot_dy = (slot_gates[..., None] * picked_grad).astype(jnp.bfloat16)
    gate_weight_grad = jnp.sum(picked_grad * expert_out, axis=-1)
    dy_all = lax.all_gather(slot_dy, "shard", axis=0, tiled=True)
    expert_down_grad = jnp.einsum(
        "cmef,cmed->efd", expert_hidden, dy_all, preferred_element_type=jnp.float32
    )
    expert_hidden_grad = jnp.einsum(
        "cmed,efd->cmef", dy_all, down_mats, preferred_element_type=jnp.float32
    )
    expert_gate_b, expert_up_b = swiglu_back(expert_pre, expert_upv, expert_hidden_grad)
    expert_gate_grad = jnp.einsum(
        "cmef,cmed->efd", expert_gate_b, rows_all, preferred_element_type=jnp.float32
    )
    expert_up_grad = jnp.einsum(
        "cmef,cmed->efd", expert_up_b, rows_all, preferred_element_type=jnp.float32
    )
    gate_term = jnp.einsum(
        "cmef,efd->cmed", expert_gate_b, gate_mats, preferred_element_type=jnp.float32
    )
    slot_grad = lax.psum_scatter(
        gate_term
        + jnp.einsum("cmef,efd->cmed", expert_up_b, up_mats, preferred_element_type=jnp.float32),
        "shard",
        scatter_dimension=0,
        tiled=True,
    )
    ffn_grad = ffn_grad + jnp.einsum("cmet,cmed->mtd", select, slot_grad, precision=highest)
    probs_grad = jnp.einsum("cmet,cme->mte", select, gate_weight_grad, precision=highest)
    probs_grad = jnp.concatenate(
        [probs_grad, jnp.zeros(probs_grad.shape[:2] + (EXPERTS - EXP_WIN,), jnp.float32)], axis=-1
    )
    logit_grad = (
        router_probs * (probs_grad - jnp.sum(router_probs * probs_grad, axis=-1, keepdims=True))
    ).astype(jnp.bfloat16)
    router_weight_grad = jnp.einsum(
        "mte,mtd->ed", logit_grad, arrange(h_ffn, 2), preferred_element_type=jnp.float32
    )
    ffn_grad = ffn_grad + jnp.einsum(
        "mte,ed->mtd", logit_grad, router_mat, preferred_element_type=jnp.float32
    )
    mid_part, ffn_gain_raw = norm_back(x_mid, inv_two, ffn_gain_b.astype(jnp.float32), ffn_grad)
    ffn_gain_grad = arrange(ffn_gain_raw, 0)
    mid_grad = grad_out + mid_part
    attn_out_grad = mid_grad.astype(jnp.bfloat16)
    out_weight_grad = jnp.einsum(
        "mto,mtd->od", arrange(attended, 2), attn_out_grad, preferred_element_type=jnp.float32
    )
    attended_grad = jnp.einsum(
        "mtd,od->mto", attn_out_grad, output_mat, preferred_element_type=jnp.float32
    ).astype(jnp.bfloat16)
    attended_grad = attended_grad.reshape(micro_count, rows_dev, HEADS, VDIM)
    query_grad_list = []
    kv_grad_list = []
    rope_grad_list = []
    for micro_idx in range(micro_count):
        heads_kv = kv_all[micro_idx].reshape(seq_len, HEADS, NOPE + VDIM)
        keys_nope = heads_kv[..., :NOPE]
        values_all = heads_kv[..., NOPE:]
        rope_keys = rope_all[micro_idx]

        def backward_block(carried, block_item):
            nope_acc, rope_acc, value_acc = carried
            q_block, q_pos, dout_block, lse_block = block_item
            scores = block_scores(q_block, q_pos, keys_nope, rope_keys, key_pos, score_scale)
            attn_probs = jnp.exp(scores - lse_block[..., None])
            dprobs = jnp.einsum(
                "qhd,khd->hqk", dout_block, values_all, preferred_element_type=jnp.float32
            )
            row_delta = jnp.sum(attn_probs * dprobs, axis=-1, keepdims=True)
            score_grad = (attn_probs * (dprobs - row_delta)).astype(jnp.bfloat16)
            q_nope_grad = (
                jnp.einsum(
                    "hqk,khd->qhd", score_grad, keys_nope, preferred_element_type=jnp.float32
                )
                * score_scale
            )
            q_rope_grad = (
                jnp.einsum("hqk,kd->qhd", score_grad, rope_keys, preferred_element_type=jnp.float32)
                * score_scale
            )
            nope_acc = (
                nope_acc
                + jnp.einsum(
                    "hqk,qhd->khd",
                    score_grad,
                    q_block[..., :NOPE],
                    preferred_element_type=jnp.float32,
                )
                * score_scale
            )
            rope_acc = (
                rope_acc
                + jnp.einsum(
                    "hqk,qhd->kd",
                    score_grad,
                    q_block[..., NOPE:],
                    preferred_element_type=jnp.float32,
                )
                * score_scale
            )
            value_acc = value_acc + jnp.einsum(
                "hqk,qhd->khd",
                attn_probs.astype(jnp.bfloat16),
                dout_block,
                preferred_element_type=jnp.float32,
            )
            return (
                (nope_acc, rope_acc, value_acc),
                jnp.concatenate([q_nope_grad, q_rope_grad], axis=-1),
            )

        start_acc = (
            jnp.zeros((seq_len, HEADS, NOPE), jnp.float32),
            jnp.zeros((seq_len, ROPE), jnp.float32),
            jnp.zeros((seq_len, HEADS, VDIM), jnp.float32),
        )
        (nope_acc, rope_acc, value_acc), q_grad_blocks = lax.scan(
            backward_block,
            start_acc,
            (
                queries[micro_idx].reshape(block_count, q_rows, HEADS, head_width),
                pos_blocks,
                attended_grad[micro_idx].reshape(block_count, q_rows, HEADS, VDIM),
                lse_list[micro_idx],
            ),
        )
        key_grad_rows = jnp.concatenate([nope_acc, value_acc], axis=-1).reshape(
            seq_len, HEADS * (NOPE + VDIM)
        )
        kv_grad_own, rope_grad_own = (
            lax.psum_scatter(key_grad_rows, "shard", scatter_dimension=0, tiled=True),
            lax.psum_scatter(rope_acc, "shard", scatter_dimension=0, tiled=True),
        )
        kv_grad_list.append(kv_grad_own)
        rope_grad_list.append(rope_grad_own)
        query_grad_list.append(q_grad_blocks.reshape(rows_dev, HEADS, head_width))
    kv_up_grad = jnp.stack(kv_grad_list).astype(jnp.bfloat16)
    kvb_weight_grad = jnp.einsum(
        "mtr,mtk->rk", arrange(latent_norm, 2), kv_up_grad, preferred_element_type=jnp.float32
    )
    latent_norm_grad = jnp.einsum(
        "mtk,rk->mtr", kv_up_grad, kv_up_mat, preferred_element_type=jnp.float32
    )
    latent_grad, kv_gain_raw = norm_back(
        latent, inv_kv, kv_gain_b.astype(jnp.float32), latent_norm_grad
    )
    kv_gain_grad = arrange(kv_gain_raw, 0)
    rope_grad_all = jnp.stack(rope_grad_list)
    kv_down_grad = jnp.concatenate(
        [latent_grad, rotate_back(rope_grad_all, cosine, sine_tab)], axis=-1
    ).astype(jnp.bfloat16)
    query_grad = jnp.stack(query_grad_list)
    q_raw_grad = jnp.concatenate(
        [
            query_grad[..., :NOPE],
            rotate_back(query_grad[..., NOPE:], cosine[:, None], sine_tab[:, None]),
        ],
        axis=-1,
    )
    q_raw_grad = q_raw_grad.astype(jnp.bfloat16).reshape(micro_count, rows_dev, HEADS * head_width)
    h_arranged = arrange(h_attn, 2)
    q_weight_grad = jnp.einsum(
        "mto,mtd->od", q_raw_grad, h_arranged, preferred_element_type=jnp.float32
    )
    kva_weight_grad = jnp.einsum(
        "mto,mtd->od", kv_down_grad, h_arranged, preferred_element_type=jnp.float32
    )
    attn_in_grad = jnp.einsum(
        "mto,od->mtd", q_raw_grad, query_mat, preferred_element_type=jnp.float32
    )
    attn_in_grad = attn_in_grad + jnp.einsum(
        "mto,od->mtd", kv_down_grad, kv_down_mat, preferred_element_type=jnp.float32
    )
    x_part, attn_gain_raw = norm_back(x_in, inv_one, attn_gain_b.astype(jnp.float32), attn_in_grad)
    attn_gain_grad = arrange(attn_gain_raw, 0)
    input_grad = (mid_grad + x_part).astype(jnp.bfloat16)
    reduced = (
        lax.psum_scatter(attn_gain_grad, ("rep", "shard"), scatter_dimension=0, tiled=True),
        lax.psum_scatter(q_weight_grad, ("rep", "shard"), scatter_dimension=1, tiled=True),
        lax.psum_scatter(kva_weight_grad, ("rep", "shard"), scatter_dimension=1, tiled=True),
        lax.psum_scatter(kv_gain_grad, ("rep", "shard"), scatter_dimension=0, tiled=True),
        lax.psum_scatter(kvb_weight_grad, ("rep", "shard"), scatter_dimension=0, tiled=True),
        lax.psum_scatter(out_weight_grad, ("rep", "shard"), scatter_dimension=0, tiled=True),
        lax.psum_scatter(ffn_gain_grad, ("rep", "shard"), scatter_dimension=0, tiled=True),
        lax.psum_scatter(router_weight_grad, ("rep", "shard"), scatter_dimension=1, tiled=True),
        lax.psum_scatter(shared_gate_grad, ("rep", "shard"), scatter_dimension=0, tiled=True),
        lax.psum_scatter(shared_up_grad, ("rep", "shard"), scatter_dimension=0, tiled=True),
        lax.psum_scatter(shared_down_grad, ("rep", "shard"), scatter_dimension=0, tiled=True),
    )
    owned = (
        lax.all_gather(reduced[0], "rep", axis=0, tiled=True),
        lax.all_gather(reduced[1], "rep", axis=1, tiled=True),
        lax.all_gather(reduced[2], "rep", axis=1, tiled=True),
        lax.all_gather(reduced[3], "rep", axis=0, tiled=True),
        lax.all_gather(reduced[4], "rep", axis=0, tiled=True),
        lax.all_gather(reduced[5], "rep", axis=0, tiled=True),
        lax.all_gather(reduced[6], "rep", axis=0, tiled=True),
        lax.all_gather(reduced[7], "rep", axis=1, tiled=True),
        lax.all_gather(reduced[8], "rep", axis=0, tiled=True),
        lax.all_gather(reduced[9], "rep", axis=0, tiled=True),
        lax.all_gather(reduced[10], "rep", axis=0, tiled=True),
    )
    expert_sums = lax.psum((expert_gate_grad, expert_up_grad, expert_down_grad), "rep")
    return (
        layer_output,
        input_grad,
        owned[0],
        owned[1],
        owned[2],
        owned[3],
        owned[4],
        owned[5],
        owned[6],
        owned[7],
        owned[8],
        owned[9],
        owned[10],
        expert_sums[0],
        expert_sums[1],
        expert_sums[2],
    )


def solution(mesh):
    return jax.shard_map(
        shards,
        mesh=mesh,
        in_specs=(
            P(None, ("rep", "shard"), None),
            P("shard"),
            P(None, "shard"),
            P(None, "shard"),
            P("shard"),
            P("shard", None),
            P("shard", None),
            P("shard"),
            P(None, "shard"),
            P("shard", None),
            P("shard", None),
            P("shard", None),
            P(None, "shard", None),
            P(None, "shard", None),
            P(None, "shard", None),
            P(None, ("rep", "shard"), None),
            P(None, ("rep", "shard"), None),
        ),
        out_specs=(
            P(None, ("rep", "shard"), None),
            P(None, ("rep", "shard"), None),
            P("shard"),
            P(None, "shard"),
            P(None, "shard"),
            P("shard"),
            P("shard", None),
            P("shard", None),
            P("shard"),
            P(None, "shard"),
            P("shard", None),
            P("shard", None),
            P("shard", None),
            P(None, "shard", None),
            P(None, "shard", None),
            P(None, "shard", None),
        ),
        check_vma=False,
    )
```

profile of v0, /device:TPU:9, one launch (start us, length us, event | category | flops | bytes accessed | tf_op | source)
XLA Modules:
  0.0 3801.2 jit_solution(17476680073378793842)
XLA Ops:
  10.8 9.5 all-gather
  20.4 6.4 all-gather.1
  28.0 32.0 all-gather.24.cloned.1.call-done
  63.4 77.6 %all-gather.26.cloned.1.call-done = bf16[512,4096]{1,0:T(8,128)(2,1)} async-done(((bf16[128,4096]{1,0:T(8,128)(2,1)}), bf16[512,4096]{1,0:T(8,128)(2,1)}) %all-gather.26.cloned.1.call-update) | async-done | bytes 4194320 | tf_op jit(solution)/shard_map/all_gather | solution.py:146
  141.1 4.8 convolution_convert_fusion
  145.9 4.9 convert_element_type.188
  154.8 11.2 all-gather.2
  167.2 14.7 all_gather.84
  181.9 114.2 %all-gather.28.cloned.1.call-done = bf16[2,512,4096]{2,1,0:T(8,128)(2,1)} async-done(((bf16[2,128,4096]{2,1,0:T(8,128)(2,1)}), bf16[2,512,4096]{2,1,0:T(8,128)(2,1)}) %all-gather.28.cloned.1.call-update) | async-done | bytes 8388624 | tf_op jit(solution)/shard_map/all_gather | solution.py:168
  296.1 5.2 fusion.201
  304.7 4.7 copy.456
  309.4 205.0 %all-gather.30.cloned.1.call-done = bf16[3072,2048]{1,0:T(8,128)(2,1)} async-done(((bf16[3072,512]{1,0:T(8,128)(2,1)}), bf16[3072,2048]{1,0:T(8,128)(2,1)}) %all-gather.30.cloned.1.call-update) | async-done | bytes 12582928 | tf_op jit(solution)/shard_map/all_gather | solution.py:143
  514.5 7.3 fusion.6
  537.2 5.0 copy.454
  552.4 111.9 %all-gather.32.cloned.1.call-done = bf16[2048,2048]{1,0:T(8,128)(2,1)} async-done(((bf16[512,2048]{1,0:T(8,128)(2,1)}), bf16[2048,2048]{1,0:T(8,128)(2,1)}) %all-gather.32.cloned.1.call-update) | async-done | bytes 8388624 | tf_op jit(solution)/shard_map/all_gather | solution.py:147
  664.3 6.2 multiply_reduce_fusion.4
  672.4 28.8 all-gather.40.cloned.1.call-done
  705.4 4.6 multiply_convert_fusion.10
  713.7 12.5 all_gather.90
  728.8 29.1 reduce-scatter.20.cloned.1.call-done
  774.3 18.6 all-gather.42.cloned.1.call-done
  793.0 4.2 multiply_convert_fusion.9
  803.5 95.4 %all-gather.38.cloned.1.call-done = bf16[1408,2048]{1,0:T(8,128)(2,1)} async-done(((bf16[352,2048]{1,0:T(8,128)(2,1)}), bf16[1408,2048]{1,0:T(8,128)(2,1)}) %all-gather.38.cloned.1.call-update) | async-done | bytes 5767184 | tf_op jit(solution)/shard_map/all_gather | solution.py:212
  898.9 5.9 fusion.12
  904.9 101.2 %all-gather.36.cloned.1.call-done = bf16[1408,2048]{1,0:T(8,128)(2,1)} async-done(((bf16[352,2048]{1,0:T(8,128)(2,1)}), bf16[1408,2048]{1,0:T(8,128)(2,1)}) %all-gather.36.cloned.1.call-update) | async-done | bytes 5767184 | tf_op jit(solution)/shard_map/all_gather | solution.py:211
  1006.0 5.6 fusion.18
  1011.6 101.1 %all-gather.34.cloned.1.call-done = bf16[1408,2048]{1,0:T(8,128)(2,1)} async-done(((bf16[352,2048]{1,0:T(8,128)(2,1)}), bf16[1408,2048]{1,0:T(8,128)(2,1)}) %all-gather.34.cloned.1.call-update) | async-done | bytes 5767184 | tf_op jit(solution)/shard_map/all_gather | solution.py:210
  1112.7 6.8 multiply_convert_fusion.4
  1125.9 32.2 reduce-scatter.22.cloned.1.call-done
  1185.2 4.6 multiply_reduce_fusion.1
  1194.3 8.2 pad_maximum_fusion.1
  1202.5 9.0 copy.394
  1215.8 5.0 pad_maximum_fusion
  1220.7 8.9 copy.392
  1235.8 135.2 %reduce-scatter.26.cloned.1.call-done = f32[128,4096]{1,0:T(8,128)} async-done(((f32[512,4096]{1,0:T(8,128)}), f32[128,4096]{1,0:T(8,128)}) %reduce-scatter.26.cloned.1.call-update) | async-done | bytes 2097168 | tf_op jit(solution)/shard_map/reduce_scatter | solution.py:400
  1373.7 144.7 %reduce-scatter.24.cloned.1.call-done = f32[128,4096]{1,0:T(8,128)} async-done(((f32[512,4096]{1,0:T(8,128)}), f32[128,4096]{1,0:T(8,128)}) %reduce-scatter.24.cloned.1.call-update) | async-done | bytes 2097168 | tf_op jit(solution)/shard_map/reduce_scatter | solution.py:400
  1520.5 4.6 multiply_reduce_fusion.5
  1530.2 6.2 convolution_bitcast_fusion.5
  1538.4 7.4 convolution_bitcast_fusion.4
  1555.4 10.3 convolution_bitcast_fusion
  1577.6 5.2 convolution_bitcast_fusion.3
  1582.9 5.2 convolution_bitcast_fusion.2
  1588.0 5.2 convolution_bitcast_fusion.1
  1593.3 1441.1 %fusion.200 = (f32[48,2048]{1,0:T(8,128)S(1)}, f32[48,2048]{1,0:T(8,128)S(1)}, f32[48,2048]{1,0:T(8,128)S(1)}) fusion(f32[1408,2048]{1,0:T(8,128)} %convolution_bitcast_fusion.3, f32[1408,2048]{1,0:T(8,128)} %convolution_bitcast_fusion.2, f32[1408,2048]{1,0:T(8,128)} %convolution_bitcast_fusion.1), kind=kCustom, calls=%all-reduce-scatter.3 | all-reduce-scatter fusion | flops 9437185 | bytes 35782656
  3036.7 5.4 collective-permute-start
  3044.1 57.5 %collective-permute-done.2 = f32[28,2048]{1,0:T(8,128)} collective-permute-done((f32[28,2048]{1,0:T(8,128)S(1)}, f32[28,2048]{1,0:T(8,128)}, u32[]{:S(2)}, u32[]{:S(2)}) %collective-permute-start.2) | collective-permute-done | bytes 229408
  3101.6 9.1 concatenate.43
  3116.5 5.0 collective-permute-start.5
  3121.5 41.1 %collective-permute-done.5 = f32[28,2048]{1,0:T(8,128)S(1)} collective-permute-done((f32[28,2048]{1,0:T(8,128)S(1)}, f32[28,2048]{1,0:T(8,128)S(1)}, u32[]{:S(2)}, u32[]{:S(2)}) %collective-permute-start.5) | collective-permute-done | bytes 229408
  3162.8 8.2 concatenate.44
  3182.8 25.8 collective-permute-done.8
  3209.4 4.2 concatenate.45
  3232.6 5.8 fusion.61
  3244.7 28.0 all-gather.56.cloned.1.call-done
  3279.6 121.5 %reduce-scatter.40.cloned.1.call-done = f32[64,64]{1,0:T(8,128)} async-done(((f32[2048,64]{1,0:T(8,128)}), f32[64,64]{1,0:T(8,128)}) %reduce-scatter.40.cloned.1.call-update) | async-done | bytes 16400
  3401.1 15.2 all_gather.100
  3417.3 6.6 fusion.4
  3427.0 40.3 %all-reduce.13 = (f32[2048]{0:T(1024)S(1)}, f32[512]{0:T(512)S(1)}, f32[2048]{0:T(1024)S(1)}) all-reduce(f32[2048]{0:T(1024)S(1)} %reshape.453, f32[512]{0:T(512)S(1)} %reshape.457, f32[2048]{0:T(1024)S(1)} %reshape.462), channel_id=8, replica_groups=mesh['rep'=8,'shard'=4] {'rep','shard'}, use_global_device_ids=true, to_apply=%region_25.26.clone | all-reduce | flops 4608 | bytes 36864
  3467.8 14.5 all-reduce.14
  3488.2 14.3 all-gather.50.cloned.1.call-done
  3502.5 47.4 %all-gather.44.cloned.1.call-done = f32[3072,512]{0,1:T(8,128)} async-done(((f32[3072,64]{0,1:T(8,128)}), f32[3072,512]{0,1:T(8,128)}) %all-gather.44.cloned.1.call-update) | async-done | bytes 6291472 | tf_op jit(solution)/shard_map/all_gather | solution.py:461
  3549.9 6.6 copy.420
  3556.5 221.2 %all-reduce.19.cloned.1.call-done = (f32[2,352,2048]{2,1,0:T(8,128)}, f32[2,352,2048]{2,1,0:T(8,128)}, f32[2,352,2048]{2,1,0:T(8,128)}) async-done(((f32[2,352,2048]{2,1,0:T(8,128)}, f32[2,352,2048]{2,1,0:T(8,128)}, f32[2,352,2048]{2,1,0:T(8,128)}), (f32[2,352,2048]{2,1,0:T(8,128)}, f32[2,352,2048]{2,1,0:T(8,128)}, f32[2,352,2048]{2,1,0:T(8,128)})) %all-reduce.19.cloned.1.call-update) | async-done | bytes 17301520 | tf_op jit(solution)/shard_map/psum | solution.py:472
  3779.0 5.9 copy.517
  (482 shorter events, 232.7 us)
Async XLA Ops:
  7.2 52.8 %all-gather.24.cloned.1.call-start = ((), (), s32[]{:S(2)}) async-start(), calls=%async_computation.11 | async-start | bytes 2949120 | tf_op jit(solution)/shard_map/all_gather | solution.py:144
  9.6 131.5 %all-gather.26.cloned.1.call-start = ((), (), s32[]{:S(2)}) async-start(), calls=%async_computation.12 | async-start | bytes 5242880 | tf_op jit(solution)/shard_map/all_gather | solution.py:146
  10.8 285.3 %all-gather.28.cloned.1.call-start = ((), (), s32[]{:S(2)}) async-start(), calls=%async_computation.13 | async-start | bytes 10485760 | tf_op jit(solution)/shard_map/all_gather | solution.py:168
  20.4 42.1 %copy-start.69 = (f32[4,1,512]{2,1,0:T(1,128)}, f32[4,1,512]{2,1,0:T(1,128)S(1)}, u32[]{:S(2)}) copy-start(f32[4,1,512]{2,1,0:T(1,128)S(1)} %convert_element_type.229) | copy-start | bytes 24580
  26.8 36.5 copy-start.92
  62.5 104.6 %copy-start.34 = (f32[2,128,576]{1,2,0:T(8,128)}, f32[2,128,576]{1,2,0:T(8,128)S(1)}, u32[]{:S(2)}) copy-start(f32[2,128,576]{1,2,0:T(8,128)S(1)} %fusion.71) | copy-start | bytes 1769476
  63.3 82.6 %copy-start.97 = (f32[2,128]{1,0:T(2,128)}, f32[2,128]{1,0:T(2,128)S(1)}, u32[]{:S(2)}) copy-start(f32[2,128]{1,0:T(2,128)S(1)} %get-tuple-element.295) | copy-start | bytes 3076
  63.4 82.4 %copy-start.43 = (bf16[2,128,512]{1,2,0:T(8,128)(2,1)}, bf16[2,128,512]{1,2,0:T(8,128)(2,1)S(1)}, u32[]{:S(2)}) copy-start(bf16[2,128,512]{1,2,0:T(8,128)(2,1)S(1)} %multiply_convert_fusion.7) | copy-start | bytes 786436
  145.9 368.6 %all-gather.30.cloned.1.call-start = ((), (), s32[]{:S(2)}) async-start(), calls=%async_computation.14 | async-start | bytes 15728640 | tf_op jit(solution)/shard_map/all_gather | solution.py:143
  150.8 513.5 %all-gather.32.cloned.1.call-start = ((), (), s32[]{:S(2)}) async-start(), calls=%async_computation.15 | async-start | bytes 10485760 | tf_op jit(solution)/shard_map/all_gather | solution.py:147
  154.7 546.5 %all-gather.40.cloned.1.call-start = ((), (), s32[]{:S(2)}) async-start(), calls=%async_computation.19 | async-start | bytes 1310720 | tf_op jit(solution)/shard_map/all_gather | solution.py:233
  166.1 505.0 %copy-start.71 = (f32[4,1,512]{2,1,0:T(1,128)}, f32[4,1,512]{2,1,0:T(1,128)S(1)}, u32[]{:S(2)}) copy-start(f32[4,1,512]{2,1,0:T(1,128)S(1)} %convert_element_type.231) | copy-start | bytes 24580
  166.8 504.5 %copy-start.85 = (pred[2,2,128]{2,1,0:T(4,128)(4,1)}, pred[2,2,128]{2,1,0:T(4,128)(4,1)S(1)}, u32[]{:S(2)}) copy-start(pred[2,2,128]{2,1,0:T(4,128)(4,1)S(1)} %broadcast_compare_fusion.1) | copy-start | bytes 1540
  166.8 504.5 %copy-start.77 = (s32[2,2,128]{2,1,0:T(2,128)}, s32[2,2,128]{2,1,0:T(2,128)S(1)}, u32[]{:S(2)}) copy-start(s32[2,2,128]{2,1,0:T(2,128)S(1)} %broadcast_add_fusion) | copy-start | bytes 6148
  167.0 355.0 %copy-start.66 = (f32[128,32]{0,1:T(8,128)}, f32[128,32]{0,1:T(8,128)S(1)}, u32[]{:S(2)}) copy-start(f32[128,32]{0,1:T(8,128)S(1)} %get-tuple-element.299) | copy-start | bytes 49156
  181.9 362.7 %copy-start.61 = (bf16[2,512,64]{1,2,0:T(8,128)(2,1)}, bf16[2,512,64]{1,2,0:T(8,128)(2,1)S(1)}, u32[]{:S(2)}) copy-start(bf16[2,512,64]{1,2,0:T(8,128)(2,1)S(1)} %all_gather.84) | copy-start | bytes 393220
  304.7 218.6 %copy-start.12 = (bf16[512,16,128]{2,1,0:T(8,128)(2,1)}, bf16[512,16,128]{2,1,0:T(8,128)(2,1)S(1)}, u32[]{:S(2)}) copy-start(bf16[512,16,128]{2,1,0:T(8,128)(2,1)S(1)} %get-tuple-element.273) | copy-start | bytes 6291460
  670.5 492.2 %copy-start.7 = (f32[2,128,2048]{2,1,0:T(8,128)}, f32[2,128,2048]{2,1,0:T(8,128)S(1)}, u32[]{:S(2)}) copy-start(f32[2,128,2048]{2,1,0:T(8,128)S(1)} %get-tuple-element.305) | copy-start | bytes 6291460
  672.3 85.6 %reduce-scatter.20.cloned.1.call-start = ((), (), s32[]{:S(2)}) async-start(), calls=%async_computation.20 | async-start | bytes 2621440 | tf_op jit(solution)/shard_map/reduce_scatter | solution.py:239
  712.7 80.2 %all-gather.42.cloned.1.call-start = ((), (), s32[]{:S(2)}) async-start(), calls=%async_computation.21 | async-start | bytes 1310720 | tf_op jit(solution)/shard_map/all_gather | solution.py:272
  764.6 134.3 %all-gather.38.cloned.1.call-start = ((), (), s32[]{:S(2)}) async-start(), calls=%async_computation.18 | async-start | bytes 7208960 | tf_op jit(solution)/shard_map/all_gather | solution.py:212
  767.8 238.3 %all-gather.36.cloned.1.call-start = ((), (), s32[]{:S(2)}) async-start(), calls=%async_computation.17 | async-start | bytes 7208960 | tf_op jit(solution)/shard_map/all_gather | solution.py:211
  771.0 341.8 %all-gather.34.cloned.1.call-start = ((), (), s32[]{:S(2)}) async-start(), calls=%async_computation.16 | async-start | bytes 7208960 | tf_op jit(solution)/shard_map/all_gather | solution.py:210
  774.3 383.8 %reduce-scatter.22.cloned.1.call-start = ((), (), s32[]{:S(2)}) async-start(), calls=%async_computation.22 | async-start | bytes 2621440 | tf_op jit(solution)/shard_map/reduce_scatter | solution.py:289
  803.2 101.6 %copy-start.74 = (f32[16,128]{1,0:T(8,128)S(1)}, f32[16,128]{1,0:T(8,128)}, u32[]{:S(2)}) copy-start(f32[16,128]{1,0:T(8,128)} %copy-done.73) | copy-start | bytes 24580
  803.2 101.6 %copy-start.82 = (f32[16,128]{1,0:T(8,128)S(1)}, f32[16,128]{1,0:T(8,128)}, u32[]{:S(2)}) copy-start(f32[16,128]{1,0:T(8,128)} %copy-done.81) | copy-start | bytes 24580
  803.2 101.6 %copy-start.76 = (f32[16,128]{1,0:T(8,128)S(1)}, f32[16,128]{1,0:T(8,128)}, u32[]{:S(2)}) copy-start(f32[16,128]{1,0:T(8,128)} %copy-done.75) | copy-start | bytes 24580
  803.2 101.6 %copy-start.84 = (f32[16,128]{1,0:T(8,128)S(1)}, f32[16,128]{1,0:T(8,128)}, u32[]{:S(2)}) copy-start(f32[16,128]{1,0:T(8,128)} %copy-done.83) | copy-start | bytes 24580
  803.3 431.7 %reduce-scatter.30.cloned.1.call-start = ((), (), s32[]{:S(2)}) async-start(), calls=%async_computation.26 | async-start | bytes 163840 | tf_op jit(solution)/shard_map/reduce_scatter | solution.py:401
  1122.7 35.4 copy-start.78
  1122.7 35.4 copy-start.86
  1125.9 35.3 copy-start.95
  1185.1 49.8 %reduce-scatter.28.cloned.1.call-start = ((), (), s32[]{:S(2)}) async-start(), calls=%async_computation.25 | async-start | bytes 163840 | tf_op jit(solution)/shard_map/reduce_scatter | solution.py:401
  1194.3 176.7 %reduce-scatter.26.cloned.1.call-start = ((), (), s32[]{:S(2)}) async-start(), calls=%async_computation.24 | async-start | bytes 10485760 | tf_op jit(solution)/shard_map/reduce_scatter | solution.py:400
  1211.5 306.9 %reduce-scatter.24.cloned.1.call-start = ((), (), s32[]{:S(2)}) async-start(), calls=%async_computation.23 | async-start | bytes 10485760 | tf_op jit(solution)/shard_map/reduce_scatter | solution.py:400
  1229.7 1987.0 %reduce-scatter.34.cloned.1.call-start = ((), (), s32[]{:S(2)}) async-start(), calls=%async_computation.29 | async-start | bytes 5406720 | tf_op jit(solution)/shard_map/reduce_scatter | solution.py:449
  1373.7 146.6 %copy-start.93 = (f32[4,1,128]{2,1,0:T(1,128)S(1)}, f32[4,1,128]{2,1,0:T(1,128)}, u32[]{:S(2)}) copy-start(f32[4,1,128]{2,1,0:T(1,128)} %copy-done.92) | copy-start | bytes 6148
  1373.7 146.6 %copy-start.98 = (f32[2,128]{1,0:T(2,128)S(1)}, f32[2,128]{1,0:T(2,128)}, u32[]{:S(2)}) copy-start(f32[2,128]{1,0:T(2,128)} %copy-done.97) | copy-start | bytes 3076
  1529.3 1688.2 %reduce-scatter.36.cloned.1.call-start = ((), (), s32[]{:S(2)}) async-start(), calls=%async_computation.31 | async-start | bytes 8650752 | tf_op jit(solution)/shard_map/reduce_scatter | solution.py:451
  1536.4 1681.6 %reduce-scatter.38.cloned.1.call-start = ((), (), s32[]{:S(2)}) async-start(), calls=%async_computation.33 | async-start | bytes 17301504 | tf_op jit(solution)/shard_map/reduce_scatter | solution.py:452
  1545.8 1672.8 %reduce-scatter.32.cloned.1.call-start = ((), (), s32[]{:S(2)}) async-start(), calls=%async_computation.27 | async-start | bytes 25952256 | tf_op jit(solution)/shard_map/reduce_scatter | solution.py:448
  1565.8 1672.7 %all-gather.52.cloned.1.call-start = ((), (), s32[]{:S(2)}) async-start(), calls=%async_computation.35 | async-start | bytes 3538944 | tf_op jit(solution)/shard_map/all_gather | solution.py:468
  3034.4 67.2 %collective-permute-start.1 = (f32[48,2048]{1,0:T(8,128)S(1)}, f32[48,2048]{1,0:T(8,128)S(1)}, u32[]{:S(2)}, u32[]{:S(2)}) collective-permute-start(f32[48,2048]{1,0:T(8,128)S(1)} %get-tuple-element.262), channel_id=1, source_target_pairs={{0,2},{1,3},{2,4},{3,5},{4,6},{5,7},{6,8},{7,9},{8,10},{9,11},{10,... | collective-permute-start | bytes 1179656
  3036.7 64.9 %collective-permute-start = (f32[48,2048]{1,0:T(8,128)S(1)}, f32[48,2048]{1,0:T(8,128)S(1)}, u32[]{:S(2)}, u32[]{:S(2)}) collective-permute-start(f32[48,2048]{1,0:T(8,128)S(1)} %get-tuple-element.262), channel_id=1, source_target_pairs={{0,1},{1,2},{2,3},{3,4},{4,5},{5,6},{6,7},{7,8},{8,9},{9,10},{10,1... | collective-permute-start | bytes 1179656
  3042.2 59.5 %collective-permute-start.2 = (f32[28,2048]{1,0:T(8,128)S(1)}, f32[28,2048]{1,0:T(8,128)}, u32[]{:S(2)}, u32[]{:S(2)}) collective-permute-start(f32[28,2048]{1,0:T(8,128)S(1)} %slice.179), channel_id=1, source_target_pairs={{0,3},{1,4},{2,5},{3,6},{4,7},{5,8},{6,9},{7,10},{8,11},{9,12},{10... | collective-permute-start | bytes 688136
  3112.6 129.0 %all-gather.54.cloned.1.call-start = ((), (), s32[]{:S(2)}) async-start(), calls=%async_computation.36 | async-start | bytes 3538944 | tf_op jit(solution)/shard_map/all_gather | solution.py:469
  3112.7 49.9 %collective-permute-start.4 = (f32[48,2048]{1,0:T(8,128)S(1)}, f32[48,2048]{1,0:T(8,128)S(1)}, u32[]{:S(2)}, u32[]{:S(2)}) collective-permute-start(f32[48,2048]{1,0:T(8,128)S(1)} %get-tuple-element.263), channel_id=1, source_target_pairs={{0,2},{1,3},{2,4},{3,5},{4,6},{5,7},{6,8},{7,9},{8,10},{9,11},{10,... | collective-permute-start | bytes 1179656
  3114.6 48.2 %collective-permute-start.3 = (f32[48,2048]{1,0:T(8,128)S(1)}, f32[48,2048]{1,0:T(8,128)S(1)}, u32[]{:S(2)}, u32[]{:S(2)}) collective-permute-start(f32[48,2048]{1,0:T(8,128)S(1)} %get-tuple-element.263), channel_id=1, source_target_pairs={{0,1},{1,2},{2,3},{3,4},{4,5},{5,6},{6,7},{7,8},{8,9},{9,10},{10,1... | collective-permute-start | bytes 1179656
  3116.5 46.0 %collective-permute-start.5 = (f32[28,2048]{1,0:T(8,128)S(1)}, f32[28,2048]{1,0:T(8,128)S(1)}, u32[]{:S(2)}, u32[]{:S(2)}) collective-permute-start(f32[28,2048]{1,0:T(8,128)S(1)} %slice.180), channel_id=1, source_target_pairs={{0,3},{1,4},{2,5},{3,6},{4,7},{5,8},{6,9},{7,10},{8,11},{9,12},{10... | collective-permute-start | bytes 688136
  3172.8 99.9 %all-gather.56.cloned.1.call-start = ((), (), s32[]{:S(2)}) async-start(), calls=%async_computation.37 | async-start | bytes 3538944 | tf_op jit(solution)/shard_map/all_gather | solution.py:470
  3172.9 35.8 collective-permute-start.7
  3174.8 34.6 collective-permute-start.6
  3178.7 29.9 collective-permute-start.8
  3214.4 186.7 %reduce-scatter.40.cloned.1.call-start = ((), (), s32[]{:S(2)}) async-start(), calls=%async_computation.38 | async-start | bytes 1081344
  3216.6 268.9 %all-gather.46.cloned.1.call-start = ((), (), s32[]{:S(2)}) async-start(), calls=%async_computation.30 | async-start | bytes 1474560 | tf_op jit(solution)/shard_map/all_gather | solution.py:462
  3217.4 270.8 %all-gather.48.cloned.1.call-start = ((), (), s32[]{:S(2)}) async-start(), calls=%async_computation.32 | async-start | bytes 2359296 | tf_op jit(solution)/shard_map/all_gather | solution.py:464
  3218.0 284.5 %all-gather.50.cloned.1.call-start = ((), (), s32[]{:S(2)}) async-start(), calls=%async_computation.34 | async-start | bytes 4718592 | tf_op jit(solution)/shard_map/all_gather | solution.py:465
  3218.6 331.4 %all-gather.44.cloned.1.call-start = ((), (), s32[]{:S(2)}) async-start(), calls=%async_computation.28 | async-start | bytes 7077888 | tf_op jit(solution)/shard_map/all_gather | solution.py:461
  3219.3 558.3 %all-reduce.19.cloned.1.call-start = ((), (), s32[]{:S(2)}) async-start(), calls=%async_computation.39 | async-start | bytes 34603008 | tf_op jit(solution)/shard_map/psum | solution.py:472
  3275.8 141.3 %copy-start.80 = (f32[2048]{0:T(1024)S(1)}, f32[2048]{0:T(1024)}, u32[]{:S(2)}) copy-start(f32[2048]{0:T(1024)} %get-tuple-element.244) | copy-start | bytes 24580
  3275.8 141.5 %copy-start.21 = (bf16[2,128,16,192]{1,3,2,0:T(8,128)(2,1)S(1)}, bf16[2,128,16,192]{1,3,2,0:T(8,128)(2,1)}, u32[]{:S(2)}) copy-start(bf16[2,128,16,192]{1,3,2,0:T(8,128)(2,1)} %copy-done.20) | copy-start | bytes 4718596
  3424.0 58.3 %copy-start.11 = (f32[2,128,2048]{2,1,0:T(8,128)S(1)}, f32[2,128,2048]{2,1,0:T(8,128)}, u32[]{:S(2)}) copy-start(f32[2,128,2048]{2,1,0:T(8,128)} %copy-done.9) | copy-start | bytes 6291460
  3424.0 58.3 %copy-start.100 = (f32[2,128]{1,0:T(2,128)S(1)}, f32[2,128]{1,0:T(2,128)}, u32[]{:S(2)}) copy-start(f32[2,128]{1,0:T(2,128)} %get-tuple-element.292) | copy-start | bytes 3076
  3488.2 289.4 %copy-start.50 = (f32[128,4096]{1,0:T(8,128)S(1)}, f32[128,4096]{1,0:T(8,128)}, u32[]{:S(2)}) copy-start(f32[128,4096]{1,0:T(8,128)} %all-gather.48.cloned.1.call-done) | copy-start | bytes 6291460
  (93 other events, 671.4 us)
Sparse Core Ops, SparseCore 0:
  10.2 49.8 all-gather.23
  62.2 78.8 all-gather.25
  146.0 150.0 all-gather.27
  298.1 216.3 all-gather.29
  516.5 147.8 all-gather.31
  672.5 28.7 all-gather.39
  712.9 45.0 reduce-scatter.19
  764.7 28.2 all-gather.41
  795.2 103.6 all-gather.37
  901.0 105.0 all-gather.35
  1007.7 104.9 all-gather.33
  1115.6 42.4 reduce-scatter.21
  1185.3 16.3 reduce-scatter.29
  1204.4 17.3 reduce-scatter.27
  1224.0 146.9 reduce-scatter.25
  1373.2 145.1 reduce-scatter.23
  1529.4 187.4 reduce-scatter.33
  1719.1 365.1 reduce-scatter.35
  2086.6 705.7 reduce-scatter.37
  2798.7 361.6 reduce-scatter.31
  3163.0 35.5 all-gather.51
  3201.2 36.4 all-gather.53
  3240.3 32.3 all-gather.55
  3275.4 125.6 reduce-scatter.39
  3403.0 30.8 all-gather.45
  3435.7 28.1 all-gather.47
  3465.6 36.8 all-gather.49
  3504.4 45.5 all-gather.43
  3554.7 222.8 all-reduce.18
where the time goes:
time: 3810 us; the launch traced here: 3800 us
  waiting for transfers between devices  1790 us (47%)
  blocking collectives  1570 us (41%)
  matrix products  194 us (5%)
  local copies, waits for them, and re-layouts  149 us (4%)
  other arithmetic  57.9 us (2%)
    unnamed x3, blocking collectives  1500 us
    reduce_scatter x2, waiting for transfers between devices, shards(): lax.psum_scatter(key_grad_rows, 'shard', scatter_dimension=0, tiled=True)  280 us
    unnamed x39, waiting for transfers between devices  249 us
    psum x1, waiting for transfers between devices, shards(): lax.psum((expert_gate_grad, expert_up_grad, expert_down_grad), 'rep')  221 us
    all_gather x1, waiting for transfers between devices, shards(): lax.all_gather(q_weight.astype(jnp.bfloat16), 'shard', axis=1, tiled=True)  205 us
    all_gather x1, waiting for transfers between devices, shards(): lax.all_gather(kv_up, 'shard', axis=1, tiled=True)  114 us
    all_gather x1, waiting for transfers between devices, shards(): lax.all_gather(out_weight.astype(jnp.bfloat16), 'shard', axis=0, tiled=True)  112 us
    all_gather x1, waiting for transfers between devices, shards(): lax.all_gather(shared_up.astype(jnp.bfloat16), 'shard', axis=0, tiled=True)  101 us
  transfers between devices with their start and end apart: 38, of which 23 were waited for; matrix products, arithmetic and copies ran while one was open for 46% of the time, Pallas kernels for 0%

commit v1 on v0

v1 whole, which is shorter than its diff:
```python
import functools

import jax
import jax.numpy as jnp
from jax import lax
from jax.experimental import pallas as pl
from jax.experimental.pallas import tpu as pltpu
from jax.sharding import PartitionSpec as P

HEADS = 16
NOPE = 128
ROPE = 64
VDIM = 128
RANK = 512
EXPERTS = 64
EXP_WIN = 2
MASK_BLOCK = 256
CAP = 16

epsilon = 1e-06
rope_base = 10000.0
masked_score = -1e30
highest = lax.Precision.HIGHEST
bf16 = jnp.bfloat16
f32 = jnp.float32
MESH = pl.DeviceIdType.MESH
HBM = pltpu.HBM
HALF_ROPE = ROPE // 2
HEAD_GROUP = 4
GROUP_LANES = HEAD_GROUP * HALF_ROPE


def dot(a, b, ca, cb):
    return lax.dot_general(a, b, (((ca,), (cb,)), ((), ())), preferred_element_type=f32)


def rms_scale(tensor):
    return lax.rsqrt(jnp.mean(tensor * tensor, axis=-1, keepdims=True) + epsilon)


def norm_back(tensor, inv_rms, gain_vec, gradient):
    scaled_grad = gradient * gain_vec
    inner_mean = jnp.mean(scaled_grad * tensor, axis=-1, keepdims=True)
    input_part = inv_rms * scaled_grad - tensor * (inv_rms * inv_rms * inv_rms) * inner_mean
    gain_part = jnp.sum(gradient * tensor * inv_rms, axis=0)
    return (input_part, gain_part)


def swiglu_back(gate_pre, up_pre, hidden_grad):
    sigmoid_gate = jax.nn.sigmoid(gate_pre)
    silu_gate = gate_pre * sigmoid_gate
    slope = sigmoid_gate * (1.0 + gate_pre * (1.0 - sigmoid_gate))
    return (
        (hidden_grad * up_pre * slope).astype(bf16),
        (hidden_grad * silu_gate).astype(bf16),
    )


def head_scores(qn, q1, q2, kv, k1, k2, limit, scale, head):
    lane = lax.broadcasted_iota(jnp.int32, (1, GROUP_LANES), 1)
    mine = (lane >= head * HALF_ROPE) & (lane < (head + 1) * HALF_ROPE)
    width = NOPE + VDIM
    q_head = qn[:, head * NOPE : (head + 1) * NOPE]
    k_head = kv[:, head * width : head * width + NOPE]
    v_head = kv[:, head * width + NOPE : (head + 1) * width]
    q1m = jnp.where(mine, q1, jnp.zeros_like(q1))
    q2m = jnp.where(mine, q2, jnp.zeros_like(q2))
    scores = dot(q_head, k_head, 1, 1) + dot(q1m, k1, 1, 1) + dot(q2m, k2, 1, 1)
    column = lax.broadcasted_iota(jnp.int32, scores.shape, 1)
    scores = jnp.where(column < limit, scores * scale, masked_score)
    top = jnp.max(scores, axis=-1, keepdims=True)
    expo = jnp.exp(scores - top)
    probs = expo / jnp.sum(expo, axis=-1, keepdims=True)
    return probs, q_head, k_head, v_head, q1m, q2m, mine


def attend_kernel(scale, lim_ref, qn_ref, q1_ref, q2_ref, lat_ref, k1_ref, k2_ref, kvb_ref, out_ref):
    kv = dot(lat_ref[0], kvb_ref[...], 1, 0).astype(bf16)
    for head in range(HEAD_GROUP):
        probs, _, _, v_head, _, _, _ = head_scores(
            qn_ref[0], q1_ref[0], q2_ref[0], kv, k1_ref[0], k2_ref[0], lim_ref[0], scale, head
        )
        out_ref[0, :, head * VDIM : (head + 1) * VDIM] = dot(
            probs.astype(bf16), v_head, 1, 0
        ).astype(bf16)


def attend_back_kernel(
    scale,
    lim_ref,
    qn_ref,
    q1_ref,
    q2_ref,
    lat_ref,
    k1_ref,
    k2_ref,
    kvb_ref,
    do_ref,
    dqn_ref,
    dq1_ref,
    dq2_ref,
    dlat_ref,
    dk1_ref,
    dk2_ref,
    dkvb_ref,
    kvg_ref,
    acc_ref,
):
    group, micro = pl.program_id(0), pl.program_id(1)
    width = NOPE + VDIM

    @pl.when(group == 0)
    def _():
        dlat_ref[micro] = jnp.zeros(dlat_ref.shape[1:], f32)
        dk1_ref[micro] = jnp.zeros(dk1_ref.shape[1:], f32)
        dk2_ref[micro] = jnp.zeros(dk2_ref.shape[1:], f32)

    lat = lat_ref[0]
    kvb = kvb_ref[...]
    kv = dot(lat, kvb, 1, 0).astype(bf16)
    k1, k2 = k1_ref[0], k2_ref[0]
    dq1 = jnp.zeros(dq1_ref.shape[1:], f32)
    dq2 = jnp.zeros(dq2_ref.shape[1:], f32)
    dk1 = jnp.zeros(k1.shape, f32)
    dk2 = jnp.zeros(k2.shape, f32)
    for head in range(HEAD_GROUP):
        probs, q_head, k_head, v_head, q1m, q2m, mine = head_scores(
            qn_ref[0], q1_ref[0], q2_ref[0], kv, k1, k2, lim_ref[0], scale, head
        )
        d_out = do_ref[0, :, head * VDIM : (head + 1) * VDIM]
        dprobs = dot(d_out, v_head, 1, 1)
        delta = jnp.sum(probs * dprobs, axis=-1, keepdims=True)
        ds = (probs * (dprobs - delta)).astype(bf16)
        dqn_ref[0, :, head * NOPE : (head + 1) * NOPE] = (dot(ds, k_head, 1, 0) * scale).astype(bf16)
        dq1 = dq1 + jnp.where(mine, dot(ds, k1, 1, 0), 0.0)
        dq2 = dq2 + jnp.where(mine, dot(ds, k2, 1, 0), 0.0)
        dk1 = dk1 + dot(ds, q1m, 0, 0)
        dk2 = dk2 + dot(ds, q2m, 0, 0)
        kvg_ref[:, head * width : head * width + NOPE] = (dot(ds, q_head, 0, 0) * scale).astype(bf16)
        kvg_ref[:, head * width + NOPE : (head + 1) * width] = dot(
            probs.astype(bf16), d_out, 0, 0
        ).astype(bf16)
    dq1_ref[0] = dq1 * scale
    dq2_ref[0] = dq2 * scale
    dk1_ref[micro] += dk1 * scale
    dk2_ref[micro] += dk2 * scale
    kvg = kvg_ref[...]
    dlat_ref[micro] += dot(kvg, kvb, 1, 1)
    part = dot(lat, kvg, 0, 0)

    @pl.when(micro == 0)
    def _():
        acc_ref[...] = part

    @pl.when(micro > 0)
    def _():
        acc_ref[...] += part

    @pl.when(micro == pl.num_programs(1) - 1)
    def _():
        dkvb_ref[...] = acc_ref[...].astype(bf16)


def attention_specs(micros, rows, length):
    groups = HEADS // HEAD_GROUP
    wide = HEAD_GROUP * NOPE
    specs = [
        pl.BlockSpec(memory_space=pltpu.SMEM),
        pl.BlockSpec((1, rows, wide), lambda g, m: (m, 0, g)),
        pl.BlockSpec((1, rows, GROUP_LANES), lambda g, m: (m, 0, g)),
        pl.BlockSpec((1, rows, GROUP_LANES), lambda g, m: (m, 0, g)),
        pl.BlockSpec((1, length, RANK), lambda g, m: (m, 0, 0)),
        pl.BlockSpec((1, length, GROUP_LANES), lambda g, m: (m, 0, 0)),
        pl.BlockSpec((1, length, GROUP_LANES), lambda g, m: (m, 0, 0)),
        pl.BlockSpec((RANK, HEAD_GROUP * (NOPE + VDIM)), lambda g, m: (0, g)),
    ]
    return (groups, micros), specs, pl.BlockSpec((1, rows, wide), lambda g, m: (m, 0, g))


def attend(limit, qn, q1, q2, lat, k1, k2, kvb, scale):
    micros, rows, _ = qn.shape
    length = lat.shape[1]
    grid, specs, out_spec = attention_specs(micros, rows, length)
    return pl.pallas_call(
        functools.partial(attend_kernel, scale),
        grid=grid,
        in_specs=specs,
        out_specs=out_spec,
        out_shape=jax.ShapeDtypeStruct(qn.shape, bf16),
        compiler_params=pltpu.CompilerParams(vmem_limit_bytes=48 << 20),
        name="attend",
    )(limit, qn, q1, q2, lat, k1, k2, kvb)


def attend_back(limit, qn, q1, q2, lat, k1, k2, kvb, d_out, scale):
    micros, rows, _ = qn.shape
    length = lat.shape[1]
    grid, specs, out_spec = attention_specs(micros, rows, length)
    whole = lambda g, m: (0, 0, 0)
    return pl.pallas_call(
        functools.partial(attend_back_kernel, scale),
        grid=grid,
        in_specs=specs + [out_spec],
        out_specs=[
            out_spec,
            pl.BlockSpec((1, rows, GROUP_LANES), lambda g, m: (m, 0, g)),
            pl.BlockSpec((1, rows, GROUP_LANES), lambda g, m: (m, 0, g)),
            pl.BlockSpec(lat.shape, whole),
            pl.BlockSpec(k1.shape, whole),
            pl.BlockSpec(k2.shape, whole),
            pl.BlockSpec((RANK, HEAD_GROUP * (NOPE + VDIM)), lambda g, m: (0, g)),
        ],
        out_shape=[
            jax.ShapeDtypeStruct(qn.shape, bf16),
            jax.ShapeDtypeStruct(q1.shape, f32),
            jax.ShapeDtypeStruct(q2.shape, f32),
            jax.ShapeDtypeStruct(lat.shape, f32),
            jax.ShapeDtypeStruct(k1.shape, f32),
            jax.ShapeDtypeStruct(k2.shape, f32),
            jax.ShapeDtypeStruct(kvb.shape, bf16),
        ],
        scratch_shapes=[
            pltpu.VMEM((length, HEAD_GROUP * (NOPE + VDIM)), bf16),
            pltpu.VMEM((RANK, HEAD_GROUP * (NOPE + VDIM)), f32),
        ],
        compiler_params=pltpu.CompilerParams(vmem_limit_bytes=48 << 20),
        name="attend_back",
    )(limit, qn, q1, q2, lat, k1, k2, kvb, d_out)


class Place:
    def __init__(self):
        self.r = lax.axis_index("rep")
        self.z = lax.axis_index("shard")
        self.core = self.r % 2
        self.chip = self.r // 2
        self.x = self.chip % 2
        self.y = self.chip // 2
        self.peer = (self.r + 1 - 2 * self.core, self.z)
        self.across = {
            "x": (self.r + 2 - 4 * self.x, self.z),
            "y": (self.r + 4 - 8 * self.y, self.z),
        }
        cx = self.chip + 1 - 2 * self.x
        cy = self.chip + 2 - 4 * self.y
        self.chips = {"": self.chip, "x": cx, "y": cy, "xy": cx + 2 - 4 * self.y}

    def along(self, step):
        return (self.r, (self.z + step) % 4)

    def shard_at(self, step):
        return (self.z + step) % 4


class Sems:
    def __init__(self, send, recv):
        self.send, self.recv = send, recv
        self.count = 0
        self.pending = []

    def slot(self):
        self.count += 1
        return self.count - 1

    def copy(self, src, dst, slot, device):
        return pltpu.make_async_remote_copy(
            src_ref=src,
            dst_ref=dst,
            send_sem=self.send.at[slot],
            recv_sem=self.recv.at[slot],
            device_id=device,
            device_id_type=MESH,
        )

    def push(self, src, dst, slot, device):
        copy = self.copy(src, dst, slot, device)
        copy.start()
        self.pending.append(copy)

    def arrived(self, dst, slot, device):
        self.copy(dst, dst, slot, device).wait_recv()

    def drain(self):
        for copy in self.pending:
            copy.wait_send()
        self.pending = []


def greet(devices):
    barrier = pltpu.get_barrier_semaphore()
    for device in devices:
        pl.semaphore_signal(barrier, inc=1, device_id=device, device_id_type=MESH)
    pl.semaphore_wait(barrier, len(devices))


def lanes(start, size):
    return pl.ds(pl.multiple_of(start, 128), size)


def rows16(start, size):
    return pl.ds(pl.multiple_of(start, 16), size)


class PlaneGather:
    def __init__(self, sems, place, part, half, by):
        self.sems, self.place, self.part, self.half, self.by = sems, place, part, half, by
        self.slots = {k: sems.slot() for k in ("x", "y", "xy", "core")}

    def first(self, src=None):
        p = self.place
        mine = self.part(p.core, p.chip)
        for axis in ("x", "y"):
            self.sems.push(mine if src is None else src, mine, self.slots[axis], p.across[axis])

    def second(self):
        p = self.place
        for axis in ("x", "y"):
            got = self.part(p.core, p.chips[axis])
            self.sems.arrived(got, self.slots[axis], p.across[axis])
        via = self.by
        other = "y" if via == "x" else "x"
        got = self.part(p.core, p.chips[via])
        self.sems.push(got, got, self.slots["xy"], p.across[other])

    def third(self):
        p = self.place
        got = self.part(p.core, p.chips["xy"])
        self.sems.arrived(got, self.slots["xy"], p.across["y" if self.by == "x" else "x"])
        half = self.half(p.core)
        self.sems.push(half, half, self.slots["core"], p.peer)

    def fourth(self):
        p = self.place
        self.sems.arrived(self.half(1 - p.core), self.slots["core"], p.peer)


def weight_regions(place, refs, shard):
    q, kr, kvb, out, sh = refs
    ds = q.shape[1] // 4
    cols = lanes(shard * ds, ds)

    def row_split(ref, n):
        half = ref.shape[0] // 2
        return (
            lambda core, chip: ref.at[rows16(core * half + chip * n, n), cols],
            lambda core: ref.at[rows16(core * half, half), cols],
        )

    def col_split(ref, full):
        rows = full // 4
        half = ref.shape[-1] // 2
        n = half // 4
        lead = (slice(None),) * (len(ref.shape) - 2)
        span = rows16(shard * rows, rows)
        return (
            lambda core, chip: ref.at[(*lead, span, lanes(core * half + chip * n, n))],
            lambda core: ref.at[(*lead, span, lanes(core * half, half))],
        )

    return [
        row_split(q, q.shape[0] // 8),
        row_split(kr, kr.shape[0] // 8),
        col_split(kvb, kvb.shape[0]),
        col_split(out, out.shape[0]),
        col_split(sh, sh.shape[1]),
    ]


def own_part(refs, place):
    q, kr, kvb, out, sh = refs
    res = []
    for ref in (q, kr):
        n = ref.shape[0] // 8
        res.append(ref.at[rows16(place.core * 4 * n + place.chip * n, n)])
    for ref in (kvb, out, sh):
        n = ref.shape[-1] // 8
        lead = (slice(None),) * (len(ref.shape) - 1)
        res.append(ref.at[(*lead, lanes(place.core * 4 * n + place.chip * n, n))])
    return res


ITEMS = 5
GATHER_SEMS = 1 + 3 + ITEMS * (3 + 3 * 4)


def gather_kernel(*refs):
    ins, gain = refs[:ITEMS], refs[ITEMS]
    outs, gains = refs[ITEMS + 1 : 2 * ITEMS + 1], refs[2 * ITEMS + 1]
    send, recv, local = refs[2 * ITEMS + 2 :]
    place = Place()
    sems = Sems(send, recv)
    greet([place.peer, place.across["x"], place.across["y"]] + [place.along(k) for k in (1, 2, 3)])
    mine = own_part(ins, place)
    ds = ins[0].shape[1]
    own = [
        outs[0].at[:, lanes(place.z * ds, ds)],
        outs[1].at[:, lanes(place.z * ds, ds)],
        outs[2].at[rows16(place.z * ins[2].shape[0], ins[2].shape[0])],
        outs[3].at[rows16(place.z * ins[3].shape[0], ins[3].shape[0])],
        outs[4].at[:, rows16(place.z * ins[4].shape[1], ins[4].shape[1])],
    ]
    kept = [pltpu.make_async_copy(ins[i], own[i], local.at[i]) for i in range(ITEMS)]
    kept.append(pltpu.make_async_copy(gain, gains.at[place.z], local.at[ITEMS]))
    zslots = [[sems.slot() for _ in range(3)] for _ in range(ITEMS + 1)]
    here = weight_regions(place, outs, place.z)
    for k in (1, 2, 3):
        sems.push(gain, gains.at[place.z], zslots[ITEMS][k - 1], place.along(k))
    for i in range(ITEMS):
        for k in (1, 2, 3):
            sems.push(mine[i], here[i][0](place.core, place.chip), zslots[i][k - 1], place.along(k))
    for copy in kept:
        copy.start()
    units = []
    flips = [["x", "y", "x"], ["x", "y", "y"], ["x", "y", "y"], ["x", "y", "x"], ["x", "y", "y"]]
    for i in range(ITEMS):
        for k in (1, 2, 3):
            shard = place.shard_at(4 - k)
            part, half = weight_regions(place, outs, shard)[i]
            units.append((i, k, part, PlaneGather(sems, place, part, half, flips[i][k - 1])))
    n = len(units)
    for step in range(n + 6):
        if step < n:
            i, k, part, g = units[step]
            sems.arrived(part(place.core, place.chip), zslots[i][k - 1], place.along(4 - k))
            g.first()
        if 0 <= step - 2 < n:
            units[step - 2][3].second()
        if 0 <= step - 4 < n:
            units[step - 4][3].third()
        if 0 <= step - 6 < n:
            units[step - 6][3].fourth()
    for k in (1, 2, 3):
        sems.arrived(gains.at[place.shard_at(4 - k)], zslots[ITEMS][k - 1], place.along(4 - k))
    sems.drain()
    for copy in kept:
        copy.wait()


def gather_weights(q, kr, kvb, out, sh, gain, fast):
    if not fast:
        every = lambda w, axis: lax.all_gather(w, "shard", axis=axis, tiled=True)
        return (
            every(q, 1),
            every(kr, 1),
            every(kvb, 0),
            every(out, 0),
            every(sh, 1),
            lax.all_gather(gain, "shard", axis=0),
        )
    shape = jax.ShapeDtypeStruct
    return pl.pallas_call(
        gather_kernel,
        in_specs=[pl.BlockSpec(memory_space=HBM)] * 6,
        out_specs=[pl.BlockSpec(memory_space=HBM)] * 6,
        out_shape=[
            shape((q.shape[0], q.shape[1] * 4), bf16),
            shape((kr.shape[0], kr.shape[1] * 4), bf16),
            shape((kvb.shape[0] * 4, kvb.shape[1]), bf16),
            shape((out.shape[0] * 4, out.shape[1]), bf16),
            shape((3, sh.shape[1] * 4, sh.shape[2]), bf16),
            shape((4,) + gain.shape, bf16),
        ],
        scratch_shapes=[
            pltpu.SemaphoreType.DMA((GATHER_SEMS + 32,)),
            pltpu.SemaphoreType.DMA((GATHER_SEMS + 32,)),
            pltpu.SemaphoreType.DMA((ITEMS + 1,)),
        ],
        compiler_params=pltpu.CompilerParams(collective_id=0, has_side_effects=True),
        name="gather_weights",
    )(q, kr, kvb, out, sh, gain)


def z_gather_kernel(count, *refs):
    ins, outs = refs[:count], refs[count : 2 * count]
    send, recv, local = refs[2 * count :]
    place = Place()
    sems = Sems(send, recv)
    greet([place.along(k) for k in (1, 2, 3)])

    def block(i, shard):
        rows = ins[i].shape[1]
        return outs[i].at[:, rows16(shard * rows, rows)]

    kept = [pltpu.make_async_copy(ins[i], block(i, place.z), local.at[i]) for i in range(count)]
    slots = [[sems.slot() for _ in range(3)] for _ in range(count)]
    for i in range(count):
        for k in (1, 2, 3):
            sems.push(ins[i], block(i, place.z), slots[i][k - 1], place.along(k))
        kept[i].start()
    for i in range(count):
        for k in (1, 2, 3):
            sems.arrived(block(i, place.shard_at(4 - k)), slots[i][k - 1], place.along(4 - k))
        kept[i].wait()
    sems.drain()


def z_gather(arrays, fast, ident):
    if not fast:
        return [lax.all_gather(a, "shard", axis=1, tiled=True) for a in arrays]
    count = len(arrays)
    return pl.pallas_call(
        functools.partial(z_gather_kernel, count),
        in_specs=[pl.BlockSpec(memory_space=HBM)] * count,
        out_specs=[pl.BlockSpec(memory_space=HBM)] * count,
        out_shape=[
            jax.ShapeDtypeStruct((a.shape[0], a.shape[1] * 4, a.shape[2]), a.dtype) for a in arrays
        ],
        scratch_shapes=[
            pltpu.SemaphoreType.DMA((3 * count,)),
            pltpu.SemaphoreType.DMA((3 * count,)),
            pltpu.SemaphoreType.DMA((count,)),
        ],
        compiler_params=pltpu.CompilerParams(collective_id=ident, has_side_effects=True),
        name="z_gather",
    )(*arrays)


def z_scatter_kernel(count, *refs):
    ins, outs = refs[:count], refs[count : 2 * count]
    send, recv, local = refs[2 * count :]
    place = Place()
    sems = Sems(send, recv)
    greet([place.along(k) for k in (1, 2, 3)])

    def block(i, shard):
        rows = ins[i].shape[1] // 4
        return ins[i].at[:, rows16(shard * rows, rows)]

    kept = [
        pltpu.make_async_copy(block(i, place.z), outs[i].at[0], local.at[i]) for i in range(count)
    ]
    slots = [[sems.slot() for _ in range(3)] for _ in range(count)]
    for i in range(count):
        for k in (1, 2, 3):
            sems.push(block(i, place.shard_at(k)), outs[i].at[k], slots[i][k - 1], place.along(k))
        kept[i].start()
    for i in range(count):
        for k in (1, 2, 3):
            sems.arrived(outs[i].at[k], slots[i][k - 1], place.along(4 - k))
        kept[i].wait()
    sems.drain()


def z_scatter(arrays, fast, ident):
    if not fast:
        return [
            lax.psum_scatter(a.astype(f32), "shard", scatter_dimension=1, tiled=True)
            for a in arrays
        ]
    count = len(arrays)
    parts = pl.pallas_call(
        functools.partial(z_scatter_kernel, count),
        in_specs=[pl.BlockSpec(memory_space=HBM)] * count,
        out_specs=[pl.BlockSpec(memory_space=HBM)] * count,
        out_shape=[
            jax.ShapeDtypeStruct((4, a.shape[0], a.shape[1] // 4, a.shape[2]), a.dtype)
            for a in arrays
        ],
        scratch_shapes=[
            pltpu.SemaphoreType.DMA((3 * count,)),
            pltpu.SemaphoreType.DMA((3 * count,)),
            pltpu.SemaphoreType.DMA((count,)),
        ],
        compiler_params=pltpu.CompilerParams(collective_id=ident, has_side_effects=True),
        name="z_scatter",
    )(*arrays)
    return [jnp.sum(p.astype(f32), axis=0) for p in parts]


def swap_kernel(count, *refs):
    ins, outs = refs[:count], refs[count : 2 * count]
    send, recv, local = refs[2 * count :]
    place = Place()
    sems = Sems(send, recv)
    greet([place.peer])
    for i in range(count):
        sems.push(ins[i].at[1 - place.core], outs[i].at[1], sems.slot(), place.peer)
    kept = [
        pltpu.make_async_copy(ins[i].at[place.core], outs[i].at[0], local.at[i])
        for i in range(count)
    ]
    for copy in kept:
        copy.start()
    for i in range(count):
        sems.arrived(outs[i].at[1], i, place.peer)
    sems.drain()
    for copy in kept:
        copy.wait()


def core_swap(arrays, fast, ident):
    count = len(arrays)
    if not fast:
        reps = lax.axis_size("rep")
        core = lax.axis_index("rep") % 2
        res = []
        for a in arrays:
            keep = lax.dynamic_index_in_dim(a, core, 0, keepdims=False)
            give = lax.dynamic_index_in_dim(a, 1 - core, 0, keepdims=False)
            got = lax.ppermute(give, "rep", [(i, i ^ 1) for i in range(reps)])
            res.append(jnp.stack([keep, got]))
        return res
    return pl.pallas_call(
        functools.partial(swap_kernel, count),
        in_specs=[pl.BlockSpec(memory_space=HBM)] * count,
        out_specs=[pl.BlockSpec(memory_space=HBM)] * count,
        out_shape=[jax.ShapeDtypeStruct(a.shape, a.dtype) for a in arrays],
        scratch_shapes=[
            pltpu.SemaphoreType.DMA((count,)),
            pltpu.SemaphoreType.DMA((count,)),
            pltpu.SemaphoreType.DMA((count,)),
        ],
        compiler_params=pltpu.CompilerParams(collective_id=ident, has_side_effects=True),
        name="core_swap",
    )(*arrays)


def add_rows(dst, terms, rows):
    lead = dst.shape[:-2]
    steps = dst.shape[-2] // rows

    def body(step, carry):
        span = pl.ds(pl.multiple_of(step * rows, rows), rows)
        where = (slice(None),) * len(lead) + (span,)
        total = terms[0][where].astype(f32)
        for t in terms[1:]:
            total = total + t[where].astype(f32)
        dst[where] = total.astype(dst.dtype)
        return carry

    lax.fori_loop(0, steps, body, 0)


RS_ITEMS = 6
LOOK = 3


def reduce_kernel(*refs):
    grads, gain = refs[:RS_ITEMS], refs[RS_ITEMS]
    outs, gain_out = refs[RS_ITEMS + 1 : 2 * RS_ITEMS + 1], refs[2 * RS_ITEMS + 1]
    rest = refs[2 * RS_ITEMS + 2 :]
    own, got1, got2, got3 = (rest[i * RS_ITEMS : (i + 1) * RS_ITEMS] for i in range(4))
    gz, gp, gs, send, recv, load, keep = rest[4 * RS_ITEMS :]
    place = Place()
    sems = Sems(send, recv)
    others = [(place.chip * 2 + 1 - place.core, place.z)]
    for axes in ("x", "y", "xy"):
        for core in (0, 1):
            flip = place.core if core == 0 else 1 - place.core
            others.append((place.chips[axes] * 2 + flip, place.z))
    greet(others + [place.along(k) for k in (1, 2, 3)])

    def grad_part(i, s, chip):
        g = grads[i]
        if i < 2:
            n, ds = g.shape[0] // 4, g.shape[1] // 4
            return g.at[rows16(chip * n, n), lanes(s * ds, ds)]
        n = g.shape[-1] // 4
        if i == 5:
            return g.at[s, :, lanes(chip * n, n)]
        rows = g.shape[-2] // 4
        lead = (slice(None),) * (len(g.shape) - 2)
        return g.at[(*lead, rows16(s * rows, rows), lanes(chip * n, n))]

    def out_split(i):
        o = outs[i]
        if i < 2:
            half = o.shape[0] // 2
            n = half // 4
            return (
                lambda core, chip: o.at[rows16(core * half + chip * n, n)],
                lambda core: o.at[rows16(core * half, half)],
            )
        half = o.shape[-1] // 2
        n = half // 4
        lead = (slice(None),) * (len(o.shape) - 1)
        return (
            lambda core, chip: o.at[(*lead, lanes(core * half + chip * n, n))],
            lambda core: o.at[(*lead, lanes(core * half, half))],
        )

    gain_slots = [sems.slot() for _ in range(3 + 7)]
    for k in (1, 2, 3):
        sems.push(gain.at[place.shard_at(k)], gz.at[k], gain_slots[k - 1], place.along(k))
    first_gain = pltpu.make_async_copy(gain.at[place.z], gz.at[0], keep.at[RS_ITEMS])
    first_gain.start()

    order = [4, 5, 3, 2, 1, 0]
    units = []
    loads = 0
    for i in order:
        if i == 5:
            steps = [(u, u, None) for u in range(6)]
        else:
            steps = [(k % 4, place.shard_at(k), k % 4) for k in (1, 2, 3, 4)]
        for n, (u, s, k) in enumerate(steps):
            axis = "x" if (n + i) % 2 == 0 else "y"
            units.append(
                dict(
                    i=i,
                    u=u,
                    s=s,
                    k=k,
                    last=n == len(steps) - 1,
                    axis=axis,
                    other="y" if axis == "x" else "x",
                    slots=[sems.slot() for _ in range(4)],
                    loads=[loads, loads + 1],
                )
            )
            loads += 2
    for unit in units:
        i, u = unit["i"], unit["u"]
        unit["copies"] = [
            pltpu.make_async_copy(
                grad_part(i, unit["s"], place.chips["" if n == 0 else unit["other"]]),
                own[i].at[u, n],
                load.at[unit["loads"][n]],
            )
            for n in (0, 1)
        ]
        for copy in unit["copies"]:
            copy.start()

    def stage1(unit):
        i, u, axis = unit["i"], unit["u"], unit["axis"]
        for n, chip in enumerate((axis, "xy")):
            sems.push(
                grad_part(i, unit["s"], place.chips[chip]),
                got1[i].at[u, n],
                unit["slots"][n],
                place.across[axis],
            )

    def stage2(unit):
        i, u, axis, other = unit["i"], unit["u"], unit["axis"], unit["other"]
        for copy in unit["copies"]:
            copy.wait()
        for n in (1, 0):
            sems.arrived(got1[i].at[u, n], unit["slots"][n], place.across[axis])
            add_rows(own[i].at[u, n], [own[i].at[u, n], got1[i].at[u, n]], 16)
            if n == 1:
                sems.push(own[i].at[u, 1], got2[i].at[u], unit["slots"][2], place.across[other])

    def stage3(unit):
        i, u = unit["i"], unit["u"]
        sems.arrived(got2[i].at[u], unit["slots"][2], place.across[unit["other"]])
        add_rows(own[i].at[u, 0], [own[i].at[u, 0], got2[i].at[u]], 16)
        if unit["k"]:
            sems.push(
                own[i].at[u, 0],
                got3[i].at[unit["k"] - 1],
                unit["slots"][3],
                place.along(unit["k"]),
            )

    gathers = []

    def stage4(unit):
        i = unit["i"]
        if not unit["last"]:
            return
        part, half = out_split(i)
        mine = part(place.core, place.chip)
        if i == 5:
            src = own[i].at[:, 0]
        else:
            for other in units:
                if other["i"] == i and other["k"]:
                    k = other["k"]
                    sems.arrived(got3[i].at[k - 1], other["slots"][3], place.along(4 - k))
            src = own[i].at[0, 0]
            add_rows(src, [src] + [got3[i].at[n] for n in range(3)], 16)
        stay = pltpu.make_async_copy(src, mine, keep.at[i])
        stay.start()
        g = PlaneGather(sems, place, part, half, "x" if i % 2 == 0 else "y")
        g.first(src)
        gathers.append((g, stay))

    n = len(units)
    done = 0
    for step in range(n + 3 * LOOK):
        if step < n:
            stage1(units[step])
        if 0 <= step - LOOK < n:
            stage2(units[step - LOOK])
        if 0 <= step - 2 * LOOK < n:
            stage3(units[step - 2 * LOOK])
        if 0 <= step - 3 * LOOK < n:
            stage4(units[step - 3 * LOOK])
    first_gain.wait()
    for k in (1, 2, 3):
        sems.arrived(gz.at[k], gain_slots[k - 1], place.along(4 - k))
    gs[...] = gz[0] + gz[1] + gz[2] + gz[3]
    for n, device in enumerate(others):
        sems.push(gs, gp.at[n], gain_slots[3 + n], device)
    for g, stay in gathers:
        g.second()
    for g, stay in gathers:
        stay.wait()
        g.third()
    for g, stay in gathers:
        g.fourth()
    total = gs[...]
    for n, device in enumerate(others):
        sems.arrived(gp.at[n], gain_slots[3 + n], device)
        total = total + gp[n]
    gain_out[...] = total
    sems.drain()


def reduce_grads(grads, gain, fast):
    if not fast:
        core = lax.axis_index("rep") % 2

        def whole(g, axis):
            wide = jnp.zeros(g.shape[:axis] + (g.shape[axis] * 2,) + g.shape[axis + 1 :], f32)
            return lax.dynamic_update_slice_in_dim(
                wide, g.astype(f32), core * g.shape[axis], axis
            )

        q, kr, kvb, out, sh, ex = grads

        def total(g, axis, along):
            g = lax.psum_scatter(whole(g, axis), "shard", scatter_dimension=along, tiled=True)
            return lax.psum(g, "rep")

        return (
            total(q, 0, 1),
            total(kr, 0, 1),
            total(kvb, 1, 0),
            total(out, 1, 0),
            total(sh, 2, 1),
            lax.psum(whole(ex, 2), "rep"),
            lax.psum(lax.psum_scatter(gain, "shard", scatter_dimension=0, tiled=True), "rep")[0],
        )
    q, kr, kvb, out, sh, ex = grads
    shape = jax.ShapeDtypeStruct
    parts = [
        (q.shape[0] // 4, q.shape[1] // 4),
        (kr.shape[0] // 4, kr.shape[1] // 4),
        (kvb.shape[0] // 4, kvb.shape[1] // 4),
        (out.shape[0] // 4, out.shape[1] // 4),
        (3, sh.shape[1] // 4, sh.shape[2] // 4),
        (ex.shape[1], ex.shape[2] // 4),
    ]
    counts = [4] * 5 + [6]
    scratch = [pltpu.VMEM((n, 2) + p, bf16) for n, p in zip(counts, parts)]
    scratch += [pltpu.VMEM((n, 2) + p, bf16) for n, p in zip(counts, parts)]
    scratch += [pltpu.VMEM((n,) + p, bf16) for n, p in zip(counts, parts)]
    scratch += [pltpu.VMEM((3,) + (p if i < 5 else (16, 128)), bf16) for i, p in enumerate(parts)]
    slots = 10 + 26 * 4 + RS_ITEMS * 4
    return pl.pallas_call(
        reduce_kernel,
        in_specs=[pl.BlockSpec(memory_space=HBM)] * 7,
        out_specs=[pl.BlockSpec(memory_space=HBM)] * 6 + [pl.BlockSpec(memory_space=pltpu.VMEM)],
        out_shape=[
            shape((q.shape[0] * 2, q.shape[1] // 4), bf16),
            shape((kr.shape[0] * 2, kr.shape[1] // 4), bf16),
            shape((kvb.shape[0] // 4, kvb.shape[1] * 2), bf16),
            shape((out.shape[0] // 4, out.shape[1] * 2), bf16),
            shape((3, sh.shape[1] // 4, sh.shape[2] * 2), bf16),
            shape((6, ex.shape[1], ex.shape[2] * 2), bf16),
            shape(gain.shape[1:], f32),
        ],
        scratch_shapes=scratch
        + [
            pltpu.VMEM((4,) + gain.shape[1:], f32),
            pltpu.VMEM((7,) + gain.shape[1:], f32),
            pltpu.VMEM(gain.shape[1:], f32),
            pltpu.SemaphoreType.DMA((slots,)),
            pltpu.SemaphoreType.DMA((slots,)),
            pltpu.SemaphoreType.DMA((52,)),
            pltpu.SemaphoreType.DMA((RS_ITEMS + 1,)),
        ],
        compiler_params=pltpu.CompilerParams(
            collective_id=1, has_side_effects=True, vmem_limit_bytes=56 << 20
        ),
        name="reduce_grads",
    )(q, kr, kvb, out, sh, ex, gain)


def head_split(weight):
    per_head = weight.reshape(HEADS, NOPE + ROPE, weight.shape[1])
    cuts = (0, NOPE, NOPE + HALF_ROPE, NOPE + ROPE)
    return jnp.concatenate(
        [per_head[:, a:b].reshape(-1, weight.shape[1]) for a, b in zip(cuts[:-1], cuts[1:])]
    )


def head_join(weight):
    cols = weight.shape[1]
    nope = weight[: HEADS * NOPE].reshape(HEADS, NOPE, cols)
    first = weight[HEADS * NOPE : HEADS * (NOPE + HALF_ROPE)].reshape(HEADS, HALF_ROPE, cols)
    second = weight[HEADS * (NOPE + HALF_ROPE) :].reshape(HEADS, HALF_ROPE, cols)
    return jnp.concatenate([nope, first, second], axis=1).reshape(-1, cols)


def halves(tensor, axis):
    size = tensor.shape[axis] // 2
    return jnp.stack(
        [
            lax.slice_in_dim(tensor, 0, size, axis=axis),
            lax.slice_in_dim(tensor, size, 2 * size, axis=axis),
        ]
    )


def shards(
    tokens,
    attn_gain,
    q_weight,
    kva_weight,
    kv_gain,
    kvb_weight,
    out_weight,
    ffn_gain,
    router_weight,
    shared_gate,
    shared_up,
    shared_down,
    expert_gate,
    expert_up,
    expert_down,
    expert_ids,
    cotangent,
):
    shard_count = lax.axis_size("shard")
    shard_index = lax.axis_index("shard")
    core = lax.axis_index("rep") % 2
    fast = lax.axis_size("rep") == 8 and shard_count == 4
    micros, rows, width = tokens.shape
    toks = micros * rows
    scale = (NOPE + ROPE) ** (-0.5)
    ga, gk = attn_gain.shape[0], kv_gain.shape[0]

    gain_pack = jnp.concatenate([attn_gain, ffn_gain, kv_gain]).astype(bf16)
    gain_pack = jnp.broadcast_to(gain_pack[None], (16, gain_pack.shape[0]))
    query_mat, kr_mat, kvb_mat, out_mat, sh_mat, gains = gather_weights(
        head_split(q_weight).astype(bf16),
        jnp.concatenate([kva_weight, router_weight]).astype(bf16),
        kvb_weight.astype(bf16),
        out_weight.astype(bf16),
        jnp.stack([shared_gate, shared_up, shared_down]).astype(bf16),
        gain_pack,
        fast,
    )
    gain_rows = gains[:, 0].astype(f32)
    attn_gain_f = gain_rows[:, :ga].reshape(-1)
    ffn_gain_f = gain_rows[:, ga : 2 * ga].reshape(-1)
    kv_gain_f = gain_rows[:, 2 * ga :].reshape(-1)
    kv_down_mat, router_mat = kr_mat[: RANK + ROPE], kr_mat[RANK + ROPE :]
    gate_mat, up_mat, down_mat = sh_mat[0], sh_mat[1], sh_mat[2]

    x_in = tokens.reshape(toks, width).astype(f32)
    inv_one = rms_scale(x_in)
    h_attn = (x_in * inv_one * attn_gain_f).astype(bf16)
    positions = (shard_index * rows + jnp.arange(rows, dtype=jnp.int32)).astype(f32)
    frequency = jnp.exp(
        -jnp.log(rope_base) * (2.0 * jnp.arange(HALF_ROPE, dtype=f32) / ROPE)
    )
    angles = positions[:, None] * frequency[None, :]
    cosine = jnp.tile(jnp.cos(angles), (micros, 1))
    sine = jnp.tile(jnp.sin(angles), (micros, 1))
    cos_all, sin_all = jnp.tile(cosine, (1, HEADS)), jnp.tile(sine, (1, HEADS))
    q_raw = dot(h_attn, query_mat, 1, 1)
    n1, n2 = HEADS * NOPE, HEADS * (NOPE + HALF_ROPE)
    q_first, q_second = q_raw[:, n1:n2], q_raw[:, n2:]
    by_micro = lambda t: t.reshape(micros, rows, t.shape[-1])
    qn = by_micro(q_raw[:, :n1].astype(bf16))
    q1 = by_micro((q_first * cos_all - q_second * sin_all).astype(bf16))
    q2 = by_micro((q_second * cos_all + q_first * sin_all).astype(bf16))
    kv_down = dot(h_attn, kv_down_mat, 1, 1)
    latent = kv_down[:, :RANK]
    inv_kv = rms_scale(latent)
    latent_norm = (latent * inv_kv * kv_gain_f).astype(bf16)
    k_first, k_second = kv_down[:, RANK : RANK + HALF_ROPE], kv_down[:, RANK + HALF_ROPE :]
    latent_pack = jnp.concatenate(
        [
            latent_norm,
            (k_first * cosine - k_second * sine).astype(bf16),
            (k_second * cosine + k_first * sine).astype(bf16),
            jnp.zeros((toks, ROPE), bf16),
        ],
        axis=-1,
    )
    (packs,) = z_gather([by_micro(latent_pack)], fast, 2)
    length = packs.shape[1]
    lat_all = packs[..., :RANK]
    k1 = jnp.tile(packs[..., RANK : RANK + HALF_ROPE], (1, 1, HEAD_GROUP))
    k2 = jnp.tile(packs[..., RANK + HALF_ROPE : RANK + ROPE], (1, 1, HEAD_GROUP))
    limit = ((shard_index * rows) // MASK_BLOCK + 1) * MASK_BLOCK
    limit = jnp.minimum(limit, length).astype(jnp.int32).reshape(1)
    attended = attend(limit, qn, q1, q2, lat_all, k1, k2, kvb_mat, scale).reshape(toks, -1)

    x_mid = x_in + dot(attended, out_mat, 1, 0)
    inv_two = rms_scale(x_mid)
    h_ffn = (x_mid * inv_two * ffn_gain_f).astype(bf16)
    router_probs = jax.nn.softmax(dot(h_ffn, router_mat, 1, 1), axis=-1)
    grad_b = cotangent.reshape(toks, width)

    member = jnp.any(
        expert_ids[:, :, None, :] == jnp.arange(EXP_WIN, dtype=jnp.int32)[None, None, :, None], axis=-1
    ).astype(jnp.int32)
    placed = jnp.cumsum(member, axis=1) - 1
    hits = (member[:, :, :, None] == 1) & (
        placed[:, :, :, None] == jnp.arange(CAP, dtype=jnp.int32)
    )
    select = jnp.transpose(hits, (2, 0, 3, 1)).astype(f32)
    select_b = select.astype(bf16)
    h3, c3 = by_micro(h_ffn), by_micro(grad_b)
    gather_slots = lambda t: jnp.einsum(
        "emct,mtd->emcd", select_b, t, preferred_element_type=f32
    )
    slot_rows = gather_slots(h3).astype(bf16)
    picked = gather_slots(c3)
    slot_gates = jnp.einsum(
        "emct,mte->emc", select, by_micro(router_probs)[..., :EXP_WIN], precision=highest
    )
    slot_dy = (slot_gates[..., None] * picked).astype(bf16)
    flat = lambda t: t.reshape(EXP_WIN, micros * CAP, width)
    rows_all, dy_all = z_gather([flat(slot_rows), flat(slot_dy)], fast, 3)
    eg, eu, ed = expert_gate.astype(bf16), expert_up.astype(bf16), expert_down.astype(bf16)
    bdot = lambda a, b, ca, cb: lax.dot_general(
        a, b, (((ca,), (cb,)), ((0,), (0,))), preferred_element_type=f32
    )
    expert_pre = bdot(rows_all, eg, 2, 2)
    expert_upv = bdot(rows_all, eu, 2, 2)
    expert_hidden = (jax.nn.silu(expert_pre) * expert_upv).astype(bf16)
    expert_part = bdot(expert_hidden, ed, 2, 1).astype(bf16)
    expert_hidden_grad = bdot(dy_all, ed, 2, 2)
    expert_gate_b, expert_up_b = swiglu_back(expert_pre, expert_upv, expert_hidden_grad)
    slot_part = (bdot(expert_gate_b, eg, 2, 1) + bdot(expert_up_b, eu, 2, 1)).astype(bf16)
    expert_out, slot_grad = z_scatter([expert_part, slot_part], fast, 4)
    back = lambda t: t.reshape(EXP_WIN, micros, CAP, width)
    expert_out, slot_grad = back(expert_out), back(slot_grad)

    gate_pre = dot(h_ffn, gate_mat, 1, 1)
    up_pre = dot(h_ffn, up_mat, 1, 1)
    shared_hidden = (jax.nn.silu(gate_pre) * up_pre).astype(bf16)
    shared_out = dot(shared_hidden, down_mat, 1, 0)
    routed = jnp.einsum("emct,emcd->mtd", select, slot_gates[..., None] * expert_out, precision=highest)
    layer_output = (x_mid + shared_out + routed.reshape(toks, width)).astype(bf16)

    shared_hidden_grad = dot(grad_b, down_mat, 1, 1)
    gate_grad_b, up_grad_b = swiglu_back(gate_pre, up_pre, shared_hidden_grad)
    ffn_grad = dot(gate_grad_b, gate_mat, 1, 0) + dot(up_grad_b, up_mat, 1, 0)
    gate_weight_grad = jnp.sum(picked * expert_out, axis=-1)
    ffn_grad = ffn_grad + jnp.einsum(
        "emct,emcd->mtd", select, slot_grad, precision=highest
    ).reshape(toks, width)
    probs_grad = jnp.einsum("emct,emc->mte", select, gate_weight_grad, precision=highest)
    probs_grad = jnp.pad(
        probs_grad.reshape(toks, EXP_WIN), ((0, 0), (0, EXPERTS - EXP_WIN))
    )
    logit_grad = (
        router_probs * (probs_grad - jnp.sum(router_probs * probs_grad, axis=-1, keepdims=True))
    ).astype(bf16)
    ffn_grad = ffn_grad + dot(logit_grad, router_mat, 1, 0)
    mid_part, ffn_gain_grad = norm_back(x_mid, inv_two, ffn_gain_f, ffn_grad)
    mid_grad = grad_b.astype(f32) + mid_part
    attn_out_grad = mid_grad.astype(bf16)
    attended_grad = by_micro(dot(attn_out_grad, out_mat, 1, 1).astype(bf16))

    dqn, dq1, dq2, dlat, dk1, dk2, dkvb = attend_back(
        limit, qn, q1, q2, lat_all, k1, k2, kvb_mat, attended_grad, scale
    )
    fold = lambda t: jnp.sum(t.reshape(micros, length, HEAD_GROUP, HALF_ROPE), axis=2)
    back_pack = jnp.concatenate(
        [dlat, fold(dk1), fold(dk2), jnp.zeros((micros, length, ROPE), f32)], axis=-1
    ).astype(bf16)
    (own_back,) = z_scatter([back_pack], fast, 5)
    own_back = own_back.reshape(toks, -1)
    latent_grad, kv_gain_grad = norm_back(latent, inv_kv, kv_gain_f, own_back[:, :RANK])
    g1, g2 = own_back[:, RANK : RANK + HALF_ROPE], own_back[:, RANK + HALF_ROPE : RANK + ROPE]
    kv_down_grad = jnp.concatenate(
        [latent_grad, g1 * cosine + g2 * sine, g2 * cosine - g1 * sine], axis=-1
    ).astype(bf16)
    dq1, dq2 = dq1.reshape(toks, -1), dq2.reshape(toks, -1)
    q_raw_grad = jnp.concatenate(
        [
            dqn.reshape(toks, -1),
            (dq1 * cos_all + dq2 * sin_all).astype(bf16),
            (dq2 * cos_all - dq1 * sin_all).astype(bf16),
        ],
        axis=-1,
    )
    attn_in_grad = dot(q_raw_grad, query_mat, 1, 0) + dot(kv_down_grad, kv_down_mat, 1, 0)
    x_part, attn_gain_grad = norm_back(x_in, inv_one, attn_gain_f, attn_in_grad)
    input_grad = (mid_grad + x_part).astype(bf16)

    both = lambda t: jnp.broadcast_to(t[None], (2,) + t.shape)
    kr_grad = jnp.concatenate(
        [dot(kv_down_grad, h_attn, 0, 0), dot(logit_grad, h_ffn, 0, 0)]
    ).astype(bf16)
    swapped = core_swap(
        [
            both(h_attn),
            halves(q_raw_grad, 1),
            halves(kr_grad, 0),
            halves(dkvb, 1),
            both(attended),
            halves(attn_out_grad, 1),
            both(jnp.concatenate([gate_grad_b, up_grad_b, shared_hidden], axis=1)),
            halves(h_ffn, 1),
            halves(grad_b, 1),
            both(jnp.concatenate([expert_gate_b, expert_up_b, expert_hidden], axis=-1).reshape(
                EXP_WIN * rows_all.shape[1], -1
            )),
            halves(rows_all.reshape(-1, width), 1),
            halves(dy_all.reshape(-1, width), 1),
        ],
        fast,
        6,
    )
    (h_s, qg_s, krg_s, kvbg_s, att_s, og_s, sh_s, hf_s, cot_s, ex_s, row_s, dy_s) = swapped
    tall = lambda t: t.reshape(-1, t.shape[-1])
    grad_q = dot(tall(qg_s), tall(h_s), 0, 0).astype(bf16)
    grad_kr = (krg_s[0].astype(f32) + krg_s[1].astype(f32)).astype(bf16)
    grad_kvb = (kvbg_s[0].astype(f32) + kvbg_s[1].astype(f32)).astype(bf16)
    grad_out = dot(tall(att_s), tall(og_s), 0, 0).astype(bf16)
    ff = shared_hidden.shape[1]
    sh_s = tall(sh_s)
    hf_s, cot_s = tall(hf_s), tall(cot_s)
    grad_sh = jnp.stack(
        [
            dot(sh_s[:, :ff], hf_s, 0, 0).astype(bf16),
            dot(sh_s[:, ff : 2 * ff], hf_s, 0, 0).astype(bf16),
            dot(sh_s[:, 2 * ff :], cot_s, 0, 0).astype(bf16),
        ]
    )
    fe = expert_hidden.shape[-1]
    by_expert = lambda t: t.reshape(2, EXP_WIN, -1, t.shape[-1])
    ex_s, row_s, dy_s = by_expert(ex_s), by_expert(row_s), by_expert(dy_s)
    edot = lambda a, b: jnp.einsum("senf,send->efd", a, b, preferred_element_type=f32).astype(bf16)
    grad_ex = jnp.concatenate(
        [
            edot(ex_s[..., :fe], row_s),
            edot(ex_s[..., fe : 2 * fe], row_s),
            edot(ex_s[..., 2 * fe :], dy_s),
        ]
    )
    lane_rows = lambda t: t.reshape(shard_count, -1)
    gain_grad = jnp.concatenate(
        [lane_rows(attn_gain_grad), lane_rows(ffn_gain_grad), lane_rows(kv_gain_grad)], axis=1
    )
    gain_len = gain_grad.shape[1]
    gain_grad = jnp.pad(gain_grad, ((0, 0), (0, 16 * 128 - gain_len))).reshape(-1, 16, 128)
    gq, gkr, gkvb, gout, gsh, gex, gg = reduce_grads(
        (grad_q, grad_kr, grad_kvb, grad_out, grad_sh, grad_ex), gain_grad, fast
    )
    gg = gg.reshape(-1)[:gain_len]
    gkr = gkr.astype(f32)
    gsh = gsh.astype(f32)
    gex = gex.astype(f32)
    return (
        by_micro(layer_output),
        by_micro(input_grad),
        gg[:ga],
        head_join(gq).astype(f32),
        gkr[: RANK + ROPE],
        gg[2 * ga :],
        gkvb.astype(f32),
        gout.astype(f32),
        gg[ga : 2 * ga],
        gkr[RANK + ROPE :],
        gsh[0],
        gsh[1],
        gsh[2],
        gex[:2],
        gex[2:4],
        gex[4:],
    )


def solution(mesh):
    token_spec = P(None, ("rep", "shard"), None)
    row_spec, col_spec, gain_spec = P("shard", None), P(None, "shard"), P("shard")
    expert_spec = P(None, "shard", None)
    weight_specs = (
        gain_spec,
        col_spec,
        col_spec,
        gain_spec,
        row_spec,
        row_spec,
        gain_spec,
        col_spec,
        row_spec,
        row_spec,
        row_spec,
        expert_spec,
        expert_spec,
        expert_spec,
    )
    return jax.shard_map(
        shards,
        mesh=mesh,
        in_specs=(token_spec,) + weight_specs + (token_spec, token_spec),
        out_specs=(token_spec, token_spec) + weight_specs,
        check_vma=False,
    )
```

time: 3810 us -> 1510 us (0.40)
  waiting for transfers between devices: 1790 us -> 0 us
  blocking collectives: 1570 us -> 0 us
  Pallas kernels: 0 us -> 1260 us
  matrix products: 194 us -> 108 us
  local copies, waits for them, and re-layouts: 149 us -> 68.3 us
    unnamed x3 -> x0, blocking collectives: 1500 us -> none
    pallas_call x0 -> x9, Pallas kernels: none -> 1260 us  [the longest x1 356 us: core_swap(): pl.pallas_call(functools.partial(swap_kernel, count), in_specs=[pl.BlockS...]
    all_gather x17 -> x0, waiting for transfers between devices: 976 us -> none  [the longest x1 205 us: shards(): lax.all_gather(q_weight.astype(jnp.bfloat16), 'shard', axis=1, tiled=True)]
    reduce_scatter x10 -> x0, waiting for transfers between devices: 341 us -> none  [the longest x2 280 us: shards(): lax.psum_scatter(key_grad_rows, 'shard', scatter_dimension=0, tiled=True)]
    unnamed x39 -> x0, waiting for transfers between devices: 249 us -> none
    psum x1 -> x0, waiting for transfers between devices: 221 us -> none  [shards(): lax.psum((expert_gate_grad, expert_up_grad, expert_down_grad), 'rep')]
    dot_general x56 -> x36, matrix products: 191 us -> 108 us  [the longest x21 84.1 us: dot(): lax.dot_general(a, b, (((ca,), (cb,)), ((), ())), preferred_element_type=...]
    unnamed x272 -> x262, local copies, waits for them, and re-layouts: 96.8 us -> 19.6 us
  transfers between devices with their start and end apart: 38 -> 0, of which waited for: 23 -> 0; matrix products, arithmetic and copies ran while one was open for 46% -> 0% of each run, Pallas kernels for 0% -> 0%
where the time goes in v1:
time: 1510 us
  Pallas kernels  1260 us (83%)
  matrix products  108 us (7%)
  local copies, waits for them, and re-layouts  68.3 us (5%)
  other arithmetic  64.4 us (4%)
    pallas_call x1, Pallas kernels, core_swap(): pl.pallas_call(functools.partial(swap_kernel, count), in_specs=[pl.BlockS...  356 us
    pallas_call x1, Pallas kernels, gather_weights(): pl.pallas_call(gather_kernel, in_specs=[pl.BlockSpec(memory_space=HBM)] *...  348 us
    pallas_call x1, Pallas kernels, reduce_grads(): pl.pallas_call(reduce_kernel, in_specs=[pl.BlockSpec(memory_space=HBM)] *...  340 us
    dot_general x21, matrix products, dot(): lax.dot_general(a, b, (((ca,), (cb,)), ((), ())), preferred_element_type=...  84.1 us
    pallas_call x2, Pallas kernels, z_gather(): pl.pallas_call(functools.partial(z_gather_kernel, count), in_specs=[pl.Bl...  78.3 us
    pallas_call x2, Pallas kernels, z_scatter(): pl.pallas_call(functools.partial(z_scatter_kernel, count), in_specs=[pl.B...  77.3 us
    pallas_call x1, Pallas kernels, attend_back(): pl.pallas_call(functools.partial(attend_back_kernel, scale), grid=grid, i...  43.9 us

profile of v1, /device:TPU:9, one launch (start us, length us, event | category | flops | bytes accessed | tf_op | source)
XLA Modules:
  0.0 1508.4 jit_solution(4794414249479935664)
XLA Ops:
  0.7 3.2 convert.88
  4.1 1.8 pad_maximum_fusion.4.refs_0_
  9.2 1.6 convert_element_type.242.refs_3_
  14.6 2.3 pad_maximum_fusion.1.refs_4_
  17.6 348.0 %gather_weights.1 = (bf16[3072,2048]{1,0:T(8,128)(2,1)}, bf16[640,2048]{1,0:T(8,128)(2,1)}, bf16[512,4096]{1,0:T(8,128)(2,1)}, bf16[2048,2048]{1,0:T(8,128)(2,1)...) custom-call(bf16[3072,512]{1,0:T(8,128)(2,1)} %pad_maximum_fusion.4.refs_0_, ...), custom_call_target="tpu_custom_call" | custom-call | tf_op jit(solution)/shard_map/gather_weights/pallas_call | solution.py:451
  367.3 6.8 fusion.129
  378.3 2.4 add_convert_fusion.2
  384.0 31.1 %z_gather.2 = bf16[2,512,640]{2,1,0:T(8,128)(2,1)} custom-call(bf16[2,128,640]{2,1,0:T(8,128)(2,1)} %bitcast.369), custom_call_target="tpu_custom_call" | custom-call | tf_op jit(solution)/shard_map/z_gather/pallas_call | solution.py:501
  416.5 1.6 fusion.125
  422.9 21.0 %attend.1 = bf16[2,128,2048]{2,1,0:T(8,128)(2,1)S(1)} custom-call(s32[1]{0:T(128)} %bitcast.1.lim_ref, bf16[2,128,2048]{2,1,0:T(8,128)(2,1)S(1)} %bitcast.321, bf16[2,128,512]{2,1,0:T(8,128)(2,1)S(1)} %bitcast.329, bf16[2,128,512]{2,1,0:T(8,128)(2,1)S(1)} %bitcast.327, bf16[2,512,512]{2,1,0:T(8,128)(2,1)S(1)} %slice.227.lat_ref, ...), custom_call_target="tpu_custom_call" | custom-call | tf_op jit(solution)/shard_map/attend/pallas_call | solution.py:184
  444.0 5.9 multiply_reduce_fusion.2
  461.7 2.3 multiply_convert_fusion.4
  464.7 47.2 %z_gather.3 = (bf16[2,128,2048]{2,1,0:T(8,128)(2,1)}, bf16[2,128,2048]{2,1,0:T(8,128)(2,1)}) custom-call(bf16[2,32,2048]{2,1,0:T(8,128)(2,1)} %bitcast.375, bf16[2,32,2048]{2,1,0:T(8,128)(2,1)} %bitcast.376), custom_call_target="tpu_custom_call" | custom-call | tf_op jit(solution)/shard_map/z_gather/pallas_call | solution.py:501
  512.0 4.0 fusion.72
  516.0 3.7 fusion.68
  519.7 3.7 multiply_convert_fusion.6
  523.5 1.7 convolution_convert_fusion.4.refs_0_
  527.0 1.7 fusion.39.refs_1_
  528.7 47.1 %z_scatter.2 = (bf16[4,2,32,2048]{3,2,1,0:T(8,128)(2,1)}, bf16[4,2,32,2048]{3,2,1,0:T(8,128)(2,1)}) custom-call(bf16[2,128,2048]{2,1,0:T(8,128)(2,1)} %convolution_convert_fusion.4.refs_0_, bf16[2,128,2048]{2,1,0:T(8,128)(2,1)} %fusion.39.refs_1_), custom_call_target="tpu_custom_call" | custom-call | tf_op jit(solution)/shard_map/z_scatter/pallas_call | solution.py:551
  575.8 1.5 convert_reduce_fusion.2
  577.4 1.7 fusion.87
  579.2 4.6 fusion.21
  583.8 15.6 %fusion.6 = f32[256,1408]{1,0:T(8,128)S(1)} fusion(bf16[256,2048]{1,0:T(8,128)(2,1)S(1)} %multiply_convert_fusion, bf16[3,1408,2048]{2,1,0:T(8,128)(2,1)} %get-tuple-element.57), kind=kOutput, calls=%fused_computation.9 | convolution fusion | flops 1476395008 | bytes 8257536 | tf_op jit(solution)/shard_map/dot_general | solution.py:34
  599.4 5.2 multiply_convert_fusion.2
  604.8 2.8 fusion.36
  608.8 1.8 fusion.4
  610.7 1.9 fusion.33
  613.0 2.0 multiply_reduce_fusion
  615.0 2.1 fusion.121
  617.1 3.4 convolution_convert_fusion.5
  620.5 43.9 %attend_back.1 = (bf16[2,128,2048]{2,1,0:T(8,128)(2,1)S(1)}, f32[2,128,512]{2,1,0:T(8,128)S(1)}, f32[2,128,512]{2,1,0:T(8,128)S(1)}, f32[2,512,512]{2,1,0:T(8,12...) custom-call(s32[1]{0:T(128)} %bitcast.1.lim_ref, ...), custom_call_target="tpu_custom_call" | custom-call | tf_op jit(solution)/shard_map/attend_back/pallas_call | solution.py:200
  664.8 9.5 fusion.55
  677.9 1.8 convert.80
  679.7 1.4 maximum_maximum_fusion.refs_0_
  681.1 30.2 %z_scatter.3 = bf16[4,2,128,640]{3,2,1,0:T(8,128)(2,1)} custom-call(bf16[2,512,640]{2,1,0:T(8,128)(2,1)} %maximum_maximum_fusion.refs_0_), custom_call_target="tpu_custom_call" | custom-call | tf_op jit(solution)/shard_map/z_scatter/pallas_call | solution.py:551
  711.3 1.6 convert_reduce_fusion
  713.9 2.0 slice.295
  715.8 2.0 copy.222
  717.9 1.6 multiply_reduce_fusion.3
  720.9 3.3 fusion.51
  724.2 1.6 fusion.48
  725.9 1.6 broadcast_in_dim.19.refs_0_
  730.7 1.7 pad_maximum_fusion.6.refs_2_
  732.4 1.4 copy-done.32
  734.2 2.4 pad_maximum_fusion.3.refs_3_
  736.5 1.6 broadcast_in_dim.20.refs_4_
  740.2 2.3 broadcast_in_dim.21.refs_6_
  749.4 356.3 %core_swap.1 = (bf16[2,256,2048]{2,1,0:T(8,128)(2,1)}, bf16[2,256,1536]{2,1,0:T(8,128)(2,1)}, bf16[2,320,2048]{2,1,0:T(8,128)(2,1)}, bf16[2,512,2048]{2,1,0:T(8,...) custom-call(bf16[2,256,2048]{2,1,0:T(8,128)(2,1)} %broadcast_in_dim., ...), custom_call_target="tpu_custom_call" | custom-call | tf_op jit(solution)/shard_map/core_swap/pallas_call | solution.py:603
  1105.7 8.6 bitcast_convert_fusion.refs_0_
  1114.3 1.5 fusion.75.refs_1_
  1115.8 2.1 fusion.41.refs_2_
  1118.0 4.4 bitcast_convert_fusion.1.refs_3_
  1122.4 1.7 fusion.20
  1124.1 1.7 fusion.19
  1125.8 1.7 fusion.18
  1127.5 4.1 pad_maximum_fusion.refs_4_
  1134.7 2.3 pad_maximum_fusion.2.refs_5_
  1137.6 339.5 %reduce_grads.1 = (bf16[3072,512]{1,0:T(8,128)(2,1)}, bf16[640,512]{1,0:T(8,128)(2,1)}, bf16[128,4096]{1,0:T(8,128)(2,1)}, bf16[512,2048]{1,0:T(8,128)(2,1)}, bf...) custom-call(bf16[1536,2048]{1,0:T(8,128)(2,1)} %bitcast_convert_fusion.refs_0_, ...), custom_call_target="tpu_custom_call" | custom-call | tf_op jit(solution)/shard_map/reduce_grads/pallas_call | solution.py:853
  1479.8 1.7 slice.267
  1481.8 3.8 bitcast_convert_fusion.2
  1488.2 1.5 convert_element_type.300
  1489.7 2.5 convert_element_type.301
  1494.0 3.7 slice_bitcast_fusion
  1497.7 10.5 fusion.122
  (384 shorter events, 68.2 us)
Async XLA Ops:
  6.1 3.0 copy-start.30
  9.2 3.4 copy-start.38
  17.6 349.0 %copy-start.15 = (bf16[2,128,2048]{2,1,0:T(8,128)(2,1)S(1)}, bf16[2,128,2048]{2,1,0:T(8,128)(2,1)}, u32[]{:S(2)}) copy-start(bf16[2,128,2048]{2,1,0:T(8,128)(2,1)} %param.17) | copy-start | bytes 3145732
  366.9 7.2 copy-start.95
  366.9 7.2 copy-start.93
  367.3 13.4 copy-start.18
  374.5 7.0 copy-start.68
  376.0 5.5 copy-start.24
  376.1 5.4 copy-start.70
  378.3 3.3 copy-start.26
  381.6 34.9 %copy-start.77 = (f32[512]{0:T(512)}, f32[512]{0:T(512)S(1)}, u32[]{:S(2)}) copy-start(f32[512]{0:T(512)S(1)} %slice_bitcast_fusion.19) | copy-start | bytes 6148
  383.0 33.5 %copy-start.80 = (bf16[640]{0:T(1024)(128)(2,1)}, bf16[640]{0:T(1024)(128)(2,1)S(1)}, u32[]{:S(2)}) copy-start(bf16[640]{0:T(1024)(128)(2,1)S(1)} %pad.59.clone) | copy-start | bytes 3844
  416.5 27.4 %copy-start = (bf16[2,512,512]{2,1,0:T(8,128)(2,1)}, bf16[2,512,512]{2,1,0:T(8,128)(2,1)S(1)}, u32[]{:S(2)}) copy-start(bf16[2,512,512]{2,1,0:T(8,128)(2,1)S(1)} %slice.227.lat_ref) | copy-start | bytes 3145732
  422.9 21.0 %copy-start.16 = (bf16[2,128,2048]{2,1,0:T(8,128)(2,1)S(1)}, bf16[2,128,2048]{2,1,0:T(8,128)(2,1)}, u32[]{:S(2)}) copy-start(bf16[2,128,2048]{2,1,0:T(8,128)(2,1)} %param.17) | copy-start | bytes 3145732
  451.4 148.0 %copy-start.9 = (bf16[256,2048]{1,0:T(8,128)(2,1)}, bf16[256,2048]{1,0:T(8,128)(2,1)S(1)}, u32[]{:S(2)}) copy-start(bf16[256,2048]{1,0:T(8,128)(2,1)S(1)} %multiply_convert_fusion) | copy-start | bytes 3145732
  461.7 3.1 copy-start.82
  511.9 4.0 copy-start.13
  511.9 11.6 slice-start.4
  516.0 3.7 copy-start.28
  516.0 7.5 slice-start.5
  516.0 9.3 slice-start
  519.7 5.6 slice-start.1
  575.8 3.3 copy-start.20
  579.1 25.6 %slice-start.8 = ((s8[17301504]{0:T(1024)(128)(4,1)}), s8[4194304]{0:T(1024)(128)(4,1)S(1)}, s32[]{:S(2)}) async-start(s8[17301504]{0:T(1024)(128)(4,1)} %bitcast.367), calls=%async_computation.8 | async-start | bytes 8388608
  579.1 25.6 %slice-start.9 = ((s8[17301504]{0:T(1024)(128)(4,1)}), s8[4194304]{0:T(1024)(128)(4,1)S(1)}, s32[]{:S(2)}) async-start(s8[17301504]{0:T(1024)(128)(4,1)} %bitcast.367), calls=%async_computation.9 | async-start | bytes 8388608
  583.8 20.9 %slice-start.10 = ((s8[17301504]{0:T(1024)(128)(4,1)}), s8[4194304]{0:T(1024)(128)(4,1)S(1)}, s32[]{:S(2)}) async-start(s8[17301504]{0:T(1024)(128)(4,1)} %bitcast.367), calls=%async_computation.10 | async-start | bytes 8388608
  599.4 5.3 copy-start.12
  599.4 5.3 slice-start.11
  599.4 5.3 slice-start.12
  604.7 4.1 copy-start.64
  604.7 5.9 copy-start.40
  610.7 6.4 slice-start.13
  613.0 4.1 slice-start.14
  617.1 3.4 copy-start.34
  617.1 3.4 copy-start.2
  617.1 3.4 copy-start.4
  617.1 3.4 copy-start.6
  620.5 43.9 %copy-start.25 = (f32[256,512]{1,0:T(8,128)S(1)}, f32[256,512]{1,0:T(8,128)}, u32[]{:S(2)}) copy-start(f32[256,512]{1,0:T(8,128)} %copy-done.24) | copy-start | bytes 1572868
  620.5 43.9 %copy-start.27 = (f32[256,512]{1,0:T(8,128)S(1)}, f32[256,512]{1,0:T(8,128)}, u32[]{:S(2)}) copy-start(f32[256,512]{1,0:T(8,128)} %copy-done.26) | copy-start | bytes 1572868
  664.4 9.9 copy-start.7
  664.4 9.9 copy-start.8
  664.8 9.5 copy-start.60
  664.8 9.5 copy-start.62
  675.8 3.9 copy-start.81
  681.1 32.7 %copy-start.69 = (f32[2,128,32]{1,0,2:T(2,128)S(1)}, f32[2,128,32]{1,0,2:T(2,128)}, u32[]{:S(2)}) copy-start(f32[2,128,32]{1,0,2:T(2,128)} %copy-done.68) | copy-start | bytes 98308
  681.1 32.7 %copy-start.71 = (f32[2,128,32]{1,0,2:T(2,128)S(1)}, f32[2,128,32]{1,0,2:T(2,128)}, u32[]{:S(2)}) copy-start(f32[2,128,32]{1,0,2:T(2,128)} %copy-done.70) | copy-start | bytes 98308
  711.3 6.5 copy-start.78
  711.3 6.5 copy-start.88
  712.9 6.6 copy-start.99
  713.8 7.0 copy-start.17
  713.8 7.0 copy-start.94
  720.9 3.3 copy-start.96
  720.9 3.3 copy-start.22
  730.7 3.1 copy-start.32
  1105.7 8.6 copy-start.43
  1105.7 10.1 copy-start.31
  1115.8 6.6 slice-start.15
  1118.0 4.4 slice-start.16
  1118.0 4.4 copy-start.104
  1127.5 4.2 copy-start.55
  1481.8 3.8 copy-start.42
  1481.8 11.1 slice-start.6
  1485.6 4.1 copy-start.44
  1485.6 7.3 slice-start.7
  (61 other events, 107.8 us)

commit v2 on v1

v2 whole, which is shorter than its diff:
```python
import functools

import jax
import jax.numpy as jnp
from jax import lax
from jax.experimental import pallas as pl
from jax.experimental.pallas import tpu as pltpu
from jax.sharding import PartitionSpec as P

HEADS = 16
NOPE = 128
ROPE = 64
VDIM = 128
RANK = 512
EXPERTS = 64
EXP_WIN = 2
MASK_BLOCK = 256
CAP = 16

epsilon = 1e-06
rope_base = 10000.0
masked_score = -1e30
highest = lax.Precision.HIGHEST
bf16 = jnp.bfloat16
f32 = jnp.float32
MESH = pl.DeviceIdType.MESH
HBM = pltpu.HBM
HALF_ROPE = ROPE // 2
HEAD_GROUP = 4
GROUP_LANES = HEAD_GROUP * HALF_ROPE


def dot(a, b, ca, cb):
    return lax.dot_general(a, b, (((ca,), (cb,)), ((), ())), preferred_element_type=f32)


def rms_scale(tensor):
    return lax.rsqrt(jnp.mean(tensor * tensor, axis=-1, keepdims=True) + epsilon)


def norm_back(tensor, inv_rms, gain_vec, gradient):
    scaled_grad = gradient * gain_vec
    inner_mean = jnp.mean(scaled_grad * tensor, axis=-1, keepdims=True)
    input_part = inv_rms * scaled_grad - tensor * (inv_rms * inv_rms * inv_rms) * inner_mean
    gain_part = jnp.sum(gradient * tensor * inv_rms, axis=0)
    return (input_part, gain_part)


def swiglu_back(gate_pre, up_pre, hidden_grad):
    sigmoid_gate = jax.nn.sigmoid(gate_pre)
    silu_gate = gate_pre * sigmoid_gate
    slope = sigmoid_gate * (1.0 + gate_pre * (1.0 - sigmoid_gate))
    return (
        (hidden_grad * up_pre * slope).astype(bf16),
        (hidden_grad * silu_gate).astype(bf16),
    )


def head_scores(qn, q1, q2, kv, k1, k2, seen, scale, head):
    lane = lax.broadcasted_iota(jnp.int32, (1, GROUP_LANES), 1)
    mine = (lane >= head * HALF_ROPE) & (lane < (head + 1) * HALF_ROPE)
    width = NOPE + VDIM
    q_head = qn[:, head * NOPE : (head + 1) * NOPE]
    k_head = kv[:, head * width : head * width + NOPE]
    v_head = kv[:, head * width + NOPE : (head + 1) * width]
    q1m = jnp.where(mine, q1, jnp.zeros_like(q1))
    q2m = jnp.where(mine, q2, jnp.zeros_like(q2))
    scores = dot(q_head, k_head, 1, 1) + dot(q1m, k1, 1, 1) + dot(q2m, k2, 1, 1)
    scores = jnp.where(seen > 0.0, scores * scale, masked_score)
    top = jnp.max(scores, axis=-1, keepdims=True)
    expo = jnp.exp(scores - top)
    probs = expo / jnp.sum(expo, axis=-1, keepdims=True)
    return probs, q_head, k_head, v_head, q1m, q2m, mine


def attend_kernel(scale, seen_ref, qn_ref, q1_ref, q2_ref, lat_ref, k1_ref, k2_ref, kvb_ref, out_ref):
    kv = dot(lat_ref[0], kvb_ref[...], 1, 0).astype(bf16)
    for head in range(HEAD_GROUP):
        probs, _, _, v_head, _, _, _ = head_scores(
            qn_ref[0], q1_ref[0], q2_ref[0], kv, k1_ref[0], k2_ref[0], seen_ref[...], scale, head
        )
        out_ref[0, :, head * VDIM : (head + 1) * VDIM] = dot(
            probs.astype(bf16), v_head, 1, 0
        ).astype(bf16)


def attend_back_kernel(
    scale,
    seen_ref,
    qn_ref,
    q1_ref,
    q2_ref,
    lat_ref,
    k1_ref,
    k2_ref,
    kvb_ref,
    do_ref,
    dqn_ref,
    dq1_ref,
    dq2_ref,
    dlat_ref,
    dk1_ref,
    dk2_ref,
    dkvb_ref,
    kvg_ref,
    acc_ref,
):
    group, micro = pl.program_id(0), pl.program_id(1)
    width = NOPE + VDIM

    @pl.when(group == 0)
    def _():
        dlat_ref[micro] = jnp.zeros(dlat_ref.shape[1:], f32)
        dk1_ref[micro] = jnp.zeros(dk1_ref.shape[1:], f32)
        dk2_ref[micro] = jnp.zeros(dk2_ref.shape[1:], f32)

    lat = lat_ref[0]
    kvb = kvb_ref[...]
    kv = dot(lat, kvb, 1, 0).astype(bf16)
    k1, k2 = k1_ref[0], k2_ref[0]
    dq1 = jnp.zeros(dq1_ref.shape[1:], f32)
    dq2 = jnp.zeros(dq2_ref.shape[1:], f32)
    dk1 = jnp.zeros(k1.shape, f32)
    dk2 = jnp.zeros(k2.shape, f32)
    for head in range(HEAD_GROUP):
        probs, q_head, k_head, v_head, q1m, q2m, mine = head_scores(
            qn_ref[0], q1_ref[0], q2_ref[0], kv, k1, k2, seen_ref[...], scale, head
        )
        d_out = do_ref[0, :, head * VDIM : (head + 1) * VDIM]
        dprobs = dot(d_out, v_head, 1, 1)
        delta = jnp.sum(probs * dprobs, axis=-1, keepdims=True)
        ds = (probs * (dprobs - delta)).astype(bf16)
        dqn_ref[0, :, head * NOPE : (head + 1) * NOPE] = (dot(ds, k_head, 1, 0) * scale).astype(bf16)
        dq1 = dq1 + jnp.where(mine, dot(ds, k1, 1, 0), 0.0)
        dq2 = dq2 + jnp.where(mine, dot(ds, k2, 1, 0), 0.0)
        dk1 = dk1 + dot(ds, q1m, 0, 0)
        dk2 = dk2 + dot(ds, q2m, 0, 0)
        kvg_ref[:, head * width : head * width + NOPE] = (dot(ds, q_head, 0, 0) * scale).astype(bf16)
        kvg_ref[:, head * width + NOPE : (head + 1) * width] = dot(
            probs.astype(bf16), d_out, 0, 0
        ).astype(bf16)
    dq1_ref[0] = dq1 * scale
    dq2_ref[0] = dq2 * scale
    dk1_ref[micro] += dk1 * scale
    dk2_ref[micro] += dk2 * scale
    kvg = kvg_ref[...]
    dlat_ref[micro] += dot(kvg, kvb, 1, 1)
    part = dot(lat, kvg, 0, 0)

    @pl.when(micro == 0)
    def _():
        acc_ref[...] = part

    @pl.when(micro > 0)
    def _():
        acc_ref[...] += part

    @pl.when(micro == pl.num_programs(1) - 1)
    def _():
        dkvb_ref[...] = acc_ref[...].astype(bf16)


def attention_specs(micros, rows, length):
    groups = HEADS // HEAD_GROUP
    wide = HEAD_GROUP * NOPE
    specs = [
        pl.BlockSpec((1, length), lambda g, m: (0, 0)),
        pl.BlockSpec((1, rows, wide), lambda g, m: (m, 0, g)),
        pl.BlockSpec((1, rows, GROUP_LANES), lambda g, m: (m, 0, g)),
        pl.BlockSpec((1, rows, GROUP_LANES), lambda g, m: (m, 0, g)),
        pl.BlockSpec((1, length, RANK), lambda g, m: (m, 0, 0)),
        pl.BlockSpec((1, length, GROUP_LANES), lambda g, m: (m, 0, 0)),
        pl.BlockSpec((1, length, GROUP_LANES), lambda g, m: (m, 0, 0)),
        pl.BlockSpec((RANK, HEAD_GROUP * (NOPE + VDIM)), lambda g, m: (0, g)),
    ]
    return (groups, micros), specs, pl.BlockSpec((1, rows, wide), lambda g, m: (m, 0, g))


def attend(seen, qn, q1, q2, lat, k1, k2, kvb, scale):
    micros, rows, _ = qn.shape
    length = lat.shape[1]
    grid, specs, out_spec = attention_specs(micros, rows, length)
    return pl.pallas_call(
        functools.partial(attend_kernel, scale),
        grid=grid,
        in_specs=specs,
        out_specs=out_spec,
        out_shape=jax.ShapeDtypeStruct(qn.shape, bf16),
        compiler_params=pltpu.CompilerParams(vmem_limit_bytes=48 << 20),
        name="attend",
    )(seen, qn, q1, q2, lat, k1, k2, kvb)


def attend_back(seen, qn, q1, q2, lat, k1, k2, kvb, d_out, scale):
    micros, rows, _ = qn.shape
    length = lat.shape[1]
    grid, specs, out_spec = attention_specs(micros, rows, length)
    whole = lambda g, m: (0, 0, 0)
    return pl.pallas_call(
        functools.partial(attend_back_kernel, scale),
        grid=grid,
        in_specs=specs + [out_spec],
        out_specs=[
            out_spec,
            pl.BlockSpec((1, rows, GROUP_LANES), lambda g, m: (m, 0, g)),
            pl.BlockSpec((1, rows, GROUP_LANES), lambda g, m: (m, 0, g)),
            pl.BlockSpec(lat.shape, whole),
            pl.BlockSpec(k1.shape, whole),
            pl.BlockSpec(k2.shape, whole),
            pl.BlockSpec((RANK, HEAD_GROUP * (NOPE + VDIM)), lambda g, m: (0, g)),
        ],
        out_shape=[
            jax.ShapeDtypeStruct(qn.shape, bf16),
            jax.ShapeDtypeStruct(q1.shape, f32),
            jax.ShapeDtypeStruct(q2.shape, f32),
            jax.ShapeDtypeStruct(lat.shape, f32),
            jax.ShapeDtypeStruct(k1.shape, f32),
            jax.ShapeDtypeStruct(k2.shape, f32),
            jax.ShapeDtypeStruct(kvb.shape, bf16),
        ],
        scratch_shapes=[
            pltpu.VMEM((length, HEAD_GROUP * (NOPE + VDIM)), bf16),
            pltpu.VMEM((RANK, HEAD_GROUP * (NOPE + VDIM)), f32),
        ],
        compiler_params=pltpu.CompilerParams(vmem_limit_bytes=48 << 20),
        name="attend_back",
    )(seen, qn, q1, q2, lat, k1, k2, kvb, d_out)


class Place:
    def __init__(self):
        self.r = lax.axis_index("rep")
        self.z = lax.axis_index("shard")
        self.core = self.r % 2
        self.chip = self.r // 2
        self.x = self.chip % 2
        self.y = self.chip // 2
        self.peer = (self.r + 1 - 2 * self.core, self.z)
        self.across = {
            "x": (self.r + 2 - 4 * self.x, self.z),
            "y": (self.r + 4 - 8 * self.y, self.z),
        }
        cx = self.chip + 1 - 2 * self.x
        cy = self.chip + 2 - 4 * self.y
        self.chips = {"": self.chip, "x": cx, "y": cy, "xy": cx + 2 - 4 * self.y}

    def along(self, step):
        return (self.r, (self.z + step) % 4)

    def shard_at(self, step):
        return (self.z + step) % 4


class Sems:
    def __init__(self, send, recv):
        self.send, self.recv = send, recv
        self.count = 0
        self.pending = []

    def slot(self):
        self.count += 1
        return self.count - 1

    def copy(self, src, dst, slot, device):
        return pltpu.make_async_remote_copy(
            src_ref=src,
            dst_ref=dst,
            send_sem=self.send.at[slot],
            recv_sem=self.recv.at[slot],
            device_id=device,
            device_id_type=MESH,
        )

    def push(self, src, dst, slot, device, when=None):
        under(when, lambda: self.copy(src, dst, slot, device).start())
        self.pending.append((lambda: self.copy(src, dst, slot, device).wait_send(), when))
        return self.pending[-1]

    def settle(self, entry):
        self.pending.remove(entry)
        under(entry[1], entry[0])

    def arrived(self, dst, slot, device, when=None):
        under(when, lambda: self.copy(dst, dst, slot, device).wait_recv())

    def drain(self):
        for wait, when in self.pending:
            under(when, wait)
        self.pending = []


def inside(z):
    return jnp.minimum(jnp.maximum(z, 0), 3)


def under(condition, act):
    if condition is None:
        act()
    else:
        pl.when(condition)(act)


def greet(devices):
    barrier = pltpu.get_barrier_semaphore()
    for device in devices:
        pl.semaphore_signal(barrier, inc=1, device_id=device, device_id_type=MESH)
    pl.semaphore_wait(barrier, len(devices))


def lanes(start, size):
    return pl.ds(pl.multiple_of(start, 128), size)


def rows16(start, size):
    return pl.ds(pl.multiple_of(start, 16), size)


class Through:
    def __init__(self, src, buffer, dst, sem):
        self.into = pltpu.make_async_copy(src, buffer, sem)
        self.out = pltpu.make_async_copy(buffer, dst, sem)

    def start(self):
        self.into.start()

    def turn(self):
        self.into.wait()
        self.out.start()

    def wait(self):
        self.out.wait()


class PlaneGather:
    def __init__(self, sems, place, part, half, by, when=None):
        self.sems, self.place, self.part, self.half, self.by = sems, place, part, half, by
        self.when = when
        self.slots = {k: sems.slot() for k in ("x", "y", "xy", "core")}

    def first(self, src=None):
        p = self.place
        mine = self.part(p.core, p.chip)
        for axis in ("x", "y"):
            self.push(mine if src is None else src, mine, self.slots[axis], p.across[axis])

    def push(self, src, dst, slot, device):
        self.sems.push(src, dst, slot, device, self.when)

    def arrived(self, dst, slot, device):
        self.sems.arrived(dst, slot, device, self.when)

    def second(self):
        p = self.place
        for axis in ("x", "y"):
            got = self.part(p.core, p.chips[axis])
            self.arrived(got, self.slots[axis], p.across[axis])
        via = self.by
        other = "y" if via == "x" else "x"
        got = self.part(p.core, p.chips[via])
        self.push(got, got, self.slots["xy"], p.across[other])

    def third(self):
        p = self.place
        got = self.part(p.core, p.chips["xy"])
        self.arrived(got, self.slots["xy"], p.across["y" if self.by == "x" else "x"])
        half = self.half(p.core)
        self.push(half, half, self.slots["core"], p.peer)

    def fourth(self):
        p = self.place
        self.arrived(self.half(1 - p.core), self.slots["core"], p.peer)


def weight_regions(place, refs, shard):
    q, kr, kvb, out = refs
    ds = q.shape[1] // 4
    cols = lanes(shard * ds, ds)

    def row_split(ref, n):
        half = ref.shape[0] // 2
        return (
            lambda core, chip: ref.at[rows16(core * half + chip * n, n), cols],
            lambda core: ref.at[rows16(core * half, half), cols],
        )

    def col_split(ref, full):
        rows = full // 4
        half = ref.shape[-1] // 2
        n = half // 4
        lead = (slice(None),) * (len(ref.shape) - 2)
        span = rows16(shard * rows, rows)
        return (
            lambda core, chip: ref.at[(*lead, span, lanes(core * half + chip * n, n))],
            lambda core: ref.at[(*lead, span, lanes(core * half, half))],
        )

    return [
        row_split(q, q.shape[0] // 8),
        row_split(kr, kr.shape[0] // 8),
        col_split(kvb, kvb.shape[0]),
        col_split(out, out.shape[0]),
    ]


def own_part(refs, place):
    q, kr, kvb, out, sh = refs
    res = []
    for ref in (q, kr):
        n = ref.shape[0] // 8
        res.append(ref.at[rows16(place.core * 4 * n + place.chip * n, n)])
    for ref in (kvb, out):
        n = ref.shape[-1] // 8
        res.append(ref.at[:, lanes(place.core * 4 * n + place.chip * n, n)])
    n = sh.shape[-1] // 8
    res.append(sh.at[:, :, lanes(place.r * n, n)])
    return res


ITEMS = 4
GATHER_ORDER = (1, 0, 2, 3)
GATHER_SEMS = 6 + ITEMS * 6 * 5
LAG = 6


class WeightGather:
    def __init__(self, place, sems, mine, outs):
        self.place, self.sems, self.mine, self.outs = place, sems, mine, outs
        z = place.z
        self.here = weight_regions(place, outs, z)
        self.slots = {}
        units = []
        for i in GATHER_ORDER:
            for d in (1, 2, 3):
                for s in (1, -1):
                    self.slots[i, d, s] = sems.slot()
                    exists = z >= d if s == 1 else z + d <= 3
                    part, half = weight_regions(place, outs, inside(z - s * d))[i]
                    by = "x" if (d + i) % 2 == 0 else "y"
                    units.append(
                        (i, d, s, exists, part, PlaneGather(sems, place, part, half, by, exists))
                    )
        for i in GATHER_ORDER[:2]:
            self.own(i)
        self.units = units

    def run(self, late):
        units = self.units
        for n in range(len(units) + 3 * LAG):
            if n == 3 * len(units) // 4:
                late()
            if n < len(units):
                if n % 6 == 0 and n // 6 + 2 < ITEMS:
                    self.own(GATHER_ORDER[n // 6 + 2])
                self.along(units[n])
            for lag, name in ((LAG, "second"), (2 * LAG, "third"), (3 * LAG, "fourth")):
                if 0 <= n - lag < len(units):
                    getattr(units[n - lag][5], name)()

    def onward(self, src, dst, i, d, s, exists=None):
        if d > 3:
            return
        z = self.place.z
        more = z < 3 if s == 1 else z > 0
        if exists is not None:
            more = more & exists
        device = (self.place.r, inside(z + s))
        self.sems.push(src, dst, self.slots[i, d, s], device, more)

    def own(self, i):
        for s in (1, -1):
            self.onward(self.mine[i], self.here[i][0](self.place.core, self.place.chip), i, 1, s)

    def along(self, unit):
        i, d, s, exists, part, spread = unit
        z = self.place.z
        got = part(self.place.core, self.place.chip)
        device = (self.place.r, inside(z - s))
        self.sems.arrived(got, self.slots[i, d, s], device, exists)
        self.onward(got, got, i, d + 1, s, exists)
        spread.first()


def gather_kernel(*refs):
    ins, shared, gain = refs[:ITEMS], refs[ITEMS], refs[ITEMS + 1]
    refs = refs[ITEMS + 2 :]
    outs, shared_out, gains = refs[:ITEMS], refs[ITEMS], refs[ITEMS + 1]
    refs = refs[ITEMS + 2 :]
    buffers, (gain_buffer, send, recv, local) = refs[:ITEMS], refs[ITEMS:]
    place = Place()
    sems = Sems(send, recv)
    greet([place.peer, place.across["x"], place.across["y"]] + [place.along(k) for k in (1, 2, 3)])
    mine = own_part((*ins, shared), place)
    ds = ins[0].shape[1]
    own = [
        outs[0].at[:, lanes(place.z * ds, ds)],
        outs[1].at[:, lanes(place.z * ds, ds)],
        outs[2].at[rows16(place.z * ins[2].shape[0], ins[2].shape[0])],
        outs[3].at[rows16(place.z * ins[3].shape[0], ins[3].shape[0])],
    ]
    kept = [Through(ins[i], buffers[i], own[i], local.at[i]) for i in range(ITEMS)]
    kept.append(Through(gain, gain_buffer, gains.at[place.z], local.at[ITEMS]))
    gain_slots = [sems.slot() for _ in range(3)]
    shared_slots = [sems.slot() for _ in range(3)]
    for k in (1, 2, 3):
        sems.push(gain, gains.at[place.z], gain_slots[k - 1], place.along(k))
    job = WeightGather(place, sems, mine, outs)
    for copy in kept:
        copy.start()
    for copy in kept:
        copy.turn()

    def late():
        for k in (1, 2, 3):
            sems.push(mine[ITEMS], shared_out.at[:, k - 1], shared_slots[k - 1], place.along(k))

    job.run(late)
    for k in (1, 2, 3):
        sems.arrived(gains.at[place.shard_at(4 - k)], gain_slots[k - 1], place.along(4 - k))
        sems.arrived(shared_out.at[:, k - 1], shared_slots[k - 1], place.along(4 - k))
    sems.drain()
    for copy in kept:
        copy.wait()


def gather_weights(q, kr, kvb, out, sh, gain, fast):
    if not fast:
        every = lambda w, axis: lax.all_gather(w, "shard", axis=axis, tiled=True)
        return (
            every(q, 1),
            every(kr, 1),
            every(kvb, 0),
            every(out, 0),
            every(sh, 1),
            lax.all_gather(gain, "shard", axis=0),
        )
    shape = jax.ShapeDtypeStruct
    *whole, rest, gains = pl.pallas_call(
        gather_kernel,
        in_specs=[pl.BlockSpec(memory_space=HBM)] * 6,
        out_specs=[pl.BlockSpec(memory_space=HBM)] * 6,
        out_shape=[
            shape((q.shape[0], q.shape[1] * 4), bf16),
            shape((kr.shape[0], kr.shape[1] * 4), bf16),
            shape((kvb.shape[0] * 4, kvb.shape[1]), bf16),
            shape((out.shape[0] * 4, out.shape[1]), bf16),
            shape((3, 3, sh.shape[1], sh.shape[2] // 8), bf16),
            shape((4,) + gain.shape, bf16),
        ],
        scratch_shapes=[pltpu.VMEM(w.shape, bf16) for w in (q, kr, kvb, out, gain)]
        + [
            pltpu.SemaphoreType.DMA((GATHER_SEMS,)),
            pltpu.SemaphoreType.DMA((GATHER_SEMS,)),
            pltpu.SemaphoreType.DMA((ITEMS + 1,)),
        ],
        compiler_params=pltpu.CompilerParams(
            collective_id=0, has_side_effects=True, vmem_limit_bytes=32 << 20
        ),
        name="gather_weights",
    )(q, kr, kvb, out, sh, gain)
    rest = lax.all_gather(rest, "rep", axis=3, tiled=True)
    return (*whole, rest.reshape(3, -1, sh.shape[2]), gains)


def along_z(tensor, step):
    return lax.ppermute(tensor, "shard", [(i, (i + step) % 4) for i in range(4)])


def over(tensor, mask):
    return lax.ppermute(tensor, "rep", [(i, i ^ mask) for i in range(8)])


def z_all(tensor, fast):
    if not fast:
        return lax.all_gather(tensor, "shard", axis=1, tiled=True)
    return jnp.concatenate([tensor] + [along_z(tensor, k) for k in (1, 2, 3)], axis=1)


def z_home(tensor, fast):
    if not fast:
        return lax.psum_scatter(tensor.astype(f32), "shard", scatter_dimension=1, tiled=True)
    rows = tensor.shape[1] // 4
    blocks = [lax.slice_in_dim(tensor, k * rows, (k + 1) * rows, axis=1) for k in range(4)]
    got = [along_z(blocks[k], -k).astype(f32) for k in (1, 2, 3)]
    return blocks[0].astype(f32) + got[0] + got[1] + got[2]


def swap_kernel(count, axes, *refs):
    ins, outs, buffers = (refs[n * count : (n + 1) * count] for n in range(3))
    send, recv, local = refs[3 * count :]
    place = Place()
    sems = Sems(send, recv)
    greet([place.peer])

    def cut(i, core):
        if axes[i] is None:
            return ins[i]
        n = ins[i].shape[axes[i]] // 2
        if axes[i] == 0:
            return ins[i].at[rows16(core * n, n)]
        return ins[i].at[:, lanes(core * n, n)]

    for i in range(count):
        sems.push(cut(i, 1 - place.core), outs[i].at[1], sems.slot(), place.peer)
    kept = [
        Through(cut(i, place.core), buffers[i], outs[i].at[0], local.at[i]) for i in range(count)
    ]
    for copy in kept:
        copy.start()
    for copy in kept:
        copy.turn()
    for i in range(count):
        sems.arrived(outs[i].at[1], i, place.peer)
    sems.drain()
    for copy in kept:
        copy.wait()


def core_swap(arrays, axes, fast, ident):
    count = len(arrays)
    if not fast:
        reps = lax.axis_size("rep")
        core = lax.axis_index("rep") % 2
        res = []
        for a, axis in zip(arrays, axes):
            keep = give = a
            if axis is not None:
                n = a.shape[axis] // 2
                keep = lax.dynamic_slice_in_dim(a, core * n, n, axis)
                give = lax.dynamic_slice_in_dim(a, (1 - core) * n, n, axis)
            got = lax.ppermute(give, "rep", [(i, i + 1 - 2 * (i % 2)) for i in range(reps)])
            res.append(jnp.stack([keep, got]))
        return res
    shapes = [
        tuple(n // 2 if d == axis else n for d, n in enumerate(a.shape))
        for a, axis in zip(arrays, axes)
    ]
    return pl.pallas_call(
        functools.partial(swap_kernel, count, axes),
        in_specs=[pl.BlockSpec(memory_space=HBM)] * count,
        out_specs=[pl.BlockSpec(memory_space=HBM)] * count,
        out_shape=[jax.ShapeDtypeStruct((2,) + s, a.dtype) for s, a in zip(shapes, arrays)],
        scratch_shapes=[pltpu.VMEM(s, a.dtype) for s, a in zip(shapes, arrays)]
        + [
            pltpu.SemaphoreType.DMA((count,)),
            pltpu.SemaphoreType.DMA((count,)),
            pltpu.SemaphoreType.DMA((count,)),
        ],
        compiler_params=pltpu.CompilerParams(
            collective_id=ident, has_side_effects=True, vmem_limit_bytes=32 << 20
        ),
        name="core_swap",
    )(*arrays)


def add_rows(dst, terms):
    lead = dst.shape[:-2]
    rows = max(n for n in (16, 32, 48, 64, 80) if dst.shape[-2] % n == 0)
    steps = dst.shape[-2] // rows

    def body(step, carry):
        span = pl.ds(pl.multiple_of(step * rows, rows), rows)
        where = (slice(None),) * len(lead) + (span,)
        total = terms[0][where].astype(f32)
        for t in terms[1:]:
            total = total + t[where].astype(f32)
        dst[where] = total.astype(dst.dtype)
        return carry

    lax.fori_loop(0, steps, body, 0)


def reduce_anywhere(q, kr, kvb, out, sh, ex, gain):
    core = lax.axis_index("rep") % 2

    def whole(g, axis):
        wide = jnp.zeros(g.shape[:axis] + (g.shape[axis] * 2,) + g.shape[axis + 1 :], f32)
        return lax.dynamic_update_slice_in_dim(wide, g.astype(f32), core * g.shape[axis], axis)

    def total(g, axis, along):
        g = lax.psum_scatter(whole(g, axis), "shard", scatter_dimension=along, tiled=True)
        return lax.psum(g, "rep")

    return (
        total(q, 0, 1),
        total(kr, 0, 1),
        total(kvb, 1, 0),
        total(out, 1, 0),
        total(sh, 2, 1),
        lax.psum(whole(ex, 2), "rep"),
        lax.psum(lax.psum_scatter(gain, "shard", scatter_dimension=0, tiled=True), "rep")[0],
    )


class Unit:
    def __init__(self, job, name, u, axis, part, got1, got2, own=None, home=None, got3=None, last=None):
        self.job, self.name, self.u = job, name, u
        self.axis, self.other = axis, "y" if axis == "x" else "x"
        self.part, self.got1, self.got2, self.own = part, got1, got2, own
        self.home, self.got3, self.last = home, got3, last
        self.slots = [job.sems.slot() for _ in range(4)]

    def stage1(self):
        job = self.job
        place = job.place
        for n, chip in enumerate((self.axis, "xy")):
            job.sems.push(
                self.part(place.chips[chip]), self.got1.at[n], self.slots[n], place.across[self.axis]
            )
        if self.own is not None:
            ring, sem = self.own
            self.loads = [
                pltpu.make_async_copy(
                    self.part(place.chips["" if n == 0 else self.other]), ring.at[n], sem.at[n]
                )
                for n in (0, 1)
            ]
            for copy in self.loads:
                copy.start()
            self.mine = [ring.at[0], ring.at[1]]
        else:
            self.mine = [self.part(place.chips[""]), self.part(place.chips[self.other])]

    def stage2(self):
        sems, place = self.job.sems, self.job.place
        for n in (1, 0):
            if self.own is not None:
                self.loads[n].wait()
            sems.arrived(self.got1.at[n], self.slots[n], place.across[self.axis])
            add_rows(self.got1.at[n], [self.got1.at[n], self.mine[n]])
            if n == 1:
                sems.push(self.got1.at[1], self.got2, self.slots[2], place.across[self.other])

    def stage3(self):
        sems, place = self.job.sems, self.job.place
        sems.arrived(self.got2, self.slots[2], place.across[self.other])
        add_rows(self.got1.at[0], [self.got1.at[0], self.got2])
        if self.home:
            sems.push(self.got1.at[0], self.got3.at[self.home - 1], self.slots[3], place.along(self.home))

    def stage4(self):
        if self.last is None:
            return
        job = self.job
        place = job.place
        for unit in job.units:
            if unit.name == self.name and unit.home:
                got = unit.got3.at[unit.home - 1]
                job.sems.arrived(got, unit.slots[3], place.along(4 - unit.home))
        if self.got3 is not None:
            add_rows(self.got1.at[0], [self.got1.at[0]] + [self.got3.at[n] for n in range(3)])
        src, part, half, sem, by = self.last
        self.stay = pltpu.make_async_copy(src, part(place.core, place.chip), sem)
        self.stay.start()
        self.spread = PlaneGather(job.sems, place, part, half, by)
        self.spread.first(src)

    def stage5(self):
        if self.last is not None:
            self.spread.second()

    def stage6(self):
        if self.last is not None:
            self.stay.wait()
            self.spread.third()

    def stage7(self):
        if self.last is not None:
            self.spread.fourth()


class Pump:
    LAGS = (0, 3, 3, 2, 1, 1, 1)

    def __init__(self, place, sems):
        self.place, self.sems = place, sems
        self.units = []
        self.at = [0] * 7

    def tick(self, flush=False):
        for n in range(7):
            ahead = len(self.units) if n == 0 else self.at[n - 1]
            if self.at[n] < ahead - (0 if flush else self.LAGS[n]):
                getattr(self.units[self.at[n]], "stage%d" % (n + 1))()
                self.at[n] += 1

    def run(self, count):
        for _ in range(count):
            self.tick()

    def end(self):
        while self.at[-1] < len(self.units):
            before = list(self.at)
            self.tick()
            if self.at == before:
                self.tick(True)


BACK_IN = (
    "gsh",
    "gex",
    "gout",
    "q",
    "kvb",
    "kq",
    "kkr",
    "x",
    "mid",
    "lat",
    "k1",
    "k2",
    "seen",
    "do",
    "ha",
    "latent",
    "kgain",
    "again",
    "fgain",
    "cos",
    "sin",
    "rtr",
)
BACK_HBM = 9
BACK_OUT = (
    "oq",
    "okr",
    "okvb",
    "oout",
    "osh",
    "osd",
    "oex",
    "zsh",
    "ogain",
    "ograd",
)
BACK_SLOTS = 3 + 3 + 5 + 10 + 28 * 4 + 7 * 4
EARLY = 2


def back_kernel(scale, names, *refs):
    r = dict(zip(names, refs))
    place = Place()
    sems = Sems(r["send"], r["recv"])
    others = [place.peer]
    for axes in ("x", "y", "xy"):
        for flip in (place.core, 1 - place.core):
            others.append((place.chips[axes] * 2 + flip, place.z))
    greet(others + [place.along(k) for k in (1, 2, 3)])
    load = r["load"]
    pump = Pump(place, sems)
    core = place.core
    toks = r["ha"].shape[0]
    rows = toks // 2

    ff = r["gsh"].shape[1] // 4
    shared_slots = [sems.slot() for _ in range(3)]
    for k in (1, 2, 3):
        sems.push(
            r["gsh"].at[:EARLY, k * ff : (k + 1) * ff], r["zsh"].at[k - 1], shared_slots[k - 1], place.along(4 - k)
        )
    swap = {name: sems.slot() for name in ("ha", "kvb", "q", "kvd", "rtr")}
    sems.push(r["ha"], r["s_ha"], swap["ha"], place.peer)
    sems.push(r["rtr"], r["s_rtr"], swap["rtr"], place.peer)
    begin = [
        pltpu.make_async_copy(r["q"], r["qs"], load.at[0]),
        pltpu.make_async_copy(r["kvb"], r["kvbs"], load.at[1]),
    ]
    for copy in begin:
        copy.start()

    def out_split(o, by_rows):
        if by_rows:
            half = o.shape[0] // 2
            n = half // 4
            return (
                lambda c, chip: o.at[rows16(c * half + chip * n, n)],
                lambda c: o.at[rows16(c * half, half)],
            )
        half = o.shape[-1] // 2
        n = half // 4
        lead = (slice(None),) * (len(o.shape) - 1)
        return (
            lambda c, chip: o.at[(*lead, lanes(c * half + chip * n, n))],
            lambda c: o.at[(*lead, lanes(c * half, half))],
        )

    rings = 0

    def ring(shape_ref):
        nonlocal rings
        slot = rings % 4
        rings += 1
        return slot

    def add_matrices(name, source, count, out, by, ringed):
        for u in range(count):
            n = source.shape[-1] // 4
            own = None
            if ringed:
                slot = ring(None)
                own = (r["ring_" + name].at[slot], r["ringsem"].at[slot])
            last = None
            if u == count - 1:
                last = (r["got1_" + name].at[:, 0], *out_split(out, False), r["keep"].at[len(pump.units) % 8], by)
            pump.units.append(
                Unit(
                    pump,
                    name,
                    u,
                    "x" if u % 2 == 0 else "y",
                    lambda chip, u=u: source.at[u, :, lanes(chip * n, n)],
                    r["got1_" + name].at[u],
                    r["got2_" + name].at[u],
                    own=own,
                    last=last,
                )
            )

    def add_sharded(name, part_of, out, by_rows, by, ringed=None):
        for n, k in enumerate((1, 2, 3, 4)):
            u, s = k % 4, place.shard_at(k)
            own = None
            if ringed:
                slot = ring(None)
                own = (r["ring_" + ringed].at[slot], r["ringsem"].at[slot])
            last = None
            if k == 4:
                last = (r["got1_" + name].at[0, 0], *out_split(out, by_rows), r["keep"].at[len(pump.units) % 8], by)
            pump.units.append(
                Unit(
                    pump,
                    name,
                    u,
                    "x" if n % 2 == 0 else "y",
                    lambda chip, s=s, k=k: part_of(s, k, chip),
                    r["got1_" + name].at[u],
                    r["got2_" + name].at[u],
                    own=own,
                    home=k % 4,
                    got3=r["got3_" + name],
                    last=last,
                )
            )

    add_matrices("ex", r["gex"], r["gex"].shape[0], r["oex"], "x", True)
    block = r["gout"].shape[0] // 4
    n_out = r["gout"].shape[1] // 4
    add_sharded(
        "out",
        lambda s, k, chip: r["gout"].at[rows16(s * block, block), lanes(chip * n_out, n_out)],
        r["oout"],
        False,
        "y",
        "out",
    )
    n_sd = r["gsh"].shape[2] // 4
    add_sharded(
        "sd",
        lambda s, k, chip: r["gsh"].at[
            EARLY, (4 - k) % 4 * ff : ((4 - k) % 4 + 1) * ff, lanes(chip * n_sd, n_sd)
        ],
        r["osd"],
        False,
        "x",
        "ex",
    )
    pump.run(3)
    for copy in begin:
        copy.wait()

    qs, kvbs, kvg, acc, dlat, dkvb = (r[n] for n in ("qs", "kvbs", "kvg", "acc", "dlat", "dkvb"))
    n1 = HEADS * NOPE
    n2 = HEADS * (NOPE + HALF_ROPE)
    width = NOPE + VDIM
    lane = lax.broadcasted_iota(jnp.int32, (1, GROUP_LANES), 1)

    def attention_step(group, micro):
        span = slice(micro * rows, (micro + 1) * rows)
        at = group * GROUP_LANES
        lat, k1, k2 = r["lat"][micro], r["k1"][micro], r["k2"][micro]
        q1, q2 = qs[span, n1 + at : n1 + at + GROUP_LANES], qs[span, n2 + at : n2 + at + GROUP_LANES]
        dq1 = jnp.zeros(q1.shape, f32)
        dq2 = jnp.zeros(q2.shape, f32)
        dk1 = jnp.zeros(k1.shape, f32)
        dk2 = jnp.zeros(k2.shape, f32)
        for pair in (0, 1):
            cols = slice((group * 4 + pair * 2) * width, (group * 4 + pair * 2 + 2) * width)
            weight = kvbs[:, cols]
            kv = dot(lat, weight, 1, 0).astype(bf16)
            for n in (0, 1):
                head = pair * 2 + n
                here = slice((group * 4 + head) * NOPE, (group * 4 + head + 1) * NOPE)
                mine = (lane >= head * HALF_ROPE) & (lane < (head + 1) * HALF_ROPE)
                q_head = qs[span, here]
                k_head = kv[:, n * width : n * width + NOPE]
                v_head = kv[:, n * width + NOPE : (n + 1) * width]
                q1m = jnp.where(mine, q1, jnp.zeros_like(q1))
                q2m = jnp.where(mine, q2, jnp.zeros_like(q2))
                scores = dot(q_head, k_head, 1, 1) + dot(q1m, k1, 1, 1) + dot(q2m, k2, 1, 1)
                scores = jnp.where(r["seen"][...] > 0.0, scores * scale, masked_score)
                expo = jnp.exp(scores - jnp.max(scores, axis=-1, keepdims=True))
                probs = expo / jnp.sum(expo, axis=-1, keepdims=True)
                d_out = r["do"][micro, :, here]
                dprobs = dot(d_out, v_head, 1, 1)
                delta = jnp.sum(probs * dprobs, axis=-1, keepdims=True)
                ds = (probs * (dprobs - delta)).astype(bf16)
                qs[span, here] = (dot(ds, k_head, 1, 0) * scale).astype(bf16)
                dq1 = dq1 + jnp.where(mine, dot(ds, k1, 1, 0), 0.0)
                dq2 = dq2 + jnp.where(mine, dot(ds, k2, 1, 0), 0.0)
                dk1 = dk1 + dot(ds, q1m, 0, 0)
                dk2 = dk2 + dot(ds, q2m, 0, 0)
                kvg[:, n * width : n * width + NOPE] = (dot(ds, q_head, 0, 0) * scale).astype(bf16)
                kvg[:, n * width + NOPE : (n + 1) * width] = dot(
                    probs.astype(bf16), d_out, 0, 0
                ).astype(bf16)
            terms = kvg[...]
            if group == 0 and pair == 0:
                dlat[micro] = dot(terms, weight, 1, 1)
            else:
                dlat[micro] += dot(terms, weight, 1, 1)
            part = dot(lat, terms, 0, 0)
            hold = slice(pair * 2 * width, (pair + 1) * 2 * width)
            if micro == 0:
                acc[:, hold] = part
            else:
                dkvb[:, cols] = (acc[:, hold] + part).astype(bf16)
        dq1, dq2 = dq1 * scale, dq2 * scale
        cosine, sine = r["cos"][...], r["sin"][...]
        qs[span, n1 + at : n1 + at + GROUP_LANES] = (dq1 * cosine + dq2 * sine).astype(bf16)
        qs[span, n2 + at : n2 + at + GROUP_LANES] = (dq2 * cosine - dq1 * sine).astype(bf16)
        for ref, value in ((r["dk1"], dk1), (r["dk2"], dk2)):
            if group == 0:
                ref[micro] = value * scale
            else:
                ref[micro] += value * scale

    for group in range(HEADS // HEAD_GROUP):
        for micro in (0, 1):
            attention_step(group, micro)
            pump.run(1)

    pack, zs = r["pack"], r["zs"]
    fold = lambda t: sum(t[:, n * HALF_ROPE : (n + 1) * HALF_ROPE] for n in range(HEAD_GROUP))
    for micro in (0, 1):
        pack[micro, :, :RANK] = dlat[micro].astype(bf16)
        pack[micro, :, RANK : RANK + HALF_ROPE] = fold(r["dk1"][micro]).astype(bf16)
        pack[micro, :, RANK + HALF_ROPE : RANK + ROPE] = fold(r["dk2"][micro]).astype(bf16)
        pack[micro, :, RANK + ROPE :] = jnp.zeros((pack.shape[1], ROPE), bf16)
    z_slots = [sems.slot() for _ in range(3)]
    for k in (1, 2, 3):
        sems.push(pack.at[:, k * rows : (k + 1) * rows], zs.at[k - 1], z_slots[k - 1], place.along(4 - k))
    half_q, half_kvb = qs.shape[1] // 2, dkvb.shape[1] // 2
    sems.push(qs.at[:, lanes((1 - core) * half_q, half_q)], r["s_q"], swap["q"], place.peer)
    kvb_push = sems.push(
        dkvb.at[:, lanes((1 - core) * half_kvb, half_kvb)], r["s_kvb"], swap["kvb"], place.peer
    )
    pump.run(1)

    sems.arrived(r["s_kvb"], swap["kvb"], place.peer)
    add_rows(r["s_kvb"], [r["s_kvb"], dkvb.at[:, lanes(core * half_kvb, half_kvb)]])
    n_kvb, b_kvb = half_kvb // 4, dkvb.shape[0] // 4
    add_sharded(
        "kvb",
        lambda s, k, chip: r["s_kvb"].at[rows16(s * b_kvb, b_kvb), lanes(chip * n_kvb, n_kvb)],
        r["okvb"],
        False,
        "x",
    )
    sems.arrived(r["s_ha"], swap["ha"], place.peer)
    sems.arrived(r["s_q"], swap["q"], place.peer)
    gq, ha, s_ha = r["gq"], r["ha"], r["s_ha"]

    def q_tile(t, carry):
        own = qs[:, lanes(core * half_q + t * 128, 128)]
        got = r["s_q"][:, lanes(t * 128, 128)]
        gq[rows16(t * 128, 128)] = (dot(own, ha[...], 0, 0) + dot(got, s_ha[...], 0, 0)).astype(bf16)
        return carry

    for part in range(4):
        lax.fori_loop(part * 3, part * 3 + 3, q_tile, 0)
        pump.run(1)
    r_q, c_q = gq.shape[0] // 4, gq.shape[1] // 4
    add_sharded(
        "q",
        lambda s, k, chip: gq.at[rows16(chip * r_q, r_q), lanes(s * c_q, c_q)],
        r["oq"],
        True,
        "y",
    )
    pump.run(4)

    for k in (1, 2, 3):
        sems.arrived(zs.at[k - 1], z_slots[k - 1], place.along(k))
    kvd, gains = r["kvd"], r["gains"]
    kv_gain_grad = jnp.zeros((1, RANK), f32)
    for micro in (0, 1):
        span = slice(micro * rows, (micro + 1) * rows)
        total = pack[micro, :rows].astype(f32)
        for k in range(3):
            total = total + zs[k, micro].astype(f32)
        upstream, latent = total[:, :RANK], r["latent"][span]
        inv = rms_scale(latent)
        scaled = upstream * r["kgain"][...]
        inner = jnp.mean(scaled * latent, axis=-1, keepdims=True)
        kvd[span, :RANK] = (inv * scaled - latent * (inv * inv * inv) * inner).astype(bf16)
        kv_gain_grad = kv_gain_grad + jnp.sum(upstream * latent * inv, axis=0, keepdims=True)
        g1, g2 = total[:, RANK : RANK + HALF_ROPE], total[:, RANK + HALF_ROPE : RANK + ROPE]
        cosine, sine = r["cos"][:, :HALF_ROPE], r["sin"][:, :HALF_ROPE]
        kvd[span, RANK : RANK + HALF_ROPE] = (g1 * cosine + g2 * sine).astype(bf16)
        kvd[span, RANK + HALF_ROPE : RANK + ROPE] = (g2 * cosine - g1 * sine).astype(bf16)
        kvd[span, RANK + ROPE :] = jnp.zeros((rows, ROPE), bf16)
    sems.push(kvd, r["s_kvd"], swap["kvd"], place.peer)

    tile = 384
    tiles = [("kq", t * tile, tile) for t in range(qs.shape[1] // tile)]
    tiles += [("kkr", 0, tile), ("kkr", tile, r["kkr"].shape[0] - tile)]
    wide = ha.shape[1]
    half_w = wide // 2

    def fetch(t):
        name, start, n = tiles[t]
        return pltpu.make_async_copy(
            r[name].at[start : start + n],
            kvbs.at[:n, (t % 2) * wide : (t % 2 + 1) * wide],
            load.at[2 + t % 2],
        )

    fetch(0).start()
    for t, (name, start, n) in enumerate(tiles):
        fetch(t).wait()
        if t + 1 < len(tiles):
            fetch(t + 1).start()
        left = (qs if name == "kq" else kvd)[:, start : start + n]
        for half in (0, 1):
            base = (t % 2) * wide + half * half_w
            value = dot(left, kvbs[:n, base : base + half_w], 1, 0)
            where = slice(half * toks, (half + 1) * toks)
            if t == 0:
                acc[where] = value
            else:
                acc[where] += value
        if t % 2 == 1:
            pump.run(1)

    for k in (1, 2, 3):
        sems.arrived(r["zsh"].at[k - 1], shared_slots[k - 1], place.along(k))
    cols = r["gsh"].shape[2]
    for j in range(EARLY):
        copies = [pltpu.make_async_copy(r["gsh"].at[j, :ff], kvbs.at[:ff, :cols], load.at[6])]
        for k in range(3):
            copies.append(
                pltpu.make_async_copy(
                    r["zsh"].at[k, j], kvbs.at[:ff, (k + 1) * cols : (k + 2) * cols], load.at[7 + k]
                )
            )
        for copy in copies:
            copy.start()
        for copy in copies:
            copy.wait()
        add_rows(r["gshs"].at[j], [kvbs.at[:ff, k * cols : (k + 1) * cols] for k in range(4)])
    add_matrices("sh", r["gshs"], EARLY, r["osh"], "y", False)
    pump.run(2)

    sems.arrived(r["s_kvd"], swap["kvd"], place.peer)
    sems.arrived(r["s_rtr"], swap["rtr"], place.peer)
    sems.settle(kvb_push)
    half_kr = r["kkr"].shape[0] // 2
    r_kr, c_kr = half_kr // 4, wide // 4
    edges = sorted(set(list(range(0, 2 * half_kr + 1, 128)) + [half_kr]))
    for start, stop in zip(edges[:-1], edges[1:]):
        value = dot(kvd[:, start:stop], ha[...], 0, 0)
        value = value + dot(r["s_kvd"][:, start:stop], s_ha[...], 0, 0)
        n = start // half_kr
        if stop == 2 * half_kr:
            first = RANK + ROPE - start
            both = r["rtr"][...].astype(f32) + r["s_rtr"][...].astype(f32)
            value = jnp.concatenate([value[:first], both])
        dkvb[start - n * half_kr : stop - n * half_kr, n * wide : (n + 1) * wide] = value.astype(bf16)
    add_sharded(
        "kr",
        lambda s, k, chip: dkvb.at[rows16(chip * r_kr, r_kr), lanes(core * wide + s * c_kr, c_kr)],
        r["okr"],
        True,
        "x",
    )
    pump.run(2)

    again = r["again"][...]
    attn_gain_grad = jnp.zeros((1, wide), f32)
    step = 32
    for start in range(0, toks, step):
        fetched = [
            pltpu.make_async_copy(r[a].at[start : start + step], r[b], load.at[4 + n])
            for n, (a, b) in enumerate((("x", "xb"), ("mid", "mb")))
        ]
        for copy in fetched:
            copy.start()
        for copy in fetched:
            copy.wait()
        x = r["xb"][...].astype(f32)
        upstream = jnp.concatenate(
            [acc[start : start + step], acc[toks + start : toks + start + step]], axis=1
        )
        inv = rms_scale(x)
        scaled = upstream * again
        inner = jnp.mean(scaled * x, axis=-1, keepdims=True)
        part = inv * scaled - x * (inv * inv * inv) * inner
        r["ograd"][start : start + step] = (r["mb"][...] + part).astype(bf16)
        attn_gain_grad = attn_gain_grad + jnp.sum(upstream * x * inv, axis=0, keepdims=True)
    n_a, n_k = wide // 4, RANK // 4
    gains[...] = jnp.zeros(gains.shape, f32)
    for s in range(4):
        gains[s, 0:1, :n_a] = attn_gain_grad[:, s * n_a : (s + 1) * n_a]
        gains[s, 0:1, n_a : 2 * n_a] = r["fgain"][:, s * n_a : (s + 1) * n_a]
        gains[s, 0:1, 2 * n_a :] = kv_gain_grad[:, s * n_k : (s + 1) * n_k]
    gain_slots = [sems.slot() for _ in range(3 + 7)]
    gz, gp, gs = r["gz"], r["gp"], r["gs"]
    for k in (1, 2, 3):
        sems.push(gains.at[place.shard_at(k)], gz.at[k - 1], gain_slots[k - 1], place.along(k))
    pump.run(2)

    for k in (1, 2, 3):
        sems.arrived(gz.at[k - 1], gain_slots[k - 1], place.along(4 - k))
    gs[...] = gains[place.z] + gz[0] + gz[1] + gz[2]
    for n, device in enumerate(others):
        sems.push(gs, gp.at[n], gain_slots[3 + n], device)
    pump.end()
    total = gs[...]
    for n, device in enumerate(others):
        sems.arrived(gp.at[n], gain_slots[3 + n], device)
        total = total + gp[n]
    r["ogain"][...] = total
    sems.drain()


def back_all(args, scale):
    shape = jax.ShapeDtypeStruct
    gsh, gex, gout, q, kvb, kq, kkr = (args[n] for n in BACK_IN[:7])
    toks, wide = args["ha"].shape
    micros, length, rank = args["lat"].shape
    fe, ff = gex.shape[1], gsh.shape[1] // 4
    rows = toks // micros
    n_a = wide // 4
    gain_shape = (8, 2 * n_a + rank // 4)
    outs = dict(
        oq=shape((q.shape[1], wide // 4), bf16),
        okr=shape((kkr.shape[0], wide // 4), bf16),
        okvb=shape((rank // 4, kvb.shape[1]), bf16),
        oout=shape((gout.shape[0] // 4, wide), bf16),
        osh=shape((EARLY, ff, wide), bf16),
        osd=shape((ff, wide), bf16),
        oex=shape((gex.shape[0], fe, wide), bf16),
        zsh=shape((3, EARLY, ff, wide // 2), bf16),
        ogain=shape(gain_shape, f32),
        ograd=shape((toks, wide), bf16),
    )
    vm = pltpu.VMEM
    parts = dict(
        out=(gout.shape[0] // 4, wide // 8),
        sd=(ff, wide // 8),
        kvb=(rank // 4, kvb.shape[1] // 8),
        q=(q.shape[1] // 8, wide // 4),
        kr=(kkr.shape[0] // 8, wide // 4),
    )
    scratch = dict(
        qs=vm(q.shape, bf16),
        kvbs=vm(kvb.shape, bf16),
        kvg=vm((length, 2 * (NOPE + VDIM)), bf16),
        acc=vm((2 * toks, wide // 2), f32),
        dlat=vm((micros, length, rank), f32),
        dk1=vm((micros, length, GROUP_LANES), f32),
        dk2=vm((micros, length, GROUP_LANES), f32),
        dkvb=vm(kvb.shape, bf16),
        pack=vm((micros, length, rank + 2 * ROPE), bf16),
        zs=vm((3, micros, rows, rank + 2 * ROPE), bf16),
        kvd=vm((toks, rank + 2 * ROPE), bf16),
        s_ha=vm((toks, wide), bf16),
        s_q=vm((toks, q.shape[1] // 2), bf16),
        s_kvb=vm((rank, kvb.shape[1] // 2), bf16),
        s_kvd=vm((toks, rank + 2 * ROPE), bf16),
        s_rtr=vm(args["rtr"].shape, bf16),
        gq=vm((q.shape[1] // 2, wide), bf16),
        gshs=vm((EARLY, ff, wide // 2), bf16),
        xb=vm((32, wide), bf16),
        mb=vm((32, wide), f32),
        gains=vm((4,) + gain_shape, f32),
        gz=vm((3,) + gain_shape, f32),
        gp=vm((7,) + gain_shape, f32),
        gs=vm(gain_shape, f32),
        ring_ex=vm((4, 2, fe, wide // 8), bf16),
        ring_out=vm((4, 2) + parts["out"], bf16),
        got1_ex=vm((gex.shape[0], 2, fe, wide // 8), bf16),
        got2_ex=vm((gex.shape[0], fe, wide // 8), bf16),
        got1_sh=vm((EARLY, 2, ff, wide // 8), bf16),
        got2_sh=vm((EARLY, ff, wide // 8), bf16),
    )
    for name, part in parts.items():
        scratch["got1_" + name] = vm((4, 2) + part, bf16)
        scratch["got2_" + name] = vm((4,) + part, bf16)
        scratch["got3_" + name] = vm((3,) + part, bf16)
    dma = pltpu.SemaphoreType.DMA
    scratch.update(
        send=dma((BACK_SLOTS,)), recv=dma((BACK_SLOTS,)), load=dma((10,)), keep=dma((8,)), ringsem=dma((4, 2))
    )
    names = (*BACK_IN, *BACK_OUT, *scratch)
    hbm, vmem = pl.BlockSpec(memory_space=HBM), pl.BlockSpec(memory_space=pltpu.VMEM)
    res = pl.pallas_call(
        functools.partial(back_kernel, scale, names),
        in_specs=[hbm] * BACK_HBM + [vmem] * (len(BACK_IN) - BACK_HBM),
        out_specs=[hbm if n not in ("ogain", "ograd") else vmem for n in BACK_OUT],
        out_shape=[outs[n] for n in BACK_OUT],
        scratch_shapes=list(scratch.values()),
        compiler_params=pltpu.CompilerParams(
            collective_id=1, has_side_effects=True, vmem_limit_bytes=61 << 20
        ),
        name="back_all",
    )(*(args[n] for n in BACK_IN))
    return dict(zip(BACK_OUT, res))


def head_split(weight):
    per_head = weight.reshape(HEADS, NOPE + ROPE, weight.shape[1])
    cuts = (0, NOPE, NOPE + HALF_ROPE, NOPE + ROPE)
    return jnp.concatenate(
        [per_head[:, a:b].reshape(-1, weight.shape[1]) for a, b in zip(cuts[:-1], cuts[1:])]
    )


def head_join(weight):
    cols = weight.shape[1]
    nope = weight[: HEADS * NOPE].reshape(HEADS, NOPE, cols)
    first = weight[HEADS * NOPE : HEADS * (NOPE + HALF_ROPE)].reshape(HEADS, HALF_ROPE, cols)
    second = weight[HEADS * (NOPE + HALF_ROPE) :].reshape(HEADS, HALF_ROPE, cols)
    return jnp.concatenate([nope, first, second], axis=1).reshape(-1, cols)


def shards(
    tokens,
    attn_gain,
    q_weight,
    kva_weight,
    kv_gain,
    kvb_weight,
    out_weight,
    ffn_gain,
    router_weight,
    shared_gate,
    shared_up,
    shared_down,
    expert_gate,
    expert_up,
    expert_down,
    expert_ids,
    cotangent,
):
    shard_count = lax.axis_size("shard")
    shard_index = lax.axis_index("shard")
    core = lax.axis_index("rep") % 2
    fast = lax.axis_size("rep") == 8 and shard_count == 4
    micros, rows, width = tokens.shape
    toks = micros * rows
    scale = (NOPE + ROPE) ** (-0.5)
    ga, gk = attn_gain.shape[0], kv_gain.shape[0]

    gain_pack = jnp.concatenate([attn_gain, ffn_gain, kv_gain]).astype(bf16)
    gain_pack = jnp.broadcast_to(gain_pack[None], (16, gain_pack.shape[0]))
    sh_own = jnp.stack([shared_gate, shared_up, shared_down]).astype(bf16)
    query_mat, kr_mat, kvb_mat, out_mat, sh_rest, gains = gather_weights(
        head_split(q_weight).astype(bf16),
        jnp.concatenate([kva_weight, router_weight]).astype(bf16),
        kvb_weight.astype(bf16),
        out_weight.astype(bf16),
        sh_own,
        gain_pack,
        fast,
    )
    gain_rows = gains[:, 0].astype(f32)
    attn_gain_f = gain_rows[:, :ga].reshape(-1)
    ffn_gain_f = gain_rows[:, ga : 2 * ga].reshape(-1)
    kv_gain_f = gain_rows[:, 2 * ga :].reshape(-1)
    kv_down_mat, router_mat = kr_mat[: RANK + ROPE], kr_mat[RANK + ROPE :]
    sh_mats = [sh_own, sh_rest] if fast else [sh_rest]

    def hidden(t, index):
        return jnp.concatenate([dot(t, m[index], 1, 1) for m in sh_mats], axis=1)

    def unhidden(t, index):
        at, total = 0, 0.0
        for m in sh_mats:
            total = total + dot(t[:, at : at + m.shape[1]], m[index], 1, 0)
            at += m.shape[1]
        return total


    x_in = tokens.reshape(toks, width).astype(f32)
    inv_one = rms_scale(x_in)
    h_attn = (x_in * inv_one * attn_gain_f).astype(bf16)
    positions = (shard_index * rows + jnp.arange(rows, dtype=jnp.int32)).astype(f32)
    frequency = jnp.exp(
        -jnp.log(rope_base) * (2.0 * jnp.arange(HALF_ROPE, dtype=f32) / ROPE)
    )
    angles = positions[:, None] * frequency[None, :]
    cosine = jnp.tile(jnp.cos(angles), (micros, 1))
    sine = jnp.tile(jnp.sin(angles), (micros, 1))
    cos_all, sin_all = jnp.tile(cosine, (1, HEADS)), jnp.tile(sine, (1, HEADS))
    q_raw = dot(h_attn, query_mat, 1, 1)
    n1, n2 = HEADS * NOPE, HEADS * (NOPE + HALF_ROPE)
    q_first, q_second = q_raw[:, n1:n2], q_raw[:, n2:]
    by_micro = lambda t: t.reshape(micros, rows, t.shape[-1])
    qn = by_micro(q_raw[:, :n1].astype(bf16))
    q1 = by_micro((q_first * cos_all - q_second * sin_all).astype(bf16))
    q2 = by_micro((q_second * cos_all + q_first * sin_all).astype(bf16))
    kv_down = dot(h_attn, kv_down_mat, 1, 1)
    latent = kv_down[:, :RANK]
    inv_kv = rms_scale(latent)
    latent_norm = (latent * inv_kv * kv_gain_f).astype(bf16)
    k_first, k_second = kv_down[:, RANK : RANK + HALF_ROPE], kv_down[:, RANK + HALF_ROPE :]
    latent_pack = jnp.concatenate(
        [
            latent_norm,
            (k_first * cosine - k_second * sine).astype(bf16),
            (k_second * cosine + k_first * sine).astype(bf16),
            jnp.zeros((toks, ROPE), bf16),
        ],
        axis=-1,
    )
    packs = z_all(by_micro(latent_pack), fast)
    length = packs.shape[1]
    lat_all = packs[..., :RANK]
    k1 = jnp.tile(packs[..., RANK : RANK + HALF_ROPE], (1, 1, HEAD_GROUP))
    k2 = jnp.tile(packs[..., RANK + HALF_ROPE : RANK + ROPE], (1, 1, HEAD_GROUP))
    key_shard = jnp.arange(length, dtype=jnp.int32) // rows
    if fast:
        key_shard = (shard_index - key_shard) % 4
    key_block = (key_shard * rows + jnp.arange(length, dtype=jnp.int32) % rows) // MASK_BLOCK
    seen = (key_block <= (shard_index * rows) // MASK_BLOCK).astype(f32).reshape(1, length)
    attended = attend(seen, qn, q1, q2, lat_all, k1, k2, kvb_mat, scale).reshape(toks, -1)

    x_mid = x_in + dot(attended, out_mat, 1, 0)
    inv_two = rms_scale(x_mid)
    h_ffn = (x_mid * inv_two * ffn_gain_f).astype(bf16)
    router_probs = jax.nn.softmax(dot(h_ffn, router_mat, 1, 1), axis=-1)
    grad_b = cotangent.reshape(toks, width)

    member = jnp.any(
        expert_ids[:, :, None, :] == jnp.arange(EXP_WIN, dtype=jnp.int32)[None, None, :, None], axis=-1
    ).astype(jnp.int32)
    placed = jnp.cumsum(member, axis=1) - 1
    hits = (member[:, :, :, None] == 1) & (
        placed[:, :, :, None] == jnp.arange(CAP, dtype=jnp.int32)
    )
    select = jnp.transpose(hits, (2, 0, 3, 1)).astype(f32)
    select_b = select.astype(bf16)
    h3, c3 = by_micro(h_ffn), by_micro(grad_b)
    gather_slots = lambda t: jnp.einsum(
        "emct,mtd->emcd", select_b, t, preferred_element_type=f32
    ).astype(bf16)
    flat = lambda t: t.reshape(EXP_WIN, micros * CAP, t.shape[-1])
    tall = lambda t: t.reshape(-1, t.shape[-1])
    picked_all = z_all(flat(gather_slots(c3)), fast)
    rows_all = z_all(flat(gather_slots(h3)), fast)

    gate_pre, up_pre = hidden(h_ffn, 0), hidden(h_ffn, 1)
    shared_hidden = (jax.nn.silu(gate_pre) * up_pre).astype(bf16)
    shared_hidden_grad = hidden(grad_b, 2)
    gate_grad_b, up_grad_b = swiglu_back(gate_pre, up_pre, shared_hidden_grad)
    sh_s, hf_s, cot_s = core_swap(
        [jnp.concatenate([gate_grad_b, up_grad_b, shared_hidden], axis=1), h_ffn, grad_b],
        (None, 1, 1),
        fast,
        7,
    )
    ff = shared_hidden.shape[1]
    sh_s, hf_s, cot_s = tall(sh_s), tall(hf_s), tall(cot_s)
    grad_sh = jnp.stack(
        [
            dot(sh_s[:, :ff], hf_s, 0, 0).astype(bf16),
            dot(sh_s[:, ff : 2 * ff], hf_s, 0, 0).astype(bf16),
            dot(sh_s[:, 2 * ff :], cot_s, 0, 0).astype(bf16),
        ]
    )
    picked_all = picked_all.astype(f32)
    slot_probs = jax.nn.softmax(
        jnp.einsum("end,xd->enx", rows_all, router_mat, preferred_element_type=f32), axis=-1
    )
    gates_all = jnp.stack([slot_probs[e, :, e] for e in range(EXP_WIN)])[..., None]
    dy_all = (gates_all * picked_all).astype(bf16)
    eg, eu, ed = expert_gate.astype(bf16), expert_up.astype(bf16), expert_down.astype(bf16)
    bdot = lambda a, b, ca, cb: lax.dot_general(
        a, b, (((ca,), (cb,)), ((0,), (0,))), preferred_element_type=f32
    )
    expert_pre = bdot(rows_all, eg, 2, 2)
    expert_upv = bdot(rows_all, eu, 2, 2)
    expert_hidden = (jax.nn.silu(expert_pre) * expert_upv).astype(bf16)
    expert_part = bdot(expert_hidden, ed, 2, 1)
    gate_part = jnp.sum(picked_all * expert_part, axis=-1, keepdims=True)
    gate_high = gate_part.astype(bf16)
    gate_low = (gate_part - gate_high.astype(f32)).astype(bf16)
    expert_hidden_grad = bdot(dy_all, ed, 2, 2)
    expert_gate_b, expert_up_b = swiglu_back(expert_pre, expert_upv, expert_hidden_grad)
    slot_part = (bdot(expert_gate_b, eg, 2, 1) + bdot(expert_up_b, eu, 2, 1)).astype(bf16)
    slot_part = jnp.concatenate(
        [slot_part, gate_high, gate_low, jnp.zeros(slot_part.shape[:2] + (126,), bf16)], axis=-1
    )
    slot_back = z_home(slot_part, fast)
    expert_back = z_home(expert_part.astype(bf16), fast)

    ex_s, row_s, dy_s = core_swap(
        [
            tall(jnp.concatenate([expert_gate_b, expert_up_b, expert_hidden], axis=-1)),
            tall(rows_all),
            tall(dy_all),
        ],
        (None, 1, 1),
        fast,
        8,
    )
    fe = expert_hidden.shape[-1]
    by_expert = lambda t: t.reshape(2, EXP_WIN, -1, t.shape[-1])
    ex_s, row_s, dy_s = by_expert(ex_s), by_expert(row_s), by_expert(dy_s)
    edot = lambda a, b: jnp.einsum("senf,send->efd", a, b, preferred_element_type=f32).astype(bf16)
    grad_ex = jnp.concatenate(
        [
            edot(ex_s[..., :fe], row_s),
            edot(ex_s[..., fe : 2 * fe], row_s),
            edot(ex_s[..., 2 * fe :], dy_s),
        ]
    )
    ffn_grad = unhidden(gate_grad_b, 0) + unhidden(up_grad_b, 1)
    back = lambda t: t.reshape(EXP_WIN, micros, CAP, t.shape[-1])
    slot_grad = back(slot_back[..., :width])
    gate_weight_grad = back(slot_back[..., width : width + 2]).sum(axis=-1)
    ffn_grad = ffn_grad + jnp.einsum(
        "emct,emcd->mtd", select, slot_grad, precision=highest
    ).reshape(toks, width)
    probs_grad = jnp.einsum("emct,emc->mte", select, gate_weight_grad, precision=highest)
    probs_grad = jnp.pad(
        probs_grad.reshape(toks, EXP_WIN), ((0, 0), (0, EXPERTS - EXP_WIN))
    )
    logit_grad = (
        router_probs * (probs_grad - jnp.sum(router_probs * probs_grad, axis=-1, keepdims=True))
    ).astype(bf16)
    ffn_grad = ffn_grad + dot(logit_grad, router_mat, 1, 0)
    mid_part, ffn_gain_grad = norm_back(x_mid, inv_two, ffn_gain_f, ffn_grad)
    mid_grad = grad_b.astype(f32) + mid_part
    attn_out_grad = mid_grad.astype(bf16)
    attended_grad = by_micro(dot(attn_out_grad, out_mat, 1, 1).astype(bf16))

    att_s, og_s = core_swap([attended, attn_out_grad], (None, 1), fast, 2)
    grad_out = dot(tall(att_s), tall(og_s), 0, 0).astype(bf16)
    expert_out = back(expert_back)
    slot_gates = jnp.einsum(
        "emct,mte->emc", select, by_micro(router_probs)[..., :EXP_WIN], precision=highest
    )
    routed = jnp.einsum("emct,emcd->mtd", select, slot_gates[..., None] * expert_out, precision=highest)
    layer_output = x_mid + unhidden(shared_hidden, 2) + routed.reshape(toks, width)
    layer_output = layer_output.astype(bf16)

    lane_rows = lambda t: t.reshape(shard_count, -1)
    if fast:
        row = lambda t: t.reshape(1, -1)
        group_tab = lambda t: jnp.tile(t[:rows], (1, HEAD_GROUP))
        res = back_all(
            dict(
                gsh=grad_sh,
                gex=grad_ex,
                gout=grad_out,
                q=jnp.concatenate([t.reshape(toks, -1) for t in (qn, q1, q2)], axis=1),
                kvb=kvb_mat,
                kq=query_mat,
                kkr=kr_mat,
                x=tokens.reshape(toks, width),
                mid=mid_grad,
                lat=lat_all,
                k1=k1,
                k2=k2,
                seen=seen,
                do=attended_grad,
                ha=h_attn,
                latent=latent,
                kgain=row(kv_gain_f),
                again=row(attn_gain_f),
                fgain=row(ffn_gain_grad),
                cos=group_tab(cosine),
                sin=group_tab(sine),
                rtr=dot(logit_grad, h_ffn, 0, 0).astype(bf16),
            ),
            scale,
        )
        gq, gkr, gkvb, gout = (res[n] for n in ("oq", "okr", "okvb", "oout"))
        gsh = (res["osh"][0], res["osh"][1], res["osd"])
        gex, gg = res["oex"], res["ogain"][0]
        input_grad = res["ograd"]
    else:
        dqn, dq1, dq2, dlat, dk1, dk2, dkvb = attend_back(
            seen, qn, q1, q2, lat_all, k1, k2, kvb_mat, attended_grad, scale
        )
        fold = lambda t: jnp.sum(t.reshape(micros, length, HEAD_GROUP, HALF_ROPE), axis=2)
        back_pack = jnp.concatenate(
            [dlat, fold(dk1), fold(dk2), jnp.zeros((micros, length, ROPE), f32)], axis=-1
        ).astype(bf16)
        own_back = z_home(back_pack, fast).reshape(toks, -1)
        latent_grad, kv_gain_grad = norm_back(latent, inv_kv, kv_gain_f, own_back[:, :RANK])
        g1, g2 = own_back[:, RANK : RANK + HALF_ROPE], own_back[:, RANK + HALF_ROPE : RANK + ROPE]
        kv_down_grad = jnp.concatenate(
            [latent_grad, g1 * cosine + g2 * sine, g2 * cosine - g1 * sine], axis=-1
        ).astype(bf16)
        dq1, dq2 = dq1.reshape(toks, -1), dq2.reshape(toks, -1)
        q_raw_grad = jnp.concatenate(
            [
                dqn.reshape(toks, -1),
                (dq1 * cos_all + dq2 * sin_all).astype(bf16),
                (dq2 * cos_all - dq1 * sin_all).astype(bf16),
            ],
            axis=-1,
        )
        attn_in_grad = dot(q_raw_grad, query_mat, 1, 0) + dot(kv_down_grad, kv_down_mat, 1, 0)
        x_part, attn_gain_grad = norm_back(x_in, inv_one, attn_gain_f, attn_in_grad)
        input_grad = (mid_grad + x_part).astype(bf16)

        kr_grad = jnp.concatenate(
            [dot(kv_down_grad, h_attn, 0, 0), dot(logit_grad, h_ffn, 0, 0)]
        ).astype(bf16)
        h_s, qg_s, krg_s, kvbg_s = core_swap(
            [h_attn, q_raw_grad, kr_grad, dkvb], (None, 1, 0, 1), fast, 6
        )
        grad_q = dot(tall(qg_s), tall(h_s), 0, 0).astype(bf16)
        grad_kr = (krg_s[0].astype(f32) + krg_s[1].astype(f32)).astype(bf16)
        grad_kvb = (kvbg_s[0].astype(f32) + kvbg_s[1].astype(f32)).astype(bf16)
        gain_grad = jnp.concatenate(
            [lane_rows(attn_gain_grad), lane_rows(ffn_gain_grad), lane_rows(kv_gain_grad)], axis=1
        )
        gain_len = gain_grad.shape[1]
        gain_grad = jnp.pad(gain_grad, ((0, 0), (0, 16 * 128 - gain_len))).reshape(-1, 16, 128)
        gq, gkr, gkvb, gout, gsh, gex, gg = reduce_anywhere(
            grad_q, grad_kr, grad_kvb, grad_out, grad_sh, grad_ex, gain_grad
        )
        gg = gg.reshape(-1)
    wide = lambda t: t.astype(f32)
    return (
        by_micro(layer_output),
        by_micro(input_grad),
        gg[:ga],
        wide(head_join(gq)),
        wide(gkr[: RANK + ROPE]),
        gg[2 * ga : 2 * ga + gk],
        wide(gkvb),
        wide(gout),
        gg[ga : 2 * ga],
        wide(gkr[RANK + ROPE :]),
        wide(gsh[0]),
        wide(gsh[1]),
        wide(gsh[2]),
        wide(gex[:2]),
        wide(gex[2:4]),
        wide(gex[4:]),
    )


def solution(mesh):
    token_spec = P(None, ("rep", "shard"), None)
    row_spec, col_spec, gain_spec = P("shard", None), P(None, "shard"), P("shard")
    expert_spec = P(None, "shard", None)
    weight_specs = (
        gain_spec,
        col_spec,
        col_spec,
        gain_spec,
        row_spec,
        row_spec,
        gain_spec,
        col_spec,
        row_spec,
        row_spec,
        row_spec,
        expert_spec,
        expert_spec,
        expert_spec,
    )
    return jax.shard_map(
        shards,
        mesh=mesh,
        in_specs=(token_spec,) + weight_specs + (token_spec, token_spec),
        out_specs=(token_spec, token_spec) + weight_specs,
        check_vma=False,
    )
```

time: 1510 us -> 840 us (0.56)
  Pallas kernels: 1260 us -> 521 us
  waiting for transfers between devices: 0 us -> 45.6 us
  starting transfers between devices: 0 us -> 22.8 us
  matrix products: 108 us -> 89.3 us
    pallas_call x7 -> x4, Pallas kernels: 895 us -> 370 us  [the longest x1 354 us: back_all(): pl.pallas_call(functools.partial(back_kernel, scale, names), in_specs=[hb...]
    pallas_call x1, Pallas kernels: 348 us -> 131 us  [gather_weights(): pl.pallas_call(gather_kernel, in_specs=[pl.BlockSpec(memory_space=HBM)] *...]
    ppermute x0 -> x15, waiting for transfers between devices: none -> 45.6 us  [along_z(): lax.ppermute(tensor, 'shard', [(i, (i + step) % 4) for i in range(4)])]
    dot_general x21 -> x23, matrix products: 84.1 us -> 53.7 us  [dot(): lax.dot_general(a, b, (((ca,), (cb,)), ((), ())), preferred_element_type=...]
    ppermute x0 -> x15, starting transfers between devices: none -> 22.8 us  [along_z(): lax.ppermute(tensor, 'shard', [(i, (i + step) % 4) for i in range(4)])]
    convert_element_type x8 -> x13, other arithmetic: 14.5 us -> 33.6 us  [the longest x8 27.4 us: shards(): wide = lambda t: t.astype(f32)]
    another operation x22 -> x9, other arithmetic: 20.5 us -> 4.49 us  [the longest x10 11.2 us: halves(): jnp.stack([lax.slice_in_dim(tensor, 0, size, axis=axis), lax.slice_in_dim...]
  transfers between devices with their start and end apart: 0 -> 16, of which waited for: 0 -> 9; matrix products, arithmetic and copies ran while one was open for 0% -> 13% of each run, Pallas kernels for 0% -> 3%
where the time goes in v2:
time: 840 us; the launch traced here: 827 us
  Pallas kernels  521 us (62%)
  matrix products  89.3 us (11%)
  local copies, waits for them, and re-layouts  66.7 us (8%)
  other arithmetic  66 us (8%)
  waiting for transfers between devices  45.6 us (5%)
  starting transfers between devices  22.8 us (3%)
  between operations  15.7 us (2%)
    pallas_call x1, Pallas kernels, back_all(): pl.pallas_call(functools.partial(back_kernel, scale, names), in_specs=[hb...  354 us
    pallas_call x1, Pallas kernels, gather_weights(): pl.pallas_call(gather_kernel, in_specs=[pl.BlockSpec(memory_space=HBM)] *...  131 us
    dot_general x23, matrix products, dot(): lax.dot_general(a, b, (((ca,), (cb,)), ((), ())), preferred_element_type=...  53.7 us
    ppermute x15, waiting for transfers between devices, along_z(): lax.ppermute(tensor, 'shard', [(i, (i + step) % 4) for i in range(4)])  45.6 us
    unnamed x164, local copies, waits for them, and re-layouts  29 us
    convert_element_type x8, other arithmetic, shards(): wide = lambda t: t.astype(f32)  27.4 us
    dot_general x6, matrix products, shards(): lax.dot_general(a, b, (((ca,), (cb,)), ((0,), (0,))), preferred_element_t...  23 us
    ppermute x15, starting transfers between devices, along_z(): lax.ppermute(tensor, 'shard', [(i, (i + step) % 4) for i in range(4)])  22.8 us
  transfers between devices with their start and end apart: 16, of which 9 were waited for; matrix products, arithmetic and copies ran while one was open for 13% of the time, Pallas kernels for 3%

profile of v2, /device:TPU:9, one launch (start us, length us, event | category | flops | bytes accessed | tf_op | source)
XLA Modules:
  0.0 827.3 jit_solution(7478432518941379531)
XLA Ops:
  7.2 3.2 convert.47
  14.1 2.0 copy-done.29
  20.1 130.7 %gather_weights.1 = (bf16[3072,2048]{1,0:T(8,128)(2,1)}, bf16[640,2048]{1,0:T(8,128)(2,1)S(1)}, bf16[512,4096]{1,0:T(8,128)(2,1)S(1)}, bf16[2048,2048]{1,0:T(8,1...) custom-call(bf16[3072,512]{1,0:T(8,128)(2,1)S(1)} %pad_maximum_fusion.3.refs_0_, ...), custom_call_target="tpu_custom_call" | custom-call | tf_op jit(solution)/shard_map/gather_weights/pallas_call | solution.py:537
  150.9 2.0 copy-done
  155.9 1.7 collective-permute-start.11
  157.6 2.1 collective-permute-start.10
  159.7 2.3 collective-permute-start.9
  172.5 6.5 fusion.116
  184.5 2.3 collective-permute-start
  189.5 6.8 collective-permute-done.9
  196.4 2.7 maximum_convert_fusion
  199.1 2.9 collective-permute-done.2
  203.5 7.0 collective-permute-done
  213.5 2.2 pad_maximum_fusion.14
  219.6 1.8 copy.154.k2_ref.refs_11_
  224.2 20.8 %attend.1 = bf16[2,128,2048]{2,1,0:T(8,128)(2,1)S(1)} custom-call(f32[1,512]{1,0:T(1,128)S(1)} %compare_convert_fusion.seen_ref.refs_12_, bf16[2,128,2048]{2,1,0:T(8,128)(2,1)S(1)} %bitcast.221, bf16[2,128,512]{2,1,0:T(8,128)(2,1)S(1)} %bitcast.227, bf16[2,128,512]{2,1,0:T(8,128)(2,1)S(1)} %bitcast.226, bf16[2,512,512]{2,1,0:T(8,128)(2,1)S(1)} %slice.283.lat_ref.refs_9_, ...), custom_call_target="tpu_custom_call" | custom-call | tf_op jit(solution)/shard_map/attend/pallas_call | solution.py:183
  245.1 6.2 multiply_reduce_fusion.3
  252.8 3.4 collective-permute-start.4
  262.2 7.3 collective-permute-done.4
  269.5 5.6 collective-permute-done.3
  275.2 2.6 fusion.112
  279.2 3.5 fusion.25
  282.8 3.7 fusion.29
  286.5 4.8 multiply_convert_fusion.7
  291.3 3.1 multiply_reduce_fusion.2
  297.7 1.9 pad_maximum_fusion.13
  299.6 2.1 copy.167
  301.7 2.0 fusion.108
  303.7 4.0 collective-permute-start.6
  308.1 2.1 collective-permute-start.7
  310.2 3.5 fusion.27
  313.7 4.5 fusion.8
  318.8 3.1 concatenate.68
  324.7 1.8 fusion.16.refs_2_
  326.5 5.6 core_swap.4
  334.2 2.3 pad_maximum_fusion.2.refs_1_
  336.5 2.2 collective-permute-start.13
  340.0 7.1 collective-permute-done.12
  348.5 6.0 collective-permute-done.13
  358.4 2.1 fusion.66
  363.5 1.8 convolution_convert_fusion.4.refs_21_
  365.3 3.0 fusion.45
  368.4 3.0 fusion.47
  371.4 5.6 fusion.103
  384.4 2.9 fusion.43
  389.1 1.6 copy-done.20
  394.8 2.6 multiply_reduce_fusion
  397.5 2.0 fusion.101
  399.5 3.6 convolution_convert_fusion.3
  403.1 3.6 core_swap.5
  406.7 5.9 core_swap.3
  412.6 1.7 fusion.2
  414.2 1.7 fusion.1
  415.9 1.7 fusion.3
  417.6 4.4 bitcast_convert_fusion.refs_2_
  422.0 4.4 pad_maximum_fusion.refs_0_
  426.5 354.5 %back_all.1 = (bf16[3072,512]{1,0:T(8,128)(2,1)}, bf16[640,512]{1,0:T(8,128)(2,1)}, bf16[128,4096]{1,0:T(8,128)(2,1)}, bf16[512,2048]{1,0:T(8,128)(2,1)}, bf16[2...) custom-call(bf16[3,1408,1024]{2,1,0:T(8,128)(2,1)} %pad_maximum_fusi, ...), custom_call_target="tpu_custom_call" | custom-call | tf_op jit(solution)/shard_map/back_all/pallas_call | solution.py:1306
  785.1 2.2 slice_convert_fusion.4
  791.4 1.9 convert_element_type.360
  793.6 3.8 bitcast_convert_fusion.1
  797.4 2.5 convert_element_type.354
  800.1 3.3 bitcast_convert_fusion.5
  803.4 10.6 %slice_convert_fusion = (f32[2,352,2048]{2,1,0:T(8,128)}, f32[2,352,2048]{2,1,0:T(8,128)}, f32[2,352,2048]{2,1,0:T(8,128)}) fusion(bf16[6,352,2048]{2,1,0:T(8,128)(2,1)} %get-tuple-element.61), kind=kLoop, calls=%fused_computation.17 | loop fusion | flops 4325376 | bytes 25952256 | tf_op jit(solution)/shard_map/convert_element_type | solution.py:1638
  814.0 5.0 fusion.9
  (296 shorter events, 90.6 us)
Async XLA Ops:
  7.2 364.2 %all-gather.2.cloned.1.call-start = ((), (), s32[]{:S(2)}) async-start(), calls=%async_computation | async-start | bytes 14598144 | tf_op jit(solution)/shard_map/all_gather | solution.py:560
  10.6 2.0 copy-start.38
  11.9 2.0 copy-start.18
  13.9 2.2 copy-start.29
  16.1 1.8 copy-start.21
  16.1 2.7 copy-start.24
  20.1 134.3 %copy-start.69 = (s32[2,128,6]{1,0,2:T(2,128)S(1)}, s32[2,128,6]{1,0,2:T(2,128)}, u32[]{:S(2)}) copy-start(s32[2,128,6]{1,0,2:T(2,128)} %param.32) | copy-start | bytes 18436
  150.9 2.0 copy-start
  154.4 10.0 %copy-start.26 = (bf16[2,128,2048]{2,1,0:T(8,128)(2,1)S(1)}, bf16[2,128,2048]{2,1,0:T(8,128)(2,1)}, u32[]{:S(2)}) copy-start(bf16[2,128,2048]{2,1,0:T(8,128)(2,1)} %param.17) | copy-start | bytes 3145732
  154.4 10.2 %copy-start.63 = (pred[2,2,128]{2,0,1:T(4,128)(4,1)}, pred[2,2,128]{2,0,1:T(4,128)(4,1)S(1)}, u32[]{:S(2)}) copy-start(pred[2,2,128]{2,0,1:T(4,128)(4,1)S(1)} %get-tuple-element.120) | copy-start | bytes 1540
  154.9 9.8 %copy-start.59 = (s32[2,2,128]{2,0,1:T(2,128)}, s32[2,2,128]{2,0,1:T(2,128)S(1)}, u32[]{:S(2)}) copy-start(s32[2,2,128]{2,0,1:T(2,128)S(1)} %copy.161) | copy-start | bytes 6148
  155.9 40.5 %copy-start.33 = (bf16[2,2,16,2048]{3,2,1,0:T(8,128)(2,1)}, bf16[2,2,16,2048]{3,2,1,0:T(8,128)(2,1)S(1)}, u32[]{:S(2)}) copy-start(bf16[2,2,16,2048]{3,2,1,0:T(8,128)(2,1)S(1)} %copy.166) | copy-start | bytes 786436
  155.9 28.6 %collective-permute-start.11 = (bf16[2,32,2048]{2,1,0:T(8,128)(2,1)S(1)}, bf16[2,32,2048]{2,1,0:T(8,128)(2,1)}, u32[]{:S(2)}, u32[]{:S(2)}) collective-permute-start(bf16[2,32,2048]{2,1,0:T(8,128)(2,1)S(1)} %bitcast.253), channel_id=1, source_target_pairs={{0,3},{1,0},{2,1},{3,2},{4,7},{5,4},{6,5},{7,6},{8,11},{9,8},{10,9... | collective-permute-start | bytes 786440 | tf_op jit(solution)/shard_map/ppermute | solution.py:565
  157.6 31.9 %collective-permute-start.10 = (bf16[2,32,2048]{2,1,0:T(8,128)(2,1)S(1)}, bf16[2,32,2048]{2,1,0:T(8,128)(2,1)}, u32[]{:S(2)}, u32[]{:S(2)}) collective-permute-start(bf16[2,32,2048]{2,1,0:T(8,128)(2,1)S(1)} %bitcast.254), channel_id=1, source_target_pairs={{0,2},{1,3},{2,0},{3,1},{4,6},{5,7},{6,4},{7,5},{8,10},{9,11},{10,... | collective-permute-start | bytes 786440 | tf_op jit(solution)/shard_map/ppermute | solution.py:565
  159.7 36.7 %collective-permute-start.9 = (bf16[2,32,2048]{2,1,0:T(8,128)(2,1)S(1)}, bf16[2,32,2048]{2,1,0:T(8,128)(2,1)}, u32[]{:S(2)}, u32[]{:S(2)}) collective-permute-start(bf16[2,32,2048]{2,1,0:T(8,128)(2,1)S(1)} %bitcast.255), channel_id=1, source_target_pairs={{0,1},{1,2},{2,3},{3,0},{4,5},{5,6},{6,7},{7,4},{8,9},{9,10},{10,1... | collective-permute-start | bytes 786440 | tf_op jit(solution)/shard_map/ppermute | solution.py:565
  162.1 2.5 copy-start.53
  162.1 2.5 copy-start.55
  163.6 2.1 copy-start.4
  165.0 7.5 copy-start.30
  169.4 32.6 %collective-permute-start.2 = (bf16[2,128,640]{2,1,0:T(8,128)(2,1)}, bf16[2,128,640]{2,1,0:T(8,128)(2,1)}, u32[]{:S(2)}, u32[]{:S(2)}) collective-permute-start(bf16[2,128,640]{2,1,0:T(8,128)(2,1)} %bitcast.17), channel_id=1, source_target_pairs={{0,3},{1,0},{2,1},{3,2},{4,7},{5,4},{6,5},{7,6},{8,11},{9,8},{10,9... | collective-permute-start | bytes 983048 | tf_op jit(solution)/shard_map/ppermute | solution.py:565
  169.4 34.1 %collective-permute-start.1 = (bf16[2,128,640]{2,1,0:T(8,128)(2,1)}, bf16[2,128,640]{2,1,0:T(8,128)(2,1)}, u32[]{:S(2)}, u32[]{:S(2)}) collective-permute-start(bf16[2,128,640]{2,1,0:T(8,128)(2,1)} %bitcast.17), channel_id=1, source_target_pairs={{0,2},{1,3},{2,0},{3,1},{4,6},{5,7},{6,4},{7,5},{8,10},{9,11},{10,... | collective-permute-start | bytes 983048 | tf_op jit(solution)/shard_map/ppermute | solution.py:565
  180.4 2.6 copy-start.25
  183.0 3.8 copy-start.56
  183.0 4.6 copy-start.54
  183.0 5.3 copy-start.62
  183.0 5.9 copy-start.61
  184.5 26.0 %collective-permute-start = (bf16[2,128,640]{2,1,0:T(8,128)(2,1)}, bf16[2,128,640]{2,1,0:T(8,128)(2,1)S(1)}, u32[]{:S(2)}, u32[]{:S(2)}) collective-permute-start(bf16[2,128,640]{2,1,0:T(8,128)(2,1)} %bitcast.17), channel_id=1, source_target_pairs={{0,1},{1,2},{2,3},{3,0},{4,5},{5,6},{6,7},{7,4},{8,9},{9,10},{10,1... | collective-permute-start | bytes 983048 | tf_op jit(solution)/shard_map/ppermute | solution.py:565
  186.8 34.6 %copy-start.14 = (f32[1,512]{1,0:T(1,128)}, f32[1,512]{1,0:T(1,128)S(1)}, u32[]{:S(2)}) copy-start(f32[1,512]{1,0:T(1,128)S(1)} %compare_convert_fusion.seen_ref.refs_12_) | copy-start | bytes 6148
  213.5 7.9 copy-start.2
  218.8 26.2 %copy-start.7 = (bf16[2,512,128]{2,1,0:T(8,128)(2,1)}, bf16[2,512,128]{2,1,0:T(8,128)(2,1)S(1)}, u32[]{:S(2)}) copy-start(bf16[2,512,128]{2,1,0:T(8,128)(2,1)S(1)} %copy.153.k1_ref.refs_10_) | copy-start | bytes 786436
  224.2 20.8 %copy-start.27 = (bf16[2,128,2048]{2,1,0:T(8,128)(2,1)S(1)}, bf16[2,128,2048]{2,1,0:T(8,128)(2,1)}, u32[]{:S(2)}) copy-start(bf16[2,128,2048]{2,1,0:T(8,128)(2,1)} %param.17) | copy-start | bytes 3145732
  245.1 6.3 copy-start.5
  245.1 6.9 copy-start.58
  252.2 6.6 copy-start.22
  252.7 9.5 %collective-permute-start.5 = (bf16[2,32,2048]{2,1,0:T(8,128)(2,1)S(1)}, bf16[2,32,2048]{2,1,0:T(8,128)(2,1)S(1)}, u32[]{:S(2)}, u32[]{:S(2)}) collective-permute-start(bf16[2,32,2048]{2,1,0:T(8,128)(2,1)S(1)} %bitcast.272), channel_id=1, source_target_pairs={{0,3},{1,0},{2,1},{3,2},{4,7},{5,4},{6,5},{7,6},{8,11},{9,8},{10,9... | collective-permute-start | bytes 786440 | tf_op jit(solution)/shard_map/ppermute | solution.py:565
  252.8 16.7 %collective-permute-start.4 = (bf16[2,32,2048]{2,1,0:T(8,128)(2,1)S(1)}, bf16[2,32,2048]{2,1,0:T(8,128)(2,1)S(1)}, u32[]{:S(2)}, u32[]{:S(2)}) collective-permute-start(bf16[2,32,2048]{2,1,0:T(8,128)(2,1)S(1)} %bitcast.273), channel_id=1, source_target_pairs={{0,2},{1,3},{2,0},{3,1},{4,6},{5,7},{6,4},{7,5},{8,10},{9,11},{10,... | collective-permute-start | bytes 786440 | tf_op jit(solution)/shard_map/ppermute | solution.py:565
  256.2 18.9 %collective-permute-start.3 = (bf16[2,32,2048]{2,1,0:T(8,128)(2,1)S(1)}, bf16[2,32,2048]{2,1,0:T(8,128)(2,1)S(1)}, u32[]{:S(2)}, u32[]{:S(2)}) collective-permute-start(bf16[2,32,2048]{2,1,0:T(8,128)(2,1)S(1)} %bitcast.274), channel_id=1, source_target_pairs={{0,1},{1,2},{2,3},{3,0},{4,5},{5,6},{6,7},{7,4},{8,9},{9,10},{10,1... | collective-permute-start | bytes 786440 | tf_op jit(solution)/shard_map/ppermute | solution.py:565
  257.6 2.0 copy-start.67
  258.9 1.8 copy-start.19
  282.8 3.7 copy-start.34
  282.8 8.5 %slice-start = ((s8[5767168]{0:T(1024)(128)(4,1)}), s8[4194304]{0:T(1024)(128)(4,1)S(1)}, s32[]{:S(2)}) async-start(s8[5767168]{0:T(1024)(128)(4,1)} %bitcast.245), calls=%async_computation.1 | async-start | bytes 8388608
  286.5 4.8 slice-start.1
  291.3 3.1 copy-start.49
  303.7 32.8 %collective-permute-start.6 = (bf16[2,32,2048]{2,1,0:T(8,128)(2,1)}, bf16[2,32,2048]{2,1,0:T(8,128)(2,1)}, u32[]{:S(2)}, u32[]{:S(2)}) collective-permute-start(bf16[2,32,2048]{2,1,0:T(8,128)(2,1)} %get-tuple-element.97), channel_id=1, source_target_pairs={{0,3},{1,0},{2,1},{3,2},{4,7},{5,4},{6,5},{7,6},{8,11},{9,8},{10,9... | collective-permute-start | bytes 786440 | tf_op jit(solution)/shard_map/ppermute | solution.py:565
  307.7 31.0 %collective-permute-start.8 = (bf16[2,32,2048]{2,1,0:T(8,128)(2,1)}, bf16[2,32,2048]{2,1,0:T(8,128)(2,1)}, u32[]{:S(2)}, u32[]{:S(2)}) collective-permute-start(bf16[2,32,2048]{2,1,0:T(8,128)(2,1)} %get-tuple-element.98), channel_id=1, source_target_pairs={{0,1},{1,2},{2,3},{3,0},{4,5},{5,6},{6,7},{7,4},{8,9},{9,10},{10,1... | collective-permute-start | bytes 786440 | tf_op jit(solution)/shard_map/ppermute | solution.py:565
  308.1 5.6 copy-start.48
  308.1 30.6 %collective-permute-start.7 = (bf16[2,32,2048]{2,1,0:T(8,128)(2,1)}, bf16[2,32,2048]{2,1,0:T(8,128)(2,1)}, u32[]{:S(2)}, u32[]{:S(2)}) collective-permute-start(bf16[2,32,2048]{2,1,0:T(8,128)(2,1)} %get-tuple-element.99), channel_id=1, source_target_pairs={{0,2},{1,3},{2,0},{3,1},{4,6},{5,7},{6,4},{7,5},{8,10},{9,11},{10,... | collective-permute-start | bytes 786440 | tf_op jit(solution)/shard_map/ppermute | solution.py:565
  321.9 4.5 copy-start.13
  323.2 23.9 %collective-permute-start.12 = (bf16[2,32,2176]{2,1,0:T(8,128)(2,1)S(1)}, bf16[2,32,2176]{2,1,0:T(8,128)(2,1)S(1)}, u32[]{:S(2)}, u32[]{:S(2)}) collective-permute-start(bf16[2,32,2176]{2,1,0:T(8,128)(2,1)S(1)} %get-tuple-element.94), channel_id=1, source_target_pairs={{0,3},{1,0},{2,1},{3,2},{4,7},{5,4},{6,5},{7,6},{8,11},{9,8},{10,9... | collective-permute-start | bytes 835592 | tf_op jit(solution)/shard_map/ppermute | solution.py:565
  323.3 25.2 %collective-permute-start.14 = (bf16[2,32,2176]{2,1,0:T(8,128)(2,1)S(1)}, bf16[2,32,2176]{2,1,0:T(8,128)(2,1)S(1)}, u32[]{:S(2)}, u32[]{:S(2)}) collective-permute-start(bf16[2,32,2176]{2,1,0:T(8,128)(2,1)S(1)} %get-tuple-element.95), channel_id=1, source_target_pairs={{0,1},{1,2},{2,3},{3,0},{4,5},{5,6},{6,7},{7,4},{8,9},{9,10},{10,1... | collective-permute-start | bytes 835592 | tf_op jit(solution)/shard_map/ppermute | solution.py:565
  336.5 17.9 %collective-permute-start.13 = (bf16[2,32,2176]{2,1,0:T(8,128)(2,1)S(1)}, bf16[2,32,2176]{2,1,0:T(8,128)(2,1)S(1)}, u32[]{:S(2)}, u32[]{:S(2)}) collective-permute-start(bf16[2,32,2176]{2,1,0:T(8,128)(2,1)S(1)} %get-tuple-element.96), channel_id=1, source_target_pairs={{0,2},{1,3},{2,0},{3,1},{4,6},{5,7},{6,4},{7,5},{8,10},{9,11},{10,... | collective-permute-start | bytes 835592 | tf_op jit(solution)/shard_map/ppermute | solution.py:565
  388.9 1.8 copy-start.20
  390.7 1.8 copy-start.23
  390.7 2.5 copy-start.28
  393.2 6.3 slice-start.2
  394.8 2.7 copy-start.70
  394.8 4.7 slice-start.3
  399.5 3.6 copy-start.6
  781.0 7.7 copy-start.31
  788.8 2.6 copy-start.41
  793.6 3.8 copy-start.35
  797.4 2.6 copy-start.32
  803.4 10.6 %copy-start.17 = (f32[256,2048]{1,0:T(8,128)S(1)}, f32[256,2048]{1,0:T(8,128)}, u32[]{:S(2)}) copy-start(f32[256,2048]{1,0:T(8,128)} %copy-done.15) | copy-start | bytes 6291460
  814.0 5.0 copy-start.47
  (30 other events, 33.4 us)
Sparse Core Ops, SparseCore 0:
  154.5 79.2 all-gather.1

commit v3 on v2

--- a/solution.py
+++ b/solution.py
@@ -189,6 +189,25 @@
         compiler_params=pltpu.CompilerParams(vmem_limit_bytes=48 << 20),
         name="attend",
     )(seen, qn, q1, q2, lat, k1, k2, kvb)
+
+
+def attend_packed(seen, q, lat, k1, k2, kvb, scale):
+    micros, rows, _ = q.shape
+    length = lat.shape[1]
+    grid, specs, out_spec = attention_specs(micros, rows, length)
+    first = HEADS * NOPE // GROUP_LANES
+    second = HEADS * (NOPE + HALF_ROPE) // GROUP_LANES
+    specs[2] = pl.BlockSpec((1, rows, GROUP_LANES), lambda g, m: (m, 0, first + g))
+    specs[3] = pl.BlockSpec((1, rows, GROUP_LANES), lambda g, m: (m, 0, second + g))
+    return pl.pallas_call(
+        functools.partial(attend_kernel, scale),
+        grid=grid,
+        in_specs=specs,
+        out_specs=out_spec,
+        out_shape=jax.ShapeDtypeStruct((micros, rows, HEADS * VDIM), bf16),
+        compiler_params=pltpu.CompilerParams(vmem_limit_bytes=48 << 20),
+        name="attend",
+    )(seen, q, q, q, lat, k1, k2, kvb)
 
 
 def attend_back(seen, qn, q1, q2, lat, k1, k2, kvb, d_out, scale):
@@ -584,6 +603,133 @@
     return blocks[0].astype(f32) + got[0] + got[1] + got[2]
 
 
+def front_kernel(
+    x_ref,
+    again_ref,
+    kgain_ref,
+    kr_ref,
+    cos_ref,
+    sin_ref,
+    mat_ref,
+    ha_ref,
+    latent_ref,
+    q_ref,
+    lat_ref,
+    k1_ref,
+    k2_ref,
+    tiles,
+    pack,
+    packs,
+    send,
+    recv,
+    load,
+):
+    place = Place()
+    sems = Sems(send, recv)
+    size = tiles.shape[1]
+
+    def fetch(t):
+        return pltpu.make_async_copy(
+            mat_ref.at[t * size : (t + 1) * size], tiles.at[t % 2], load.at[t % 2]
+        )
+
+    fetch(0).start()
+    greet([place.along(k) for k in (1, 2, 3)])
+
+    def normed(t, carry):
+        span = pl.ds(pl.multiple_of(t * 32, 32), 32)
+        x = x_ref[span].astype(f32)
+        ha_ref[span] = (x * rms_scale(x) * again_ref[...]).astype(bf16)
+        return carry
+
+    lax.fori_loop(0, x_ref.shape[0] // 32, normed, 0)
+    ha = ha_ref[...]
+    kv_down = dot(ha, kr_ref[...], 1, 1)
+    latent = kv_down[:, :RANK]
+    latent_ref[...] = latent
+    micros, rows, _ = pack.shape
+    normal = (latent * rms_scale(latent) * kgain_ref[...]).astype(bf16)
+    first = kv_down[:, RANK : RANK + HALF_ROPE]
+    second = kv_down[:, RANK + HALF_ROPE : RANK + ROPE]
+    cosine, sine = cos_ref[:, :HALF_ROPE], sin_ref[:, :HALF_ROPE]
+    turned = (
+        (first * cosine - second * sine).astype(bf16),
+        (second * cosine + first * sine).astype(bf16),
+    )
+    for micro in range(micros):
+        span = slice(micro * rows, (micro + 1) * rows)
+        pack[micro, :, :RANK] = normal[span]
+        pack[micro, :, RANK : RANK + HALF_ROPE] = turned[0][span]
+        pack[micro, :, RANK + HALF_ROPE : RANK + ROPE] = turned[1][span]
+        pack[micro, :, RANK + ROPE :] = jnp.zeros((rows, ROPE), bf16)
+    block = lambda k: packs.at[:, k * rows : (k + 1) * rows]
+    for k in (1, 2, 3):
+        sems.push(pack, block(k), k - 1, place.along(k))
+
+    count = mat_ref.shape[0] // size
+    held = None
+    for t in range(count):
+        fetch(t).wait()
+        if t + 1 < count:
+            fetch(t + 1).start()
+        value = dot(ha, tiles[t % 2], 1, 1)
+        if t < count - 2:
+            q_ref[:, t * size : (t + 1) * size] = value.astype(bf16)
+        elif held is None:
+            held = value
+        else:
+            cosine, sine = cos_ref[...], sin_ref[...]
+            q_ref[:, (t - 1) * size : t * size] = (held * cosine - value * sine).astype(bf16)
+            q_ref[:, t * size : (t + 1) * size] = (value * cosine + held * sine).astype(bf16)
+
+    for k in (1, 2, 3):
+        sems.arrived(block(k), k - 1, place.along(4 - k))
+    for micro in range(micros):
+        for k in range(4):
+            span = slice(k * rows, (k + 1) * rows)
+            part = pack[micro] if k == 0 else packs[micro, span]
+            lat_ref[micro, span] = part[:, :RANK]
+            for ref, start in ((k1_ref, RANK), (k2_ref, RANK + HALF_ROPE)):
+                lanes32 = part[:, start : start + HALF_ROPE]
+                ref[micro, span] = jnp.concatenate([lanes32] * HEAD_GROUP, axis=1)
+    sems.drain()
+
+
+def front(x, again, kgain, kr, cosine, sine, mat, micros):
+    toks, wide = x.shape
+    length = 4 * (toks // micros)
+    shape = jax.ShapeDtypeStruct
+    vm, dma = pltpu.VMEM, pltpu.SemaphoreType.DMA
+    size = HEADS * HALF_ROPE
+    packed = RANK + 2 * ROPE
+    vmem = pl.BlockSpec(memory_space=pltpu.VMEM)
+    return pl.pallas_call(
+        front_kernel,
+        in_specs=[vmem] * 6 + [pl.BlockSpec(memory_space=HBM)],
+        out_specs=[vmem] * 6,
+        out_shape=[
+            shape((toks, wide), bf16),
+            shape((toks, RANK), f32),
+            shape((toks, mat.shape[0]), bf16),
+            shape((micros, length, RANK), bf16),
+            shape((micros, length, GROUP_LANES), bf16),
+            shape((micros, length, GROUP_LANES), bf16),
+        ],
+        scratch_shapes=[
+            vm((2, size, wide), bf16),
+            vm((micros, toks // micros, packed), bf16),
+            vm((micros, length, packed), bf16),
+            dma((3,)),
+            dma((3,)),
+            dma((2,)),
+        ],
+        compiler_params=pltpu.CompilerParams(
+            collective_id=9, has_side_effects=True, vmem_limit_bytes=40 << 20
+        ),
+        name="front",
+    )(x, again, kgain, kr, cosine, sine, mat)
+
+
 def swap_kernel(count, axes, *refs):
     ins, outs, buffers = (refs[n * count : (n + 1) * count] for n in range(3))
     send, recv, local = refs[3 * count :]
@@ -706,6 +852,9 @@
             job.sems.push(
                 self.part(place.chips[chip]), self.got1.at[n], self.slots[n], place.across[self.axis]
             )
+
+    def stage2(self):
+        place = self.job.place
         if self.own is not None:
             ring, sem = self.own
             self.loads = [
@@ -720,7 +869,7 @@
         else:
             self.mine = [self.part(place.chips[""]), self.part(place.chips[self.other])]
 
-    def stage2(self):
+    def stage3(self):
         sems, place = self.job.sems, self.job.place
         for n in (1, 0):
             if self.own is not None:
@@ -730,14 +879,14 @@
             if n == 1:
                 sems.push(self.got1.at[1], self.got2, self.slots[2], place.across[self.other])
 
-    def stage3(self):
+    def stage4(self):
         sems, place = self.job.sems, self.job.place
         sems.arrived(self.got2, self.slots[2], place.across[self.other])
         add_rows(self.got1.at[0], [self.got1.at[0], self.got2])
         if self.home:
             sems.push(self.got1.at[0], self.got3.at[self.home - 1], self.slots[3], place.along(self.home))
 
-    def stage4(self):
+    def stage5(self):
         if self.last is None:
             return
         job = self.job
@@ -754,34 +903,39 @@
         self.spread = PlaneGather(job.sems, place, part, half, by)
         self.spread.first(src)
 
-    def stage5(self):
+    def stage6(self):
         if self.last is not None:
             self.spread.second()
 
-    def stage6(self):
+    def stage7(self):
         if self.last is not None:
             self.stay.wait()
             self.spread.third()
 
-    def stage7(self):
+    def stage8(self):
         if self.last is not None:
             self.spread.fourth()
 
 
 class Pump:
-    LAGS = (0, 3, 3, 2, 1, 1, 1)
+    LAGS = (0, 4, 2, 3, 2, 1, 1, 1)
 
     def __init__(self, place, sems):
         self.place, self.sems = place, sems
         self.units = []
-        self.at = [0] * 7
+        self.at = [0] * 8
 
     def tick(self, flush=False):
-        for n in range(7):
+        for n in range(8):
             ahead = len(self.units) if n == 0 else self.at[n - 1]
             if self.at[n] < ahead - (0 if flush else self.LAGS[n]):
                 getattr(self.units[self.at[n]], "stage%d" % (n + 1))()
                 self.at[n] += 1
+
+    def ahead(self, count):
+        for _ in range(min(count, len(self.units) - self.at[0])):
+            self.units[self.at[0]].stage1()
+            self.at[0] += 1
 
     def run(self, count):
         for _ in range(count):
@@ -963,7 +1117,7 @@
         "x",
         "ex",
     )
-    pump.run(3)
+    pump.ahead(4)
     for copy in begin:
         copy.wait()
 
@@ -1206,6 +1360,7 @@
         part = inv * scaled - x * (inv * inv * inv) * inner
         r["ograd"][start : start + step] = (r["mb"][...] + part).astype(bf16)
         attn_gain_grad = attn_gain_grad + jnp.sum(upstream * x * inv, axis=0, keepdims=True)
+        pump.run(1)
     n_a, n_k = wide // 4, RANK // 4
     gains[...] = jnp.zeros(gains.shape, f32)
     for s in range(4):
@@ -1392,8 +1547,6 @@
 
 
     x_in = tokens.reshape(toks, width).astype(f32)
-    inv_one = rms_scale(x_in)
-    h_attn = (x_in * inv_one * attn_gain_f).astype(bf16)
     positions = (shard_index * rows + jnp.arange(rows, dtype=jnp.int32)).astype(f32)
     frequency = jnp.exp(
         -jnp.log(rope_base) * (2.0 * jnp.arange(HALF_ROPE, dtype=f32) / ROPE)
@@ -1402,38 +1555,58 @@
     cosine = jnp.tile(jnp.cos(angles), (micros, 1))
     sine = jnp.tile(jnp.sin(angles), (micros, 1))
     cos_all, sin_all = jnp.tile(cosine, (1, HEADS)), jnp.tile(sine, (1, HEADS))
-    q_raw = dot(h_attn, query_mat, 1, 1)
     n1, n2 = HEADS * NOPE, HEADS * (NOPE + HALF_ROPE)
-    q_first, q_second = q_raw[:, n1:n2], q_raw[:, n2:]
     by_micro = lambda t: t.reshape(micros, rows, t.shape[-1])
-    qn = by_micro(q_raw[:, :n1].astype(bf16))
-    q1 = by_micro((q_first * cos_all - q_second * sin_all).astype(bf16))
-    q2 = by_micro((q_second * cos_all + q_first * sin_all).astype(bf16))
-    kv_down = dot(h_attn, kv_down_mat, 1, 1)
-    latent = kv_down[:, :RANK]
-    inv_kv = rms_scale(latent)
-    latent_norm = (latent * inv_kv * kv_gain_f).astype(bf16)
-    k_first, k_second = kv_down[:, RANK : RANK + HALF_ROPE], kv_down[:, RANK + HALF_ROPE :]
-    latent_pack = jnp.concatenate(
-        [
-            latent_norm,
-            (k_first * cosine - k_second * sine).astype(bf16),
-            (k_second * cosine + k_first * sine).astype(bf16),
-            jnp.zeros((toks, ROPE), bf16),
-        ],
-        axis=-1,
-    )
-    packs = z_all(by_micro(latent_pack), fast)
-    length = packs.shape[1]
-    lat_all = packs[..., :RANK]
-    k1 = jnp.tile(packs[..., RANK : RANK + HALF_ROPE], (1, 1, HEAD_GROUP))
-    k2 = jnp.tile(packs[..., RANK + HALF_ROPE : RANK + ROPE], (1, 1, HEAD_GROUP))
+    row = lambda t: t.reshape(1, -1)
+    if fast:
+        h_attn, latent, q_all, lat_all, k1, k2 = front(
+            tokens.reshape(toks, width),
+            row(attn_gain_f),
+            row(kv_gain_f),
+            kr_mat,
+            cos_all,
+            sin_all,
+            query_mat,
+            micros,
+        )
+        length = lat_all.shape[1]
+    else:
+        inv_one = rms_scale(x_in)
+        h_attn = (x_in * inv_one * attn_gain_f).astype(bf16)
+        q_raw = dot(h_attn, query_mat, 1, 1)
+        q_first, q_second = q_raw[:, n1:n2], q_raw[:, n2:]
+        qn = by_micro(q_raw[:, :n1].astype(bf16))
+        q1 = by_micro((q_first * cos_all - q_second * sin_all).astype(bf16))
+        q2 = by_micro((q_second * cos_all + q_first * sin_all).astype(bf16))
+        kv_down = dot(h_attn, kv_down_mat, 1, 1)
+        latent = kv_down[:, :RANK]
+        inv_kv = rms_scale(latent)
+        latent_norm = (latent * inv_kv * kv_gain_f).astype(bf16)
+        k_first, k_second = kv_down[:, RANK : RANK + HALF_ROPE], kv_down[:, RANK + HALF_ROPE :]
+        latent_pack = jnp.concatenate(
+            [
+                latent_norm,
+                (k_first * cosine - k_second * sine).astype(bf16),
+                (k_second * cosine + k_first * sine).astype(bf16),
+                jnp.zeros((toks, ROPE), bf16),
+            ],
+            axis=-1,
+        )
+        packs = z_all(by_micro(latent_pack), fast)
+        length = packs.shape[1]
+        lat_all = packs[..., :RANK]
+        k1 = jnp.tile(packs[..., RANK : RANK + HALF_ROPE], (1, 1, HEAD_GROUP))
+        k2 = jnp.tile(packs[..., RANK + HALF_ROPE : RANK + ROPE], (1, 1, HEAD_GROUP))
     key_shard = jnp.arange(length, dtype=jnp.int32) // rows
     if fast:
         key_shard = (shard_index - key_shard) % 4
     key_block = (key_shard * rows + jnp.arange(length, dtype=jnp.int32) % rows) // MASK_BLOCK
     seen = (key_block <= (shard_index * rows) // MASK_BLOCK).astype(f32).reshape(1, length)
-    attended = attend(seen, qn, q1, q2, lat_all, k1, k2, kvb_mat, scale).reshape(toks, -1)
+    if fast:
+        attended = attend_packed(seen, by_micro(q_all), lat_all, k1, k2, kvb_mat, scale)
+    else:
+        attended = attend(seen, qn, q1, q2, lat_all, k1, k2, kvb_mat, scale)
+    attended = attended.reshape(toks, -1)
 
     x_mid = x_in + dot(attended, out_mat, 1, 0)
     inv_two = rms_scale(x_mid)
@@ -1557,14 +1730,13 @@
 
     lane_rows = lambda t: t.reshape(shard_count, -1)
     if fast:
-        row = lambda t: t.reshape(1, -1)
         group_tab = lambda t: jnp.tile(t[:rows], (1, HEAD_GROUP))
         res = back_all(
             dict(
                 gsh=grad_sh,
                 gex=grad_ex,
                 gout=grad_out,
-                q=jnp.concatenate([t.reshape(toks, -1) for t in (qn, q1, q2)], axis=1),
+                q=q_all,
                 kvb=kvb_mat,
                 kq=query_mat,
                 kkr=kr_mat,

time: 840 us -> 792 us (0.943)
  waiting for transfers between devices: 45.6 us -> 22.2 us
  Pallas kernels: 521 us -> 544 us
  local copies, waits for them, and re-layouts: 66.7 us -> 51.2 us
  matrix products: 89.3 us -> 76 us
  other arithmetic: 66 us -> 52.8 us
    pallas_call x1 -> x2, Pallas kernels: 20.8 us -> 60.8 us  [the longest x1 38.9 us: front(): pl.pallas_call(front_kernel, in_specs=[vmem] * 6 + [pl.BlockSpec(memory_s...]
    ppermute x15 -> x12, waiting for transfers between devices: 45.6 us -> 22.2 us  [along_z(): lax.ppermute(tensor, 'shard', [(i, (i + step) % 4) for i in range(4)])]
    pallas_call x1, Pallas kernels: 354 us -> 337 us  [back_all(): pl.pallas_call(functools.partial(back_kernel, scale, names), in_specs=[hb...]
    dot_general x23 -> x21, matrix products: 53.7 us -> 44.3 us  [dot(): lax.dot_general(a, b, (((ca,), (cb,)), ((), ())), preferred_element_type=...]
    unnamed x164 -> x149, local copies, waits for them, and re-layouts: 29 us -> 24.6 us
    ppermute x15 -> x12, starting transfers between devices: 22.8 us -> 21.8 us  [along_z(): lax.ppermute(tensor, 'shard', [(i, (i + step) % 4) for i in range(4)])]
  transfers between devices with their start and end apart: 16 -> 13, of which waited for: 9 -> 5; matrix products, arithmetic and copies ran while one was open for 13% -> 9% of each run, Pallas kernels for 3% -> 9%
where the time goes in v3:
time: 792 us; the launch traced here: 784 us
  Pallas kernels  544 us (69%)
  matrix products  76 us (10%)
  other arithmetic  52.8 us (7%)
  local copies, waits for them, and re-layouts  51.2 us (6%)
  waiting for transfers between devices  22.2 us (3%)
  starting transfers between devices  21.9 us (3%)
  between operations  15.8 us (2%)
    pallas_call x1, Pallas kernels, back_all(): pl.pallas_call(functools.partial(back_kernel, scale, names), in_specs=[hb...  337 us
    pallas_call x1, Pallas kernels, gather_weights(): pl.pallas_call(gather_kernel, in_specs=[pl.BlockSpec(memory_space=HBM)] *...  131 us
    dot_general x21, matrix products, dot(): lax.dot_general(a, b, (((ca,), (cb,)), ((), ())), preferred_element_type=...  44.3 us
    pallas_call x1, Pallas kernels, front(): pl.pallas_call(front_kernel, in_specs=[vmem] * 6 + [pl.BlockSpec(memory_s...  38.9 us
    convert_element_type x8, other arithmetic, shards(): wide = lambda t: t.astype(f32)  27.4 us
    unnamed x149, local copies, waits for them, and re-layouts  24.6 us
    dot_general x6, matrix products, shards(): lax.dot_general(a, b, (((ca,), (cb,)), ((0,), (0,))), preferred_element_t...  23 us
    ppermute x12, waiting for transfers between devices, along_z(): lax.ppermute(tensor, 'shard', [(i, (i + step) % 4) for i in range(4)])  22.2 us
  transfers between devices with their start and end apart: 13, of which 5 were waited for; matrix products, arithmetic and copies ran while one was open for 9% of the time, Pallas kernels for 9%

profile of v3, /device:TPU:9, one launch (start us, length us, event | category | flops | bytes accessed | tf_op | source)
XLA Modules:
  0.0 784.1 jit_solution(8945087703605929019)
XLA Ops:
  7.2 3.2 convert.43
  14.1 2.0 copy-done.28
  20.1 130.7 %gather_weights.1 = (bf16[3072,2048]{1,0:T(8,128)(2,1)}, bf16[640,2048]{1,0:T(8,128)(2,1)S(1)}, bf16[512,4096]{1,0:T(8,128)(2,1)S(1)}, bf16[2048,2048]{1,0:T(8,1...) custom-call(bf16[3072,512]{1,0:T(8,128)(2,1)S(1)} %pad_maximum_fusion.3.refs_0_, ...), custom_call_target="tpu_custom_call" | custom-call | tf_op jit(solution)/shard_map/gather_weights/pallas_call | solution.py:556
  150.9 2.0 copy-done.1
  155.9 1.9 collective-permute-start.8
  157.8 2.1 collective-permute-start.7
  161.0 1.6 tile.58
  164.0 2.2 copy-done.4
  166.2 38.9 %front.1 = (bf16[256,2048]{1,0:T(8,128)(2,1)S(1)}, f32[256,512]{1,0:T(8,128)S(1)}, bf16[256,3072]{1,0:T(8,128)(2,1)S(1)}, bf16[2,512,512]{2,1,0:T(8,128)(2,1)S(1...) custom-call(bf16[256,2048]{1,0:T(8,128)(2,1)S(1)} %bitcast.203, f32[1,2048]{1,0:T(1,128)S(1)} %bitcast.212, ...), custom_call_target="tpu_custom_call" | custom-call | tf_op jit(solution)/shard_map/front/pallas_call | solution.py:706
  206.9 21.9 %attend.1 = bf16[2,128,2048]{2,1,0:T(8,128)(2,1)S(1)} custom-call(f32[1,512]{1,0:T(1,128)S(1)} %compare_convert_fusion.seen_ref.refs_12_, bf16[2,128,3072]{2,1,0:T(8,128)(2,1)S(1)} %bitcast.196, bf16[2,128,3072]{2,1,0:T(8,128)(2,1)S(1)} %bitcast.197, bf16[2,128,3072]{2,1,0:T(8,128)(2,1)S(1)} %bitcast.198, ...), custom_call_target="tpu_custom_call" | custom-call | tf_op jit(solution)/shard_map/attend/pallas_call | solution.py:202
  228.9 2.6 multiply_reduce_fusion.3
  232.9 3.5 collective-permute-start.1
  236.4 2.3 collective-permute-start
  242.2 3.4 fusion.82
  245.7 1.5 fusion.85
  249.6 3.4 collective-permute-done.1
  253.6 4.9 collective-permute-done
  261.2 3.5 fusion.21
  264.8 3.7 fusion.25
  268.5 4.8 multiply_convert_fusion.6
  273.3 3.1 multiply_reduce_fusion.2
  279.1 1.9 pad_maximum_fusion.11
  281.0 2.1 copy.121
  283.1 2.0 fusion.100
  285.2 5.8 collective-permute-start.3
  291.0 2.1 collective-permute-start.4
  293.1 3.5 fusion.23
  296.6 4.5 fusion.8
  301.7 3.1 concatenate.57
  309.9 6.0 core_swap.4
  318.0 2.3 pad_maximum_fusion.2.refs_1_
  320.3 2.1 collective-permute-start.10
  324.0 7.8 collective-permute-done.11
  331.7 6.0 collective-permute-done.10
  340.4 2.3 fusion.41
  342.8 2.3 fusion.43
  345.1 5.6 fusion.95
  350.7 1.6 convolution_bitcast_fusion
  352.3 1.6 fusion.107
  353.9 1.6 fusion.106
  356.6 1.6 fusion.35
  358.2 2.9 fusion.39
  361.1 1.6 fusion.37
  362.8 1.6 copy-done.22
  368.5 2.6 multiply_reduce_fusion
  371.2 2.0 fusion.93
  373.2 3.6 convolution_convert_fusion.3
  376.8 3.6 core_swap.5
  380.4 5.9 core_swap.3
  386.3 1.7 fusion.2
  387.9 1.7 fusion.1
  389.6 1.7 fusion.3
  391.3 4.4 bitcast_convert_fusion.refs_2_
  395.7 4.4 pad_maximum_fusion.refs_0_
  400.1 337.4 %back_all.1 = (bf16[3072,512]{1,0:T(8,128)(2,1)}, bf16[640,512]{1,0:T(8,128)(2,1)}, bf16[128,4096]{1,0:T(8,128)(2,1)}, bf16[512,2048]{1,0:T(8,128)(2,1)}, bf16[2...) custom-call(bf16[3,1408,1024]{2,1,0:T(8,128)(2,1)} %pad_maximum_fusi, ...), custom_call_target="tpu_custom_call" | custom-call | tf_op jit(solution)/shard_map/back_all/pallas_call | solution.py:1461
  740.2 1.5 slice_convert_fusion.4
  741.7 2.2 slice_convert_fusion.3
  746.4 1.5 convert_element_type.324
  747.9 1.9 convert_element_type.331
  750.4 3.8 bitcast_convert_fusion.1
  754.3 2.5 convert_element_type.325
  756.9 3.3 bitcast_convert_fusion.5
  760.2 10.6 %slice_convert_fusion = (f32[2,352,2048]{2,1,0:T(8,128)}, f32[2,352,2048]{2,1,0:T(8,128)}, f32[2,352,2048]{2,1,0:T(8,128)}) fusion(bf16[6,352,2048]{2,1,0:T(8,128)(2,1)} %get-tuple-element.73), kind=kLoop, calls=%fused_computation.17 | loop fusion | flops 4325376 | bytes 25952256 | tf_op jit(solution)/shard_map/convert_element_type | solution.py:1810
  770.8 5.0 fusion.9
  (248 shorter events, 52.1 us)
Async XLA Ops:
  7.2 337.9 %all-gather.2.cloned.1.call-start = ((), (), s32[]{:S(2)}) async-start(), calls=%async_computation | async-start | bytes 14598144 | tf_op jit(solution)/shard_map/all_gather | solution.py:579
  10.6 2.0 copy-start.32
  11.9 2.0 copy-start.20
  13.9 2.2 copy-start.28
  16.1 1.8 copy-start.23
  16.1 2.7 copy-start.25
  20.1 134.3 %copy-start.59 = (s32[2,128,6]{1,0,2:T(2,128)S(1)}, s32[2,128,6]{1,0,2:T(2,128)}, u32[]{:S(2)}) copy-start(s32[2,128,6]{1,0,2:T(2,128)} %param.32) | copy-start | bytes 18436
  150.9 2.0 copy-start.1
  155.9 8.2 %copy-start.5 = (bf16[2,128,2048]{2,1,0:T(8,128)(2,1)S(1)}, bf16[2,128,2048]{2,1,0:T(8,128)(2,1)}, u32[]{:S(2)}) copy-start(bf16[2,128,2048]{2,1,0:T(8,128)(2,1)} %param.17) | copy-start | bytes 3145732
  155.9 112.6 %collective-permute-start.8 = (bf16[2,32,2048]{2,1,0:T(8,128)(2,1)S(1)}, bf16[2,32,2048]{2,1,0:T(8,128)(2,1)}, u32[]{:S(2)}, u32[]{:S(2)}) collective-permute-start(bf16[2,32,2048]{2,1,0:T(8,128)(2,1)S(1)} %bitcast.236), channel_id=1, source_target_pairs={{0,3},{1,0},{2,1},{3,2},{4,7},{5,4},{6,5},{7,6},{8,11},{9,8},{10,9... | collective-permute-start | bytes 786440 | tf_op jit(solution)/shard_map/ppermute | solution.py:584
  157.8 110.7 %collective-permute-start.7 = (bf16[2,32,2048]{2,1,0:T(8,128)(2,1)S(1)}, bf16[2,32,2048]{2,1,0:T(8,128)(2,1)}, u32[]{:S(2)}, u32[]{:S(2)}) collective-permute-start(bf16[2,32,2048]{2,1,0:T(8,128)(2,1)S(1)} %bitcast.237), channel_id=1, source_target_pairs={{0,2},{1,3},{2,0},{3,1},{4,6},{5,7},{6,4},{7,5},{8,10},{9,11},{10,... | collective-permute-start | bytes 786440 | tf_op jit(solution)/shard_map/ppermute | solution.py:584
  163.9 41.2 %copy-start.15 = (f32[4,128]{1,0:T(4,128)}, f32[4,128]{1,0:T(4,128)S(1)}, u32[]{:S(2)}) copy-start(f32[4,128]{1,0:T(4,128)S(1)} %slice.235) | copy-start | bytes 6148
  163.9 68.2 %copy-start.51 = (f32[1,4,4,128]{3,1,2,0:T(4,128)}, f32[1,4,4,128]{3,1,2,0:T(4,128)S(1)}, u32[]{:S(2)}) copy-start(f32[1,4,4,128]{3,1,2,0:T(4,128)S(1)} %copy.160) | copy-start | bytes 24580
  164.0 41.1 %copy-start.14 = (f32[1,1,4,512]{3,1,2,0:T(1,128)}, f32[1,1,4,512]{3,1,2,0:T(1,128)S(1)}, u32[]{:S(2)}) copy-start(f32[1,1,4,512]{3,1,2,0:T(1,128)S(1)} %copy.157) | copy-start | bytes 24580
  164.0 2.2 copy-start.4
  206.9 22.0 %copy-start = (bf16[256,3072]{1,0:T(8,128)(2,1)}, bf16[256,3072]{1,0:T(8,128)(2,1)S(1)}, u32[]{:S(2)}) copy-start(bf16[256,3072]{1,0:T(8,128)(2,1)S(1)} %get-tuple-element.48.refs_3_) | copy-start | bytes 4718596
  206.9 22.0 %copy-start.6 = (bf16[2,512,512]{2,1,0:T(8,128)(2,1)}, bf16[2,512,512]{2,1,0:T(8,128)(2,1)S(1)}, u32[]{:S(2)}) copy-start(bf16[2,512,512]{2,1,0:T(8,128)(2,1)S(1)} %get-tuple-element.49.lat_ref.refs_9_) | copy-start | bytes 3145732
  206.9 22.0 %copy-start.10 = (bf16[2,512,128]{2,1,0:T(8,128)(2,1)}, bf16[2,512,128]{2,1,0:T(8,128)(2,1)S(1)}, u32[]{:S(2)}) copy-start(bf16[2,512,128]{2,1,0:T(8,128)(2,1)S(1)} %get-tuple-element.50.k1_ref.refs_10_) | copy-start | bytes 786436
  206.9 22.0 %copy-start.11 = (bf16[2,512,128]{2,1,0:T(8,128)(2,1)}, bf16[2,512,128]{2,1,0:T(8,128)(2,1)S(1)}, u32[]{:S(2)}) copy-start(bf16[2,512,128]{2,1,0:T(8,128)(2,1)S(1)} %get-tuple-element.51.k2_ref.refs_11_) | copy-start | bytes 786436
  206.9 22.0 %copy-start.16 = (f32[1,512]{1,0:T(1,128)}, f32[1,512]{1,0:T(1,128)S(1)}, u32[]{:S(2)}) copy-start(f32[1,512]{1,0:T(1,128)S(1)} %compare_convert_fusion.seen_ref.refs_12_) | copy-start | bytes 6148
  206.9 22.0 %copy-start.64 = (bf16[2048,2048]{1,0:T(8,128)(2,1)S(1)}, bf16[2048,2048]{1,0:T(8,128)(2,1)}, u32[]{:S(2)}) copy-start(bf16[2048,2048]{1,0:T(8,128)(2,1)} %get-tuple-element.53) | copy-start | bytes 25165828
  228.9 2.6 copy-start.7
  232.1 6.6 copy-start.49
  232.1 7.3 copy-start.47
  232.8 12.8 %copy-start.40 = (bf16[2,2,16,2048]{3,2,1,0:T(8,128)(2,1)}, bf16[2,2,16,2048]{3,2,1,0:T(8,128)(2,1)S(1)}, u32[]{:S(2)}) copy-start(bf16[2,2,16,2048]{3,2,1,0:T(8,128)(2,1)S(1)} %copy.116) | copy-start | bytes 786436
  232.9 16.2 %collective-permute-start.2 = (bf16[2,32,2048]{2,1,0:T(8,128)(2,1)S(1)}, bf16[2,32,2048]{2,1,0:T(8,128)(2,1)S(1)}, u32[]{:S(2)}, u32[]{:S(2)}) collective-permute-start(bf16[2,32,2048]{2,1,0:T(8,128)(2,1)S(1)} %bitcast.253), channel_id=1, source_target_pairs={{0,3},{1,0},{2,1},{3,2},{4,7},{5,4},{6,5},{7,6},{8,11},{9,8},{10,9... | collective-permute-start | bytes 786440 | tf_op jit(solution)/shard_map/ppermute | solution.py:584
  232.9 20.0 %collective-permute-start.1 = (bf16[2,32,2048]{2,1,0:T(8,128)(2,1)S(1)}, bf16[2,32,2048]{2,1,0:T(8,128)(2,1)S(1)}, u32[]{:S(2)}, u32[]{:S(2)}) collective-permute-start(bf16[2,32,2048]{2,1,0:T(8,128)(2,1)S(1)} %bitcast.254), channel_id=1, source_target_pairs={{0,2},{1,3},{2,0},{3,1},{4,6},{5,7},{6,4},{7,5},{8,10},{9,11},{10,... | collective-permute-start | bytes 786440 | tf_op jit(solution)/shard_map/ppermute | solution.py:584
  236.4 22.1 %collective-permute-start = (bf16[2,32,2048]{2,1,0:T(8,128)(2,1)S(1)}, bf16[2,32,2048]{2,1,0:T(8,128)(2,1)}, u32[]{:S(2)}, u32[]{:S(2)}) collective-permute-start(bf16[2,32,2048]{2,1,0:T(8,128)(2,1)S(1)} %bitcast.255), channel_id=1, source_target_pairs={{0,1},{1,2},{2,3},{3,0},{4,5},{5,6},{6,7},{7,4},{8,9},{9,10},{10,1... | collective-permute-start | bytes 786440 | tf_op jit(solution)/shard_map/ppermute | solution.py:584
  241.6 4.1 copy-start.57
  242.2 3.4 copy-start.21
  245.7 2.0 copy-start.26
  247.6 10.9 %copy-start.41 = (bf16[2,2,16,2048]{3,2,1,0:T(8,128)(2,1)S(1)}, bf16[2,2,16,2048]{3,2,1,0:T(8,128)(2,1)}, u32[]{:S(2)}) copy-start(bf16[2,2,16,2048]{3,2,1,0:T(8,128)(2,1)} %copy-done.40) | copy-start | bytes 786436
  249.1 3.8 copy-start.44
  249.1 19.4 %collective-permute-start.6 = (bf16[2,32,2048]{2,1,0:T(8,128)(2,1)S(1)}, bf16[2,32,2048]{2,1,0:T(8,128)(2,1)}, u32[]{:S(2)}, u32[]{:S(2)}) collective-permute-start(bf16[2,32,2048]{2,1,0:T(8,128)(2,1)S(1)} %bitcast.238), channel_id=1, source_target_pairs={{0,1},{1,2},{2,3},{3,0},{4,5},{5,6},{6,7},{7,4},{8,9},{9,10},{10,1... | collective-permute-start | bytes 786440 | tf_op jit(solution)/shard_map/ppermute | solution.py:584
  264.8 8.6 %slice-start = ((s8[5767168]{0:T(1024)(128)(4,1)}), s8[4194304]{0:T(1024)(128)(4,1)S(1)}, s32[]{:S(2)}) async-start(s8[5767168]{0:T(1024)(128)(4,1)} %bitcast.228), calls=%async_computation.1 | async-start | bytes 8388608
  268.5 4.8 slice-start.1
  273.3 3.1 copy-start.43
  285.2 35.2 %collective-permute-start.3 = (bf16[2,32,2048]{2,1,0:T(8,128)(2,1)}, bf16[2,32,2048]{2,1,0:T(8,128)(2,1)}, u32[]{:S(2)}, u32[]{:S(2)}) collective-permute-start(bf16[2,32,2048]{2,1,0:T(8,128)(2,1)} %get-tuple-element.105), channel_id=1, source_target_pairs={{0,3},{1,0},{2,1},{3,2},{4,7},{5,4},{6,5},{7,6},{8,11},{9,8},{10,9... | collective-permute-start | bytes 786440 | tf_op jit(solution)/shard_map/ppermute | solution.py:584
  291.0 31.5 %collective-permute-start.5 = (bf16[2,32,2048]{2,1,0:T(8,128)(2,1)}, bf16[2,32,2048]{2,1,0:T(8,128)(2,1)}, u32[]{:S(2)}, u32[]{:S(2)}) collective-permute-start(bf16[2,32,2048]{2,1,0:T(8,128)(2,1)} %get-tuple-element.106), channel_id=1, source_target_pairs={{0,1},{1,2},{2,3},{3,0},{4,5},{5,6},{6,7},{7,4},{8,9},{9,10},{10,1... | collective-permute-start | bytes 786440 | tf_op jit(solution)/shard_map/ppermute | solution.py:584
  291.0 5.6 copy-start.42
  291.0 31.5 %collective-permute-start.4 = (bf16[2,32,2048]{2,1,0:T(8,128)(2,1)}, bf16[2,32,2048]{2,1,0:T(8,128)(2,1)}, u32[]{:S(2)}, u32[]{:S(2)}) collective-permute-start(bf16[2,32,2048]{2,1,0:T(8,128)(2,1)} %get-tuple-element.107), channel_id=1, source_target_pairs={{0,2},{1,3},{2,0},{3,1},{4,6},{5,7},{6,4},{7,5},{8,10},{9,11},{10,... | collective-permute-start | bytes 786440 | tf_op jit(solution)/shard_map/ppermute | solution.py:584
  306.0 18.0 %collective-permute-start.9 = (bf16[2,32,2176]{2,1,0:T(8,128)(2,1)S(1)}, bf16[2,32,2176]{2,1,0:T(8,128)(2,1)S(1)}, u32[]{:S(2)}, u32[]{:S(2)}) collective-permute-start(bf16[2,32,2176]{2,1,0:T(8,128)(2,1)S(1)} %get-tuple-element.102), channel_id=1, source_target_pairs={{0,3},{1,0},{2,1},{3,2},{4,7},{5,4},{6,5},{7,6},{8,11},{9,8},{10,9... | collective-permute-start | bytes 835592 | tf_op jit(solution)/shard_map/ppermute | solution.py:584
  306.1 25.7 %collective-permute-start.11 = (bf16[2,32,2176]{2,1,0:T(8,128)(2,1)S(1)}, bf16[2,32,2176]{2,1,0:T(8,128)(2,1)S(1)}, u32[]{:S(2)}, u32[]{:S(2)}) collective-permute-start(bf16[2,32,2176]{2,1,0:T(8,128)(2,1)S(1)} %get-tuple-element.103), channel_id=1, source_target_pairs={{0,1},{1,2},{2,3},{3,0},{4,5},{5,6},{6,7},{7,4},{8,9},{9,10},{10,1... | collective-permute-start | bytes 835592 | tf_op jit(solution)/shard_map/ppermute | solution.py:584
  320.3 18.8 %copy-start.58 = (f32[256]{0:T(256)S(1)}, f32[256]{0:T(256)}, u32[]{:S(2)}) copy-start(f32[256]{0:T(256)} %copy-done.57) | copy-start | bytes 3076
  320.3 18.8 %copy-start.60 = (f32[256]{0:T(256)S(1)}, f32[256]{0:T(256)}, u32[]{:S(2)}) copy-start(f32[256]{0:T(256)} %fusion.62) | copy-start | bytes 3076
  320.3 17.3 %collective-permute-start.10 = (bf16[2,32,2176]{2,1,0:T(8,128)(2,1)S(1)}, bf16[2,32,2176]{2,1,0:T(8,128)(2,1)S(1)}, u32[]{:S(2)}, u32[]{:S(2)}) collective-permute-start(bf16[2,32,2176]{2,1,0:T(8,128)(2,1)S(1)} %get-tuple-element.104), channel_id=1, source_target_pairs={{0,2},{1,3},{2,0},{3,1},{4,6},{5,7},{6,4},{7,5},{8,10},{9,11},{10,... | collective-permute-start | bytes 835592 | tf_op jit(solution)/shard_map/ppermute | solution.py:584
  353.8 1.6 copy-start.33
  353.8 1.6 copy-start.34
  353.8 1.6 copy-start.35
  362.7 1.8 copy-start.22
  364.5 1.8 copy-start.24
  364.5 2.5 copy-start.27
  366.9 1.6 copy-start.18
  366.9 1.6 copy-start.52
  366.9 6.2 slice-start.2
  368.5 2.6 copy-start.61
  368.5 4.7 slice-start.3
  373.2 3.6 copy-start.8
  737.5 7.7 copy-start.29
  745.3 2.6 copy-start.36
  750.4 3.8 copy-start.31
  754.3 2.6 copy-start.30
  760.2 10.6 %copy-start.19 = (f32[256,2048]{1,0:T(8,128)S(1)}, f32[256,2048]{1,0:T(8,128)}, u32[]{:S(2)}) copy-start(f32[256,2048]{1,0:T(8,128)} %copy-done.17) | copy-start | bytes 6291460
  770.8 5.0 copy-start.39
  (19 other events, 17.5 us)
Sparse Core Ops, SparseCore 0:
  154.5 79.2 all-gather.1

commit v4 on v3

--- a/solution.py
+++ b/solution.py
@@ -918,7 +918,7 @@
 
 
 class Pump:
-    LAGS = (0, 4, 2, 3, 2, 1, 1, 1)
+    LAGS = (0, 4, 2, 4, 3, 2, 2, 2)
 
     def __init__(self, place, sems):
         self.place, self.sems = place, sems
@@ -950,8 +950,12 @@
 
 
 BACK_IN = (
-    "gsh",
-    "gex",
+    "gs0",
+    "gs1",
+    "gs2",
+    "ge0",
+    "ge1",
+    "ge2",
     "gout",
     "q",
     "kvb",
@@ -973,7 +977,7 @@
     "sin",
     "rtr",
 )
-BACK_HBM = 9
+BACK_HBM = 13
 BACK_OUT = (
     "oq",
     "okr",
@@ -986,7 +990,7 @@
     "ogain",
     "ograd",
 )
-BACK_SLOTS = 3 + 3 + 5 + 10 + 28 * 4 + 7 * 4
+BACK_SLOTS = 6 + 3 + 5 + 10 + 28 * 4 + 7 * 4
 EARLY = 2
 
 
@@ -1005,12 +1009,18 @@
     toks = r["ha"].shape[0]
     rows = toks // 2
 
-    ff = r["gsh"].shape[1] // 4
-    shared_slots = [sems.slot() for _ in range(3)]
-    for k in (1, 2, 3):
-        sems.push(
-            r["gsh"].at[:EARLY, k * ff : (k + 1) * ff], r["zsh"].at[k - 1], shared_slots[k - 1], place.along(4 - k)
-        )
+    shared = [r["gs0"], r["gs1"], r["gs2"]]
+    experts = [r["ge0"], r["ge1"], r["ge2"]]
+    ff = shared[0].shape[0] // 4
+    shared_slots = [[sems.slot() for _ in range(3)] for _ in range(EARLY)]
+    for j in range(EARLY):
+        for k in (1, 2, 3):
+            sems.push(
+                shared[j].at[k * ff : (k + 1) * ff],
+                r["zsh"].at[k - 1, j],
+                shared_slots[j][k - 1],
+                place.along(4 - k),
+            )
     swap = {name: sems.slot() for name in ("ha", "kvb", "q", "kvd", "rtr")}
     sems.push(r["ha"], r["s_ha"], swap["ha"], place.peer)
     sems.push(r["rtr"], r["s_rtr"], swap["rtr"], place.peer)
@@ -1045,9 +1055,10 @@
         rings += 1
         return slot
 
-    def add_matrices(name, source, count, out, by, ringed):
+    def add_matrices(name, sources, out, by, ringed):
+        count = len(sources)
         for u in range(count):
-            n = source.shape[-1] // 4
+            n = sources[u].shape[-1] // 4
             own = None
             if ringed:
                 slot = ring(None)
@@ -1061,7 +1072,7 @@
                     name,
                     u,
                     "x" if u % 2 == 0 else "y",
-                    lambda chip, u=u: source.at[u, :, lanes(chip * n, n)],
+                    lambda chip, u=u: sources[u].at[:, lanes(chip * n, n)],
                     r["got1_" + name].at[u],
                     r["got2_" + name].at[u],
                     own=own,
@@ -1095,7 +1106,7 @@
                 )
             )
 
-    add_matrices("ex", r["gex"], r["gex"].shape[0], r["oex"], "x", True)
+    add_matrices("ex", [t.at[e] for t in experts for e in range(EXP_WIN)], r["oex"], "x", True)
     block = r["gout"].shape[0] // 4
     n_out = r["gout"].shape[1] // 4
     add_sharded(
@@ -1106,11 +1117,11 @@
         "y",
         "out",
     )
-    n_sd = r["gsh"].shape[2] // 4
+    n_sd = shared[EARLY].shape[1] // 4
     add_sharded(
         "sd",
-        lambda s, k, chip: r["gsh"].at[
-            EARLY, (4 - k) % 4 * ff : ((4 - k) % 4 + 1) * ff, lanes(chip * n_sd, n_sd)
+        lambda s, k, chip: shared[EARLY].at[
+            (4 - k) % 4 * ff : ((4 - k) % 4 + 1) * ff, lanes(chip * n_sd, n_sd)
         ],
         r["osd"],
         False,
@@ -1295,11 +1306,11 @@
         if t % 2 == 1:
             pump.run(1)
 
-    for k in (1, 2, 3):
-        sems.arrived(r["zsh"].at[k - 1], shared_slots[k - 1], place.along(k))
-    cols = r["gsh"].shape[2]
+    cols = shared[0].shape[1]
     for j in range(EARLY):
-        copies = [pltpu.make_async_copy(r["gsh"].at[j, :ff], kvbs.at[:ff, :cols], load.at[6])]
+        for k in (1, 2, 3):
+            sems.arrived(r["zsh"].at[k - 1, j], shared_slots[j][k - 1], place.along(k))
+        copies = [pltpu.make_async_copy(shared[j].at[:ff], kvbs.at[:ff, :cols], load.at[6])]
         for k in range(3):
             copies.append(
                 pltpu.make_async_copy(
@@ -1311,7 +1322,7 @@
         for copy in copies:
             copy.wait()
         add_rows(r["gshs"].at[j], [kvbs.at[:ff, k * cols : (k + 1) * cols] for k in range(4)])
-    add_matrices("sh", r["gshs"], EARLY, r["osh"], "y", False)
+    add_matrices("sh", [r["gshs"].at[j] for j in range(EARLY)], r["osh"], "y", False)
     pump.run(2)
 
     sems.arrived(r["s_kvd"], swap["kvd"], place.peer)
@@ -1389,10 +1400,11 @@
 
 def back_all(args, scale):
     shape = jax.ShapeDtypeStruct
-    gsh, gex, gout, q, kvb, kq, kkr = (args[n] for n in BACK_IN[:7])
+    gout, q, kvb, kq, kkr = (args[n] for n in ("gout", "q", "kvb", "kq", "kkr"))
     toks, wide = args["ha"].shape
     micros, length, rank = args["lat"].shape
-    fe, ff = gex.shape[1], gsh.shape[1] // 4
+    fe, ff = args["ge0"].shape[1], args["gs0"].shape[0] // 4
+    mats = 3 * EXP_WIN
     rows = toks // micros
     n_a = wide // 4
     gain_shape = (8, 2 * n_a + rank // 4)
@@ -1403,7 +1415,7 @@
         oout=shape((gout.shape[0] // 4, wide), bf16),
         osh=shape((EARLY, ff, wide), bf16),
         osd=shape((ff, wide), bf16),
-        oex=shape((gex.shape[0], fe, wide), bf16),
+        oex=shape((mats, fe, wide), bf16),
         zsh=shape((3, EARLY, ff, wide // 2), bf16),
         ogain=shape(gain_shape, f32),
         ograd=shape((toks, wide), bf16),
@@ -1443,8 +1455,8 @@
         gs=vm(gain_shape, f32),
         ring_ex=vm((4, 2, fe, wide // 8), bf16),
         ring_out=vm((4, 2) + parts["out"], bf16),
-        got1_ex=vm((gex.shape[0], 2, fe, wide // 8), bf16),
-        got2_ex=vm((gex.shape[0], fe, wide // 8), bf16),
+        got1_ex=vm((mats, 2, fe, wide // 8), bf16),
+        got2_ex=vm((mats, fe, wide // 8), bf16),
         got1_sh=vm((EARLY, 2, ff, wide // 8), bf16),
         got2_sh=vm((EARLY, ff, wide // 8), bf16),
     )
@@ -1636,21 +1648,16 @@
     shared_hidden = (jax.nn.silu(gate_pre) * up_pre).astype(bf16)
     shared_hidden_grad = hidden(grad_b, 2)
     gate_grad_b, up_grad_b = swiglu_back(gate_pre, up_pre, shared_hidden_grad)
-    sh_s, hf_s, cot_s = core_swap(
-        [jnp.concatenate([gate_grad_b, up_grad_b, shared_hidden], axis=1), h_ffn, grad_b],
-        (None, 1, 1),
+    hf_s, cot_s, *sh_s = core_swap(
+        [h_ffn, grad_b, gate_grad_b, up_grad_b, shared_hidden],
+        (1, 1, None, None, None),
         fast,
         7,
     )
-    ff = shared_hidden.shape[1]
-    sh_s, hf_s, cot_s = tall(sh_s), tall(hf_s), tall(cot_s)
-    grad_sh = jnp.stack(
-        [
-            dot(sh_s[:, :ff], hf_s, 0, 0).astype(bf16),
-            dot(sh_s[:, ff : 2 * ff], hf_s, 0, 0).astype(bf16),
-            dot(sh_s[:, 2 * ff :], cot_s, 0, 0).astype(bf16),
-        ]
-    )
+    grad_sh = [
+        dot(tall(a), tall(b), 0, 0).astype(bf16) for a, b in zip(sh_s, (hf_s, hf_s, cot_s))
+    ]
+
     picked_all = picked_all.astype(f32)
     slot_probs = jax.nn.softmax(
         jnp.einsum("end,xd->enx", rows_all, router_mat, preferred_element_type=f32), axis=-1
@@ -1677,27 +1684,18 @@
     slot_back = z_home(slot_part, fast)
     expert_back = z_home(expert_part.astype(bf16), fast)
 
-    ex_s, row_s, dy_s = core_swap(
-        [
-            tall(jnp.concatenate([expert_gate_b, expert_up_b, expert_hidden], axis=-1)),
-            tall(rows_all),
-            tall(dy_all),
-        ],
-        (None, 1, 1),
+    row_s, dy_s, *ex_s = core_swap(
+        [tall(t) for t in (rows_all, dy_all, expert_gate_b, expert_up_b, expert_hidden)],
+        (1, 1, None, None, None),
         fast,
         8,
     )
-    fe = expert_hidden.shape[-1]
     by_expert = lambda t: t.reshape(2, EXP_WIN, -1, t.shape[-1])
-    ex_s, row_s, dy_s = by_expert(ex_s), by_expert(row_s), by_expert(dy_s)
-    edot = lambda a, b: jnp.einsum("senf,send->efd", a, b, preferred_element_type=f32).astype(bf16)
-    grad_ex = jnp.concatenate(
-        [
-            edot(ex_s[..., :fe], row_s),
-            edot(ex_s[..., fe : 2 * fe], row_s),
-            edot(ex_s[..., 2 * fe :], dy_s),
-        ]
-    )
+    edot = lambda a, b: jnp.einsum(
+        "senf,send->efd", by_expert(a), by_expert(b), preferred_element_type=f32
+    ).astype(bf16)
+    grad_ex = [edot(a, b) for a, b in zip(ex_s, (row_s, row_s, dy_s))]
+
     ffn_grad = unhidden(gate_grad_b, 0) + unhidden(up_grad_b, 1)
     back = lambda t: t.reshape(EXP_WIN, micros, CAP, t.shape[-1])
     slot_grad = back(slot_back[..., :width])
@@ -1720,6 +1718,7 @@
 
     att_s, og_s = core_swap([attended, attn_out_grad], (None, 1), fast, 2)
     grad_out = dot(tall(att_s), tall(og_s), 0, 0).astype(bf16)
+
     expert_out = back(expert_back)
     slot_gates = jnp.einsum(
         "emct,mte->emc", select, by_micro(router_probs)[..., :EXP_WIN], precision=highest
@@ -1733,8 +1732,12 @@
         group_tab = lambda t: jnp.tile(t[:rows], (1, HEAD_GROUP))
         res = back_all(
             dict(
-                gsh=grad_sh,
-                gex=grad_ex,
+                gs0=grad_sh[0],
+                gs1=grad_sh[1],
+                gs2=grad_sh[2],
+                ge0=grad_ex[0],
+                ge1=grad_ex[1],
+                ge2=grad_ex[2],
                 gout=grad_out,
                 q=q_all,
                 kvb=kvb_mat,
@@ -1804,7 +1807,7 @@
         gain_len = gain_grad.shape[1]
         gain_grad = jnp.pad(gain_grad, ((0, 0), (0, 16 * 128 - gain_len))).reshape(-1, 16, 128)
         gq, gkr, gkvb, gout, gsh, gex, gg = reduce_anywhere(
-            grad_q, grad_kr, grad_kvb, grad_out, grad_sh, grad_ex, gain_grad
+            grad_q, grad_kr, grad_kvb, grad_out, jnp.stack(grad_sh), jnp.concatenate(grad_ex), gain_grad
         )
         gg = gg.reshape(-1)
     wide = lambda t: t.astype(f32)

time: 792 us -> 772 us (0.975)
  Pallas kernels: 544 us -> 524 us
  matrix products: 76 us -> 85.5 us
  other arithmetic: 52.8 us -> 43.9 us
    pallas_call x1, Pallas kernels: 337 us -> 317 us  [back_all(): pl.pallas_call(functools.partial(back_kernel, scale, names), in_specs=[hb...]
    unnamed x149 -> x159, local copies, waits for them, and re-layouts: 24.6 us -> 23.3 us
  transfers between devices with their start and end apart: 13 -> 13, of which waited for: 5 -> 4; matrix products, arithmetic and copies ran while one was open for 9% -> 10% of each run, Pallas kernels for 9% -> 9%
where the time goes in v4:
time: 772 us; the launch traced here: 764 us
  Pallas kernels  524 us (68%)
  matrix products  85.5 us (11%)
  local copies, waits for them, and re-layouts  51.2 us (7%)
  other arithmetic  43.9 us (6%)
  starting transfers between devices  21.9 us (3%)
  waiting for transfers between devices  21.5 us (3%)
  between operations  15.7 us (2%)
    pallas_call x1, Pallas kernels, back_all(): pl.pallas_call(functools.partial(back_kernel, scale, names), in_specs=[hb...  317 us
    pallas_call x1, Pallas kernels, gather_weights(): pl.pallas_call(gather_kernel, in_specs=[pl.BlockSpec(memory_space=HBM)] *...  131 us
    dot_general x21, matrix products, dot(): lax.dot_general(a, b, (((ca,), (cb,)), ((), ())), preferred_element_type=...  48.9 us
    pallas_call x1, Pallas kernels, front(): pl.pallas_call(front_kernel, in_specs=[vmem] * 6 + [pl.BlockSpec(memory_s...  38.9 us
    convert_element_type x8, other arithmetic, shards(): wide = lambda t: t.astype(f32)  27.4 us
    dot_general x6, matrix products, shards(): lax.dot_general(a, b, (((ca,), (cb,)), ((0,), (0,))), preferred_element_t...  24.6 us
    unnamed x159, local copies, waits for them, and re-layouts  23.3 us
    pallas_call x1, Pallas kernels, attend_packed(): pl.pallas_call(functools.partial(attend_kernel, scale), grid=grid, in_spe...  21.9 us
  transfers between devices with their start and end apart: 13, of which 4 were waited for; matrix products, arithmetic and copies ran while one was open for 10% of the time, Pallas kernels for 9%

profile of v4, /device:TPU:9, one launch (start us, length us, event | category | flops | bytes accessed | tf_op | source)
XLA Modules:
  0.0 764.1 jit_solution(2102450386381694988)
XLA Ops:
  7.2 3.2 convert.43
  14.1 2.0 copy-done.28
  20.1 130.7 %gather_weights.1 = (bf16[3072,2048]{1,0:T(8,128)(2,1)}, bf16[640,2048]{1,0:T(8,128)(2,1)S(1)}, bf16[512,4096]{1,0:T(8,128)(2,1)S(1)}, bf16[2048,2048]{1,0:T(8,1...) custom-call(bf16[3072,512]{1,0:T(8,128)(2,1)S(1)} %pad_maximum_fusion.1.refs_0_, ...), custom_call_target="tpu_custom_call" | custom-call | tf_op jit(solution)/shard_map/gather_weights/pallas_call | solution.py:556
  150.9 2.0 copy-done.1
  152.9 1.5 copy-done.3
  155.9 1.9 collective-permute-start.8
  157.8 2.1 collective-permute-start.7
  161.0 1.6 tile.58
  164.0 2.2 copy-done.4
  166.2 38.9 %front.1 = (bf16[256,2048]{1,0:T(8,128)(2,1)S(1)}, f32[256,512]{1,0:T(8,128)S(1)}, bf16[256,3072]{1,0:T(8,128)(2,1)S(1)}, bf16[2,512,512]{2,1,0:T(8,128)(2,1)S(1...) custom-call(bf16[256,2048]{1,0:T(8,128)(2,1)S(1)} %bitcast.210, f32[1,2048]{1,0:T(1,128)S(1)} %bitcast.223, ...), custom_call_target="tpu_custom_call" | custom-call | tf_op jit(solution)/shard_map/front/pallas_call | solution.py:706
  207.0 21.9 %attend.1 = bf16[2,128,2048]{2,1,0:T(8,128)(2,1)S(1)} custom-call(f32[1,512]{1,0:T(1,128)S(1)} %compare_convert_fusion.seen_ref.refs_16_, bf16[2,128,3072]{2,1,0:T(8,128)(2,1)S(1)} %bitcast.203, bf16[2,128,3072]{2,1,0:T(8,128)(2,1)S(1)} %bitcast.204, bf16[2,128,3072]{2,1,0:T(8,128)(2,1)S(1)} %bitcast.205, ...), custom_call_target="tpu_custom_call" | custom-call | tf_op jit(solution)/shard_map/attend/pallas_call | solution.py:202
  229.0 2.6 multiply_reduce_fusion.3
  233.2 3.5 collective-permute-start.1
  236.7 2.3 collective-permute-start
  242.5 3.4 fusion.70
  246.0 1.5 fusion.73
  249.9 3.3 collective-permute-done.1
  253.9 4.9 collective-permute-done
  262.1 3.5 fusion.15
  265.6 3.5 fusion.19
  269.2 4.8 multiply_convert_fusion.6
  275.1 4.8 multiply_reduce_fusion.2
  282.4 1.7 copy.136
  284.2 2.0 fusion.87
  286.2 5.8 collective-permute-start.3
  292.1 2.1 collective-permute-start.4
  294.2 3.5 fusion.17
  297.7 4.5 fusion.5
  302.8 3.1 concatenate.45
  311.0 6.0 core_swap.4
  317.0 1.7 bitcast_convert_fusion.7.refs_3_
  318.7 1.7 bitcast_convert_fusion.6.refs_4_
  320.4 1.7 bitcast_convert_fusion.5.refs_5_
  322.1 2.1 collective-permute-start.10
  325.6 7.3 collective-permute-done.11
  332.8 6.0 collective-permute-done.10
  341.6 2.3 fusion.32
  343.9 2.4 fusion.34
  346.3 6.1 fusion.83
  352.5 1.6 convolution_bitcast_fusion
  354.0 1.5 fusion.94
  355.6 1.5 fusion.93
  358.3 1.6 fusion.28
  359.9 1.6 fusion.26
  365.8 2.6 multiply_reduce_fusion
  368.4 2.0 fusion.81
  370.5 3.3 convolution_convert_fusion
  373.8 3.6 core_swap.5
  377.4 2.9 fusion.30
  380.3 5.9 core_swap.3
  386.2 3.3 bitcast_convert_fusion.3.refs_0_
  389.5 3.3 bitcast_convert_fusion.2.refs_1_
  392.7 4.4 bitcast_convert_fusion.refs_6_
  397.1 3.3 bitcast_convert_fusion.1.refs_2_
  400.4 317.4 %back_all.1 = (bf16[3072,512]{1,0:T(8,128)(2,1)}, bf16[640,512]{1,0:T(8,128)(2,1)}, bf16[128,4096]{1,0:T(8,128)(2,1)}, bf16[512,2048]{1,0:T(8,128)(2,1)}, bf16[2...) custom-call(bf16[1408,1024]{1,0:T(8,128)(2,1)} %bitcast_convert_fusi, ...), custom_call_target="tpu_custom_call" | custom-call | tf_op jit(solution)/shard_map/back_all/pallas_call | solution.py:1473
  720.5 1.5 slice_convert_fusion.4
  722.0 2.2 slice_convert_fusion.3
  726.7 1.5 convert_element_type.324
  728.3 1.9 convert_element_type.331
  730.5 3.8 bitcast_convert_fusion.4
  734.3 2.5 convert_element_type.325
  736.9 3.3 bitcast_convert_fusion.8
  740.2 10.6 %slice_convert_fusion = (f32[2,352,2048]{2,1,0:T(8,128)}, f32[2,352,2048]{2,1,0:T(8,128)}, f32[2,352,2048]{2,1,0:T(8,128)}) fusion(bf16[6,352,2048]{2,1,0:T(8,128)(2,1)} %get-tuple-element.81), kind=kLoop, calls=%fused_computation.12 | loop fusion | flops 4325376 | bytes 25952256 | tf_op jit(solution)/shard_map/convert_element_type | solution.py:1813
  750.8 5.0 fusion.6
  (254 shorter events, 50.0 us)
Async XLA Ops:
  7.2 339.1 %all-gather.2.cloned.1.call-start = ((), (), s32[]{:S(2)}) async-start(), calls=%async_computation | async-start | bytes 14598144 | tf_op jit(solution)/shard_map/all_gather | solution.py:579
  10.6 2.0 copy-start.33
  11.9 2.0 copy-start.20
  13.9 2.2 copy-start.28
  16.1 1.8 copy-start.23
  16.1 2.7 copy-start.25
  20.1 134.3 %copy-start.65 = (s32[2,128,6]{1,0,2:T(2,128)S(1)}, s32[2,128,6]{1,0,2:T(2,128)}, u32[]{:S(2)}) copy-start(s32[2,128,6]{1,0,2:T(2,128)} %param.32) | copy-start | bytes 18436
  150.9 2.0 copy-start.1
  155.9 8.2 %copy-start.5 = (bf16[2,128,2048]{2,1,0:T(8,128)(2,1)S(1)}, bf16[2,128,2048]{2,1,0:T(8,128)(2,1)}, u32[]{:S(2)}) copy-start(bf16[2,128,2048]{2,1,0:T(8,128)(2,1)} %param.17) | copy-start | bytes 3145732
  155.9 113.3 %copy-start.31 = (bf16[2,2,16,2048]{3,2,1,0:T(8,128)(2,1)}, bf16[2,2,16,2048]{3,2,1,0:T(8,128)(2,1)S(1)}, u32[]{:S(2)}) copy-start(bf16[2,2,16,2048]{3,2,1,0:T(8,128)(2,1)S(1)} %copy.135) | copy-start | bytes 786436
  155.9 113.3 %collective-permute-start.8 = (bf16[2,32,2048]{2,1,0:T(8,128)(2,1)S(1)}, bf16[2,32,2048]{2,1,0:T(8,128)(2,1)}, u32[]{:S(2)}, u32[]{:S(2)}) collective-permute-start(bf16[2,32,2048]{2,1,0:T(8,128)(2,1)S(1)} %bitcast.239), channel_id=1, source_target_pairs={{0,3},{1,0},{2,1},{3,2},{4,7},{5,4},{6,5},{7,6},{8,11},{9,8},{10,9... | collective-permute-start | bytes 786440 | tf_op jit(solution)/shard_map/ppermute | solution.py:584
  157.8 111.3 %collective-permute-start.7 = (bf16[2,32,2048]{2,1,0:T(8,128)(2,1)S(1)}, bf16[2,32,2048]{2,1,0:T(8,128)(2,1)}, u32[]{:S(2)}, u32[]{:S(2)}) collective-permute-start(bf16[2,32,2048]{2,1,0:T(8,128)(2,1)S(1)} %bitcast.240), channel_id=1, source_target_pairs={{0,2},{1,3},{2,0},{3,1},{4,6},{5,7},{6,4},{7,5},{8,10},{9,11},{10,... | collective-permute-start | bytes 786440 | tf_op jit(solution)/shard_map/ppermute | solution.py:584
  163.9 41.2 %copy-start.15 = (f32[4,128]{1,0:T(4,128)}, f32[4,128]{1,0:T(4,128)S(1)}, u32[]{:S(2)}) copy-start(f32[4,128]{1,0:T(4,128)S(1)} %slice.211) | copy-start | bytes 6148
  164.0 68.2 %copy-start.53 = (f32[1,4,4,128]{3,1,2,0:T(4,128)}, f32[1,4,4,128]{3,1,2,0:T(4,128)S(1)}, u32[]{:S(2)}) copy-start(f32[1,4,4,128]{3,1,2,0:T(4,128)S(1)} %copy.174) | copy-start | bytes 24580
  164.0 41.1 %copy-start.14 = (f32[1,1,4,512]{3,1,2,0:T(1,128)}, f32[1,1,4,512]{3,1,2,0:T(1,128)S(1)}, u32[]{:S(2)}) copy-start(f32[1,1,4,512]{3,1,2,0:T(1,128)S(1)} %copy.171) | copy-start | bytes 24580
  164.0 2.2 copy-start.4
  206.9 22.0 %copy-start = (bf16[256,3072]{1,0:T(8,128)(2,1)}, bf16[256,3072]{1,0:T(8,128)(2,1)S(1)}, u32[]{:S(2)}) copy-start(bf16[256,3072]{1,0:T(8,128)(2,1)S(1)} %get-tuple-element.52.refs_7_) | copy-start | bytes 4718596
  206.9 22.0 %copy-start.6 = (bf16[2,512,512]{2,1,0:T(8,128)(2,1)}, bf16[2,512,512]{2,1,0:T(8,128)(2,1)S(1)}, u32[]{:S(2)}) copy-start(bf16[2,512,512]{2,1,0:T(8,128)(2,1)S(1)} %get-tuple-element.53.lat_ref.refs_13_) | copy-start | bytes 3145732
  206.9 22.0 %copy-start.9 = (bf16[2,512,128]{2,1,0:T(8,128)(2,1)}, bf16[2,512,128]{2,1,0:T(8,128)(2,1)S(1)}, u32[]{:S(2)}) copy-start(bf16[2,512,128]{2,1,0:T(8,128)(2,1)S(1)} %get-tuple-element.54.k1_ref.refs_14_) | copy-start | bytes 786436
  206.9 22.0 %copy-start.10 = (bf16[2,512,128]{2,1,0:T(8,128)(2,1)}, bf16[2,512,128]{2,1,0:T(8,128)(2,1)S(1)}, u32[]{:S(2)}) copy-start(bf16[2,512,128]{2,1,0:T(8,128)(2,1)S(1)} %get-tuple-element.55.k2_ref.refs_15_) | copy-start | bytes 786436
  207.0 22.0 %copy-start.16 = (f32[1,512]{1,0:T(1,128)}, f32[1,512]{1,0:T(1,128)S(1)}, u32[]{:S(2)}) copy-start(f32[1,512]{1,0:T(1,128)S(1)} %compare_convert_fusion.seen_ref.refs_16_) | copy-start | bytes 6148
  207.0 22.0 %copy-start.71 = (bf16[2048,2048]{1,0:T(8,128)(2,1)S(1)}, bf16[2048,2048]{1,0:T(8,128)(2,1)}, u32[]{:S(2)}) copy-start(bf16[2048,2048]{1,0:T(8,128)(2,1)} %get-tuple-element.57) | copy-start | bytes 25165828
  228.9 2.6 copy-start.7
  232.2 6.8 copy-start.51
  232.2 7.6 copy-start.49
  233.1 12.8 %copy-start.41 = (bf16[2,2,16,2048]{3,2,1,0:T(8,128)(2,1)}, bf16[2,2,16,2048]{3,2,1,0:T(8,128)(2,1)S(1)}, u32[]{:S(2)}) copy-start(bf16[2,2,16,2048]{3,2,1,0:T(8,128)(2,1)S(1)} %copy.128) | copy-start | bytes 786436
  233.1 16.3 %collective-permute-start.2 = (bf16[2,32,2048]{2,1,0:T(8,128)(2,1)S(1)}, bf16[2,32,2048]{2,1,0:T(8,128)(2,1)S(1)}, u32[]{:S(2)}, u32[]{:S(2)}) collective-permute-start(bf16[2,32,2048]{2,1,0:T(8,128)(2,1)S(1)} %bitcast.256), channel_id=1, source_target_pairs={{0,3},{1,0},{2,1},{3,2},{4,7},{5,4},{6,5},{7,6},{8,11},{9,8},{10,9... | collective-permute-start | bytes 786440 | tf_op jit(solution)/shard_map/ppermute | solution.py:584
  233.2 20.0 %collective-permute-start.1 = (bf16[2,32,2048]{2,1,0:T(8,128)(2,1)S(1)}, bf16[2,32,2048]{2,1,0:T(8,128)(2,1)S(1)}, u32[]{:S(2)}, u32[]{:S(2)}) collective-permute-start(bf16[2,32,2048]{2,1,0:T(8,128)(2,1)S(1)} %bitcast.257), channel_id=1, source_target_pairs={{0,2},{1,3},{2,0},{3,1},{4,6},{5,7},{6,4},{7,5},{8,10},{9,11},{10,... | collective-permute-start | bytes 786440 | tf_op jit(solution)/shard_map/ppermute | solution.py:584
  236.7 22.1 %collective-permute-start = (bf16[2,32,2048]{2,1,0:T(8,128)(2,1)S(1)}, bf16[2,32,2048]{2,1,0:T(8,128)(2,1)}, u32[]{:S(2)}, u32[]{:S(2)}) collective-permute-start(bf16[2,32,2048]{2,1,0:T(8,128)(2,1)S(1)} %bitcast.258), channel_id=1, source_target_pairs={{0,1},{1,2},{2,3},{3,0},{4,5},{5,6},{6,7},{7,4},{8,9},{9,10},{10,1... | collective-permute-start | bytes 786440 | tf_op jit(solution)/shard_map/ppermute | solution.py:584
  241.9 4.1 copy-start.44
  241.9 4.1 copy-start.63
  242.5 3.4 copy-start.21
  246.0 2.0 copy-start.26
  247.9 10.9 %copy-start.42 = (bf16[2,2,16,2048]{3,2,1,0:T(8,128)(2,1)S(1)}, bf16[2,2,16,2048]{3,2,1,0:T(8,128)(2,1)}, u32[]{:S(2)}) copy-start(bf16[2,2,16,2048]{3,2,1,0:T(8,128)(2,1)} %copy-done.41) | copy-start | bytes 786436
  249.4 3.8 copy-start.46
  249.4 19.7 %collective-permute-start.6 = (bf16[2,32,2048]{2,1,0:T(8,128)(2,1)S(1)}, bf16[2,32,2048]{2,1,0:T(8,128)(2,1)}, u32[]{:S(2)}, u32[]{:S(2)}) collective-permute-start(bf16[2,32,2048]{2,1,0:T(8,128)(2,1)S(1)} %bitcast.241), channel_id=1, source_target_pairs={{0,1},{1,2},{2,3},{3,0},{4,5},{5,6},{6,7},{7,4},{8,9},{9,10},{10,1... | collective-permute-start | bytes 786440 | tf_op jit(solution)/shard_map/ppermute | solution.py:584
  286.2 35.8 %collective-permute-start.3 = (bf16[2,32,2048]{2,1,0:T(8,128)(2,1)}, bf16[2,32,2048]{2,1,0:T(8,128)(2,1)}, u32[]{:S(2)}, u32[]{:S(2)}) collective-permute-start(bf16[2,32,2048]{2,1,0:T(8,128)(2,1)} %get-tuple-element.110), channel_id=1, source_target_pairs={{0,3},{1,0},{2,1},{3,2},{4,7},{5,4},{6,5},{7,6},{8,11},{9,8},{10,9... | collective-permute-start | bytes 786440 | tf_op jit(solution)/shard_map/ppermute | solution.py:584
  292.1 32.2 %collective-permute-start.5 = (bf16[2,32,2048]{2,1,0:T(8,128)(2,1)}, bf16[2,32,2048]{2,1,0:T(8,128)(2,1)}, u32[]{:S(2)}, u32[]{:S(2)}) collective-permute-start(bf16[2,32,2048]{2,1,0:T(8,128)(2,1)} %get-tuple-element.111), channel_id=1, source_target_pairs={{0,1},{1,2},{2,3},{3,0},{4,5},{5,6},{6,7},{7,4},{8,9},{9,10},{10,1... | collective-permute-start | bytes 786440 | tf_op jit(solution)/shard_map/ppermute | solution.py:584
  292.1 5.6 copy-start.43
  292.1 32.2 %collective-permute-start.4 = (bf16[2,32,2048]{2,1,0:T(8,128)(2,1)}, bf16[2,32,2048]{2,1,0:T(8,128)(2,1)}, u32[]{:S(2)}, u32[]{:S(2)}) collective-permute-start(bf16[2,32,2048]{2,1,0:T(8,128)(2,1)} %get-tuple-element.112), channel_id=1, source_target_pairs={{0,2},{1,3},{2,0},{3,1},{4,6},{5,7},{6,4},{7,5},{8,10},{9,11},{10,... | collective-permute-start | bytes 786440 | tf_op jit(solution)/shard_map/ppermute | solution.py:584
  305.9 4.1 copy-start.68
  307.1 18.5 %collective-permute-start.9 = (bf16[2,32,2176]{2,1,0:T(8,128)(2,1)S(1)}, bf16[2,32,2176]{2,1,0:T(8,128)(2,1)S(1)}, u32[]{:S(2)}, u32[]{:S(2)}) collective-permute-start(bf16[2,32,2176]{2,1,0:T(8,128)(2,1)S(1)} %get-tuple-element.107), channel_id=1, source_target_pairs={{0,3},{1,0},{2,1},{3,2},{4,7},{5,4},{6,5},{7,6},{8,11},{9,8},{10,9... | collective-permute-start | bytes 835592 | tf_op jit(solution)/shard_map/ppermute | solution.py:584
  307.2 25.7 %collective-permute-start.11 = (bf16[2,32,2176]{2,1,0:T(8,128)(2,1)S(1)}, bf16[2,32,2176]{2,1,0:T(8,128)(2,1)S(1)}, u32[]{:S(2)}, u32[]{:S(2)}) collective-permute-start(bf16[2,32,2176]{2,1,0:T(8,128)(2,1)S(1)} %get-tuple-element.108), channel_id=1, source_target_pairs={{0,1},{1,2},{2,3},{3,0},{4,5},{5,6},{6,7},{7,4},{8,9},{9,10},{10,1... | collective-permute-start | bytes 835592 | tf_op jit(solution)/shard_map/ppermute | solution.py:584
  322.1 18.0 %copy-start.57 = (s32[2,2,128]{2,0,1:T(2,128)S(1)}, s32[2,2,128]{2,0,1:T(2,128)}, u32[]{:S(2)}) copy-start(s32[2,2,128]{2,0,1:T(2,128)} %copy-done.55) | copy-start | bytes 6148
  322.1 18.0 %copy-start.60 = (pred[2,2,128]{2,0,1:T(4,128)(4,1)S(1)}, pred[2,2,128]{2,0,1:T(4,128)(4,1)}, u32[]{:S(2)}) copy-start(pred[2,2,128]{2,0,1:T(4,128)(4,1)} %copy-done.58) | copy-start | bytes 1540
  322.1 18.2 %copy-start.45 = (f32[256,64]{0,1:T(8,128)S(1)}, f32[256,64]{0,1:T(8,128)}, u32[]{:S(2)}) copy-start(f32[256,64]{0,1:T(8,128)} %copy-done.44) | copy-start | bytes 196612
  322.1 18.2 %copy-start.64 = (f32[256]{0:T(256)S(1)}, f32[256]{0:T(256)}, u32[]{:S(2)}) copy-start(f32[256]{0:T(256)} %copy-done.63) | copy-start | bytes 3076
  322.1 18.2 %copy-start.66 = (f32[256]{0:T(256)S(1)}, f32[256]{0:T(256)}, u32[]{:S(2)}) copy-start(f32[256]{0:T(256)} %fusion.50) | copy-start | bytes 3076
  322.1 16.7 %collective-permute-start.10 = (bf16[2,32,2176]{2,1,0:T(8,128)(2,1)S(1)}, bf16[2,32,2176]{2,1,0:T(8,128)(2,1)S(1)}, u32[]{:S(2)}, u32[]{:S(2)}) collective-permute-start(bf16[2,32,2176]{2,1,0:T(8,128)(2,1)S(1)} %get-tuple-element.109), channel_id=1, source_target_pairs={{0,2},{1,3},{2,0},{3,1},{4,6},{5,7},{6,4},{7,5},{8,10},{9,11},{10,... | collective-permute-start | bytes 835592 | tf_op jit(solution)/shard_map/ppermute | solution.py:584
  355.6 1.6 copy-start.34
  359.9 1.8 copy-start.22
  361.7 1.8 copy-start.24
  361.7 2.5 copy-start.27
  364.2 1.6 copy-start.62
  364.2 6.3 slice-start
  365.8 2.6 copy-start.67
  365.8 4.7 slice-start.1
  370.4 3.3 copy-start.8
  717.8 7.7 %copy-start.29 = (bf16[3072,512]{1,0:T(8,128)(2,1)S(1)}, bf16[3072,512]{1,0:T(8,128)(2,1)}, u32[]{:S(2)}) copy-start(bf16[3072,512]{1,0:T(8,128)(2,1)} %get-tuple-element.75) | copy-start | bytes 9437188
  725.7 2.6 copy-start.37
  730.5 3.8 copy-start.32
  734.3 2.6 copy-start.30
  740.2 10.6 %copy-start.19 = (f32[256,2048]{1,0:T(8,128)S(1)}, f32[256,2048]{1,0:T(8,128)}, u32[]{:S(2)}) copy-start(f32[256,2048]{1,0:T(8,128)} %copy-done.17) | copy-start | bytes 6291460
  750.8 5.0 copy-start.40
  (24 other events, 25.5 us)
Sparse Core Ops, SparseCore 0:
  154.5 79.2 all-gather.1

commit v5 on v4

--- a/solution.py
+++ b/solution.py
@@ -438,7 +438,7 @@
 ITEMS = 4
 GATHER_ORDER = (1, 0, 2, 3)
 GATHER_SEMS = 6 + ITEMS * 6 * 5
-LAG = 6
+LAG = 8
 
 
 class WeightGather:
@@ -465,7 +465,7 @@
     def run(self, late):
         units = self.units
         for n in range(len(units) + 3 * LAG):
-            if n == 3 * len(units) // 4:
+            if n == len(units):
                 late()
             if n < len(units):
                 if n % 6 == 0 and n // 6 + 2 < ITEMS:

time: 772 us -> 764 us (0.990)
  no operation moved by 1% of the time
where the time goes in v5:
time: 764 us; the launch traced here: 758 us
  Pallas kernels  519 us (68%)
  matrix products  85.5 us (11%)
  local copies, waits for them, and re-layouts  50.8 us (7%)
  other arithmetic  43.9 us (6%)
  starting transfers between devices  21.6 us (3%)
  waiting for transfers between devices  21.5 us (3%)
  between operations  15.7 us (2%)
    pallas_call x1, Pallas kernels, back_all(): pl.pallas_call(functools.partial(back_kernel, scale, names), in_specs=[hb...  320 us
    pallas_call x1, Pallas kernels, gather_weights(): pl.pallas_call(gather_kernel, in_specs=[pl.BlockSpec(memory_space=HBM)] *...  123 us
    dot_general x21, matrix products, dot(): lax.dot_general(a, b, (((ca,), (cb,)), ((), ())), preferred_element_type=...  48.8 us
    pallas_call x1, Pallas kernels, front(): pl.pallas_call(front_kernel, in_specs=[vmem] * 6 + [pl.BlockSpec(memory_s...  38.7 us
    convert_element_type x8, other arithmetic, shards(): wide = lambda t: t.astype(f32)  27.4 us
    dot_general x6, matrix products, shards(): lax.dot_general(a, b, (((ca,), (cb,)), ((0,), (0,))), preferred_element_t...  24.6 us
    unnamed x159, local copies, waits for them, and re-layouts  22.9 us
    pallas_call x1, Pallas kernels, attend_packed(): pl.pallas_call(functools.partial(attend_kernel, scale), grid=grid, in_spe...  21.9 us
  transfers between devices with their start and end apart: 13, of which 4 were waited for; matrix products, arithmetic and copies ran while one was open for 10% of the time, Pallas kernels for 9%

profile of v5, /device:TPU:9, one launch (start us, length us, event | category | flops | bytes accessed | tf_op | source)
XLA Modules:
  0.0 757.9 jit_solution(17339787511129854381)
XLA Ops:
  7.2 3.2 convert.43
  14.1 2.0 copy-done.28
  20.1 123.1 %gather_weights.1 = (bf16[3072,2048]{1,0:T(8,128)(2,1)}, bf16[640,2048]{1,0:T(8,128)(2,1)S(1)}, bf16[512,4096]{1,0:T(8,128)(2,1)S(1)}, bf16[2048,2048]{1,0:T(8,1...) custom-call(bf16[3072,512]{1,0:T(8,128)(2,1)S(1)} %pad_maximum_fusion.1.refs_0_, ...), custom_call_target="tpu_custom_call" | custom-call | tf_op jit(solution)/shard_map/gather_weights/pallas_call | solution.py:556
  143.2 2.0 copy-done.1
  145.2 1.5 copy-done.3
  148.5 3.4 collective-permute-start.7
  153.0 1.6 tile.58
  156.0 1.7 copy-done.4
  157.8 38.7 %front.1 = (bf16[256,2048]{1,0:T(8,128)(2,1)S(1)}, f32[256,512]{1,0:T(8,128)S(1)}, bf16[256,3072]{1,0:T(8,128)(2,1)S(1)}, bf16[2,512,512]{2,1,0:T(8,128)(2,1)S(1...) custom-call(bf16[256,2048]{1,0:T(8,128)(2,1)S(1)} %bitcast.210, f32[1,2048]{1,0:T(1,128)S(1)} %bitcast.223, ...), custom_call_target="tpu_custom_call" | custom-call | tf_op jit(solution)/shard_map/front/pallas_call | solution.py:706
  198.4 21.9 %attend.1 = bf16[2,128,2048]{2,1,0:T(8,128)(2,1)S(1)} custom-call(f32[1,512]{1,0:T(1,128)S(1)} %compare_convert_fusion.seen_ref.refs_16_, bf16[2,128,3072]{2,1,0:T(8,128)(2,1)S(1)} %bitcast.203, bf16[2,128,3072]{2,1,0:T(8,128)(2,1)S(1)} %bitcast.204, bf16[2,128,3072]{2,1,0:T(8,128)(2,1)S(1)} %bitcast.205, ...), custom_call_target="tpu_custom_call" | custom-call | tf_op jit(solution)/shard_map/attend/pallas_call | solution.py:202
  220.3 2.6 multiply_reduce_fusion.3
  224.6 3.5 collective-permute-start.1
  228.1 2.3 collective-permute-start
  233.9 3.4 fusion.70
  237.4 1.5 fusion.73
  239.3 1.5 fusion.66
  241.3 3.3 collective-permute-done.1
  245.3 4.9 collective-permute-done
  253.4 3.5 fusion.15
  257.0 3.5 fusion.19
  260.6 4.8 multiply_convert_fusion.6
  266.4 4.8 multiply_reduce_fusion.2
  273.8 1.7 copy.136
  275.5 2.0 fusion.87
  277.6 5.9 collective-permute-start.3
  283.5 2.1 collective-permute-start.4
  285.5 3.5 fusion.17
  289.1 4.5 fusion.5
  294.2 3.1 concatenate.45
  302.4 6.0 core_swap.4
  308.4 1.7 bitcast_convert_fusion.7.refs_3_
  310.0 1.7 bitcast_convert_fusion.6.refs_4_
  311.7 1.7 bitcast_convert_fusion.5.refs_5_
  313.5 2.1 collective-permute-start.10
  317.0 7.3 collective-permute-done.11
  324.2 6.0 collective-permute-done.10
  332.9 2.3 fusion.32
  335.3 2.4 fusion.34
  337.7 6.1 fusion.83
  343.8 1.6 convolution_bitcast_fusion
  345.4 1.5 fusion.94
  347.0 1.5 fusion.93
  349.7 1.6 fusion.28
  351.3 1.6 fusion.26
  357.2 2.6 multiply_reduce_fusion
  359.8 2.0 fusion.81
  361.8 3.3 convolution_convert_fusion
  365.2 3.6 core_swap.5
  368.8 2.9 fusion.30
  371.7 5.9 core_swap.3
  377.6 3.3 bitcast_convert_fusion.3.refs_0_
  380.9 3.3 bitcast_convert_fusion.2.refs_1_
  384.1 4.4 bitcast_convert_fusion.refs_6_
  388.5 3.3 bitcast_convert_fusion.1.refs_2_
  391.8 319.8 %back_all.1 = (bf16[3072,512]{1,0:T(8,128)(2,1)}, bf16[640,512]{1,0:T(8,128)(2,1)}, bf16[128,4096]{1,0:T(8,128)(2,1)}, bf16[512,2048]{1,0:T(8,128)(2,1)}, bf16[2...) custom-call(bf16[1408,1024]{1,0:T(8,128)(2,1)} %bitcast_convert_fusi, ...), custom_call_target="tpu_custom_call" | custom-call | tf_op jit(solution)/shard_map/back_all/pallas_call | solution.py:1473
  714.2 1.5 slice_convert_fusion.4
  715.7 2.2 slice_convert_fusion.3
  720.5 1.5 convert_element_type.324
  722.0 1.9 convert_element_type.331
  724.2 3.8 bitcast_convert_fusion.4
  728.0 2.5 convert_element_type.325
  730.7 3.3 bitcast_convert_fusion.8
  734.0 10.6 %slice_convert_fusion = (f32[2,352,2048]{2,1,0:T(8,128)}, f32[2,352,2048]{2,1,0:T(8,128)}, f32[2,352,2048]{2,1,0:T(8,128)}) fusion(bf16[6,352,2048]{2,1,0:T(8,128)(2,1)} %get-tuple-element.81), kind=kLoop, calls=%fused_computation.12 | loop fusion | flops 4325376 | bytes 25952256 | tf_op jit(solution)/shard_map/convert_element_type | solution.py:1813
  744.6 5.0 fusion.6
  (254 shorter events, 48.8 us)
Async XLA Ops:
  7.2 330.5 %all-gather.2.cloned.1.call-start = ((), (), s32[]{:S(2)}) async-start(), calls=%async_computation | async-start | bytes 14598144 | tf_op jit(solution)/shard_map/all_gather | solution.py:579
  10.6 2.0 copy-start.33
  11.9 2.0 copy-start.20
  13.9 2.2 copy-start.28
  16.1 1.8 copy-start.23
  16.1 2.7 copy-start.25
  20.1 126.6 %copy-start.65 = (s32[2,128,6]{1,0,2:T(2,128)S(1)}, s32[2,128,6]{1,0,2:T(2,128)}, u32[]{:S(2)}) copy-start(s32[2,128,6]{1,0,2:T(2,128)} %param.32) | copy-start | bytes 18436
  143.2 2.0 copy-start.1
  148.2 7.8 %copy-start.5 = (bf16[2,128,2048]{2,1,0:T(8,128)(2,1)S(1)}, bf16[2,128,2048]{2,1,0:T(8,128)(2,1)}, u32[]{:S(2)}) copy-start(bf16[2,128,2048]{2,1,0:T(8,128)(2,1)} %param.17) | copy-start | bytes 3145732
  148.2 112.3 %copy-start.31 = (bf16[2,2,16,2048]{3,2,1,0:T(8,128)(2,1)}, bf16[2,2,16,2048]{3,2,1,0:T(8,128)(2,1)S(1)}, u32[]{:S(2)}) copy-start(bf16[2,2,16,2048]{3,2,1,0:T(8,128)(2,1)S(1)} %copy.135) | copy-start | bytes 786436
  148.2 112.3 %collective-permute-start.8 = (bf16[2,32,2048]{2,1,0:T(8,128)(2,1)S(1)}, bf16[2,32,2048]{2,1,0:T(8,128)(2,1)}, u32[]{:S(2)}, u32[]{:S(2)}) collective-permute-start(bf16[2,32,2048]{2,1,0:T(8,128)(2,1)S(1)} %bitcast.239), channel_id=1, source_target_pairs={{0,3},{1,0},{2,1},{3,2},{4,7},{5,4},{6,5},{7,6},{8,11},{9,8},{10,9... | collective-permute-start | bytes 786440 | tf_op jit(solution)/shard_map/ppermute | solution.py:584
  148.5 112.0 %collective-permute-start.7 = (bf16[2,32,2048]{2,1,0:T(8,128)(2,1)S(1)}, bf16[2,32,2048]{2,1,0:T(8,128)(2,1)}, u32[]{:S(2)}, u32[]{:S(2)}) collective-permute-start(bf16[2,32,2048]{2,1,0:T(8,128)(2,1)S(1)} %bitcast.240), channel_id=1, source_target_pairs={{0,2},{1,3},{2,0},{3,1},{4,6},{5,7},{6,4},{7,5},{8,10},{9,11},{10,... | collective-permute-start | bytes 786440 | tf_op jit(solution)/shard_map/ppermute | solution.py:584
  155.9 40.6 %copy-start.15 = (f32[4,128]{1,0:T(4,128)}, f32[4,128]{1,0:T(4,128)S(1)}, u32[]{:S(2)}) copy-start(f32[4,128]{1,0:T(4,128)S(1)} %slice.211) | copy-start | bytes 6148
  155.9 67.6 %copy-start.53 = (f32[1,4,4,128]{3,1,2,0:T(4,128)}, f32[1,4,4,128]{3,1,2,0:T(4,128)S(1)}, u32[]{:S(2)}) copy-start(f32[1,4,4,128]{3,1,2,0:T(4,128)S(1)} %copy.174) | copy-start | bytes 24580
  156.0 40.5 %copy-start.14 = (f32[1,1,4,512]{3,1,2,0:T(1,128)}, f32[1,1,4,512]{3,1,2,0:T(1,128)S(1)}, u32[]{:S(2)}) copy-start(f32[1,1,4,512]{3,1,2,0:T(1,128)S(1)} %copy.171) | copy-start | bytes 24580
  156.0 1.7 copy-start.4
  198.3 22.0 %copy-start = (bf16[256,3072]{1,0:T(8,128)(2,1)}, bf16[256,3072]{1,0:T(8,128)(2,1)S(1)}, u32[]{:S(2)}) copy-start(bf16[256,3072]{1,0:T(8,128)(2,1)S(1)} %get-tuple-element.52.refs_7_) | copy-start | bytes 4718596
  198.3 22.0 %copy-start.6 = (bf16[2,512,512]{2,1,0:T(8,128)(2,1)}, bf16[2,512,512]{2,1,0:T(8,128)(2,1)S(1)}, u32[]{:S(2)}) copy-start(bf16[2,512,512]{2,1,0:T(8,128)(2,1)S(1)} %get-tuple-element.53.lat_ref.refs_13_) | copy-start | bytes 3145732
  198.3 22.0 %copy-start.9 = (bf16[2,512,128]{2,1,0:T(8,128)(2,1)}, bf16[2,512,128]{2,1,0:T(8,128)(2,1)S(1)}, u32[]{:S(2)}) copy-start(bf16[2,512,128]{2,1,0:T(8,128)(2,1)S(1)} %get-tuple-element.54.k1_ref.refs_14_) | copy-start | bytes 786436
  198.3 22.0 %copy-start.10 = (bf16[2,512,128]{2,1,0:T(8,128)(2,1)}, bf16[2,512,128]{2,1,0:T(8,128)(2,1)S(1)}, u32[]{:S(2)}) copy-start(bf16[2,512,128]{2,1,0:T(8,128)(2,1)S(1)} %get-tuple-element.55.k2_ref.refs_15_) | copy-start | bytes 786436
  198.3 22.0 %copy-start.16 = (f32[1,512]{1,0:T(1,128)}, f32[1,512]{1,0:T(1,128)S(1)}, u32[]{:S(2)}) copy-start(f32[1,512]{1,0:T(1,128)S(1)} %compare_convert_fusion.seen_ref.refs_16_) | copy-start | bytes 6148
  198.3 22.0 %copy-start.71 = (bf16[2048,2048]{1,0:T(8,128)(2,1)S(1)}, bf16[2048,2048]{1,0:T(8,128)(2,1)}, u32[]{:S(2)}) copy-start(bf16[2048,2048]{1,0:T(8,128)(2,1)} %get-tuple-element.57) | copy-start | bytes 25165828
  220.3 2.6 copy-start.7
  223.5 6.8 copy-start.51
  223.5 7.6 copy-start.49
  224.5 12.8 %copy-start.41 = (bf16[2,2,16,2048]{3,2,1,0:T(8,128)(2,1)}, bf16[2,2,16,2048]{3,2,1,0:T(8,128)(2,1)S(1)}, u32[]{:S(2)}) copy-start(bf16[2,2,16,2048]{3,2,1,0:T(8,128)(2,1)S(1)} %copy.128) | copy-start | bytes 786436
  224.5 16.3 %collective-permute-start.2 = (bf16[2,32,2048]{2,1,0:T(8,128)(2,1)S(1)}, bf16[2,32,2048]{2,1,0:T(8,128)(2,1)S(1)}, u32[]{:S(2)}, u32[]{:S(2)}) collective-permute-start(bf16[2,32,2048]{2,1,0:T(8,128)(2,1)S(1)} %bitcast.256), channel_id=1, source_target_pairs={{0,3},{1,0},{2,1},{3,2},{4,7},{5,4},{6,5},{7,6},{8,11},{9,8},{10,9... | collective-permute-start | bytes 786440 | tf_op jit(solution)/shard_map/ppermute | solution.py:584
  224.6 20.0 %collective-permute-start.1 = (bf16[2,32,2048]{2,1,0:T(8,128)(2,1)S(1)}, bf16[2,32,2048]{2,1,0:T(8,128)(2,1)S(1)}, u32[]{:S(2)}, u32[]{:S(2)}) collective-permute-start(bf16[2,32,2048]{2,1,0:T(8,128)(2,1)S(1)} %bitcast.257), channel_id=1, source_target_pairs={{0,2},{1,3},{2,0},{3,1},{4,6},{5,7},{6,4},{7,5},{8,10},{9,11},{10,... | collective-permute-start | bytes 786440 | tf_op jit(solution)/shard_map/ppermute | solution.py:584
  228.1 22.1 %collective-permute-start = (bf16[2,32,2048]{2,1,0:T(8,128)(2,1)S(1)}, bf16[2,32,2048]{2,1,0:T(8,128)(2,1)}, u32[]{:S(2)}, u32[]{:S(2)}) collective-permute-start(bf16[2,32,2048]{2,1,0:T(8,128)(2,1)S(1)} %bitcast.258), channel_id=1, source_target_pairs={{0,1},{1,2},{2,3},{3,0},{4,5},{5,6},{6,7},{7,4},{8,9},{9,10},{10,1... | collective-permute-start | bytes 786440 | tf_op jit(solution)/shard_map/ppermute | solution.py:584
  233.3 4.1 copy-start.44
  233.3 4.1 copy-start.63
  233.9 3.4 copy-start.21
  237.4 2.0 copy-start.26
  239.3 10.9 %copy-start.42 = (bf16[2,2,16,2048]{3,2,1,0:T(8,128)(2,1)S(1)}, bf16[2,2,16,2048]{3,2,1,0:T(8,128)(2,1)}, u32[]{:S(2)}) copy-start(bf16[2,2,16,2048]{3,2,1,0:T(8,128)(2,1)} %copy-done.41) | copy-start | bytes 786436
  240.8 3.7 copy-start.46
  240.8 19.7 %collective-permute-start.6 = (bf16[2,32,2048]{2,1,0:T(8,128)(2,1)S(1)}, bf16[2,32,2048]{2,1,0:T(8,128)(2,1)}, u32[]{:S(2)}, u32[]{:S(2)}) collective-permute-start(bf16[2,32,2048]{2,1,0:T(8,128)(2,1)S(1)} %bitcast.241), channel_id=1, source_target_pairs={{0,1},{1,2},{2,3},{3,0},{4,5},{5,6},{6,7},{7,4},{8,9},{9,10},{10,1... | collective-permute-start | bytes 786440 | tf_op jit(solution)/shard_map/ppermute | solution.py:584
  277.6 35.9 %collective-permute-start.3 = (bf16[2,32,2048]{2,1,0:T(8,128)(2,1)}, bf16[2,32,2048]{2,1,0:T(8,128)(2,1)}, u32[]{:S(2)}, u32[]{:S(2)}) collective-permute-start(bf16[2,32,2048]{2,1,0:T(8,128)(2,1)} %get-tuple-element.110), channel_id=1, source_target_pairs={{0,3},{1,0},{2,1},{3,2},{4,7},{5,4},{6,5},{7,6},{8,11},{9,8},{10,9... | collective-permute-start | bytes 786440 | tf_op jit(solution)/shard_map/ppermute | solution.py:584
  283.5 32.2 %collective-permute-start.5 = (bf16[2,32,2048]{2,1,0:T(8,128)(2,1)}, bf16[2,32,2048]{2,1,0:T(8,128)(2,1)}, u32[]{:S(2)}, u32[]{:S(2)}) collective-permute-start(bf16[2,32,2048]{2,1,0:T(8,128)(2,1)} %get-tuple-element.111), channel_id=1, source_target_pairs={{0,1},{1,2},{2,3},{3,0},{4,5},{5,6},{6,7},{7,4},{8,9},{9,10},{10,1... | collective-permute-start | bytes 786440 | tf_op jit(solution)/shard_map/ppermute | solution.py:584
  283.5 5.6 copy-start.43
  283.5 32.2 %collective-permute-start.4 = (bf16[2,32,2048]{2,1,0:T(8,128)(2,1)}, bf16[2,32,2048]{2,1,0:T(8,128)(2,1)}, u32[]{:S(2)}, u32[]{:S(2)}) collective-permute-start(bf16[2,32,2048]{2,1,0:T(8,128)(2,1)} %get-tuple-element.112), channel_id=1, source_target_pairs={{0,2},{1,3},{2,0},{3,1},{4,6},{5,7},{6,4},{7,5},{8,10},{9,11},{10,... | collective-permute-start | bytes 786440 | tf_op jit(solution)/shard_map/ppermute | solution.py:584
  297.3 4.1 copy-start.68
  298.5 18.5 %collective-permute-start.9 = (bf16[2,32,2176]{2,1,0:T(8,128)(2,1)S(1)}, bf16[2,32,2176]{2,1,0:T(8,128)(2,1)S(1)}, u32[]{:S(2)}, u32[]{:S(2)}) collective-permute-start(bf16[2,32,2176]{2,1,0:T(8,128)(2,1)S(1)} %get-tuple-element.107), channel_id=1, source_target_pairs={{0,3},{1,0},{2,1},{3,2},{4,7},{5,4},{6,5},{7,6},{8,11},{9,8},{10,9... | collective-permute-start | bytes 835592 | tf_op jit(solution)/shard_map/ppermute | solution.py:584
  298.6 25.7 %collective-permute-start.11 = (bf16[2,32,2176]{2,1,0:T(8,128)(2,1)S(1)}, bf16[2,32,2176]{2,1,0:T(8,128)(2,1)S(1)}, u32[]{:S(2)}, u32[]{:S(2)}) collective-permute-start(bf16[2,32,2176]{2,1,0:T(8,128)(2,1)S(1)} %get-tuple-element.108), channel_id=1, source_target_pairs={{0,1},{1,2},{2,3},{3,0},{4,5},{5,6},{6,7},{7,4},{8,9},{9,10},{10,1... | collective-permute-start | bytes 835592 | tf_op jit(solution)/shard_map/ppermute | solution.py:584
  313.5 18.0 %copy-start.57 = (s32[2,2,128]{2,0,1:T(2,128)S(1)}, s32[2,2,128]{2,0,1:T(2,128)}, u32[]{:S(2)}) copy-start(s32[2,2,128]{2,0,1:T(2,128)} %copy-done.55) | copy-start | bytes 6148
  313.5 18.0 %copy-start.60 = (pred[2,2,128]{2,0,1:T(4,128)(4,1)S(1)}, pred[2,2,128]{2,0,1:T(4,128)(4,1)}, u32[]{:S(2)}) copy-start(pred[2,2,128]{2,0,1:T(4,128)(4,1)} %copy-done.58) | copy-start | bytes 1540
  313.5 18.2 %copy-start.45 = (f32[256,64]{0,1:T(8,128)S(1)}, f32[256,64]{0,1:T(8,128)}, u32[]{:S(2)}) copy-start(f32[256,64]{0,1:T(8,128)} %copy-done.44) | copy-start | bytes 196612
  313.5 18.2 %copy-start.64 = (f32[256]{0:T(256)S(1)}, f32[256]{0:T(256)}, u32[]{:S(2)}) copy-start(f32[256]{0:T(256)} %copy-done.63) | copy-start | bytes 3076
  313.5 18.2 %copy-start.66 = (f32[256]{0:T(256)S(1)}, f32[256]{0:T(256)}, u32[]{:S(2)}) copy-start(f32[256]{0:T(256)} %fusion.50) | copy-start | bytes 3076
  313.5 16.7 %collective-permute-start.10 = (bf16[2,32,2176]{2,1,0:T(8,128)(2,1)S(1)}, bf16[2,32,2176]{2,1,0:T(8,128)(2,1)S(1)}, u32[]{:S(2)}, u32[]{:S(2)}) collective-permute-start(bf16[2,32,2176]{2,1,0:T(8,128)(2,1)S(1)} %get-tuple-element.109), channel_id=1, source_target_pairs={{0,2},{1,3},{2,0},{3,1},{4,6},{5,7},{6,4},{7,5},{8,10},{9,11},{10,... | collective-permute-start | bytes 835592 | tf_op jit(solution)/shard_map/ppermute | solution.py:584
  347.0 1.6 copy-start.34
  351.3 1.8 copy-start.22
  353.1 1.8 copy-start.24
  353.1 2.5 copy-start.27
  355.6 1.6 copy-start.62
  355.6 6.3 slice-start
  357.2 2.6 copy-start.67
  357.2 4.7 slice-start.1
  361.8 3.3 copy-start.8
  711.6 7.7 %copy-start.29 = (bf16[3072,512]{1,0:T(8,128)(2,1)S(1)}, bf16[3072,512]{1,0:T(8,128)(2,1)}, u32[]{:S(2)}) copy-start(bf16[3072,512]{1,0:T(8,128)(2,1)} %get-tuple-element.75) | copy-start | bytes 9437188
  719.4 2.6 copy-start.37
  724.2 3.8 copy-start.32
  728.0 2.6 copy-start.30
  734.0 10.6 %copy-start.19 = (f32[256,2048]{1,0:T(8,128)S(1)}, f32[256,2048]{1,0:T(8,128)}, u32[]{:S(2)}) copy-start(f32[256,2048]{1,0:T(8,128)} %copy-done.17) | copy-start | bytes 6291460
  744.6 5.0 copy-start.40
  (24 other events, 25.5 us)
Sparse Core Ops, SparseCore 0:
  146.8 80.7 all-gather.1
